TPU v7x, 32 devices: a whole 2x2x4 slice. The times are simulated.
32 devices in a mesh: league: 2 (over y), dp: 4 (over x, core), fsdp: 4 (over z).
Axes of the slice: x: 2, y: 2, z: 4, core: 2. Of those that a mesh axis runs over, the one named last changes fastest.
Arguments:
- tokens: bfloat16 [16384, 5120], P(('league', 'dp', 'fsdp')), parts along dimension 0, may hold values from -6 to 6
- value_cotangent: bfloat16 [16384, 1024], P(('league', 'dp', 'fsdp')), parts along dimension 0, may hold values from -6 to 6
- value_weight: bfloat16 [5120, 1024], P('fsdp'), may hold values from -0.078125 to 0.078125
- adapter_down: bfloat16 [8, 64, 5120], P('dp', None, 'fsdp'), may hold values from -0.078125 to 0.078125
- adapter_up: bfloat16 [8, 64, 1024], P('dp'), may hold values from -0.1875 to 0.1875
- tile_token_policy: int32 [128], P(('league', 'dp', 'fsdp')), parts along dimension 0, may hold values from 0 to 7
- tile_live_length: int32 [128], P(('league', 'dp', 'fsdp')), parts along dimension 0, may hold values from 1 to 128
Outputs:
- input_cotangent: bfloat16 [16384, 5120], P(('league', 'dp', 'fsdp')), parts along dimension 0
- grad_a: float32 [16, 64, 5120], P(('league', 'dp'), None, 'fsdp'), parts along dimension 0
- grad_b: float32 [16, 64, 1024], P(('league', 'dp')), parts along dimension 0
There are 2 independent parts, one for each index of `league`. A program takes and returns all parts, laid end to end along the dimension named above; an argument that names none is the same for every part. Nothing has to cross between parts.
All inputs are finite; a program needn't handle non-finite values.
Results may differ from a plain program's by a relative error of at most 0.0032.
Values may be sent and summed in bfloat16 or wider, within the bound.
No kernel may reach another device: no remote copies, remote signals or barrier semaphores. Data moves between devices by JAX's collectives and lax.ppermute only.
A program may use at most 192 MiB of HBM per device.

v0:
```python
import math

import jax
import jax.numpy as jnp
from jax import lax
from jax.sharding import PartitionSpec as P

adapter_scale = 2.0


def body(
    tokens,
    value_cotangent,
    value_weight,
    adapter_down,
    adapter_up,
    tile_token_policy,
    tile_live_length,
):
    tokens_per_device = tokens.shape[0]
    hidden_width = tokens.shape[1]
    tile_count = tile_token_policy.shape[0]
    tile_rows = tokens_per_device // tile_count
    width_kv = value_cotangent.shape[1]
    row_index = jnp.arange(tile_rows, dtype=jnp.int32)
    live_mask = row_index[None, :] < tile_live_length[:, None]
    masked_tiles = jnp.where(
        live_mask[:, :, None],
        value_cotangent.reshape(tile_count, tile_rows, width_kv),
        jnp.zeros((), value_cotangent.dtype),
    )
    masked = masked_tiles.reshape(tokens_per_device, width_kv)
    widened_down = lax.all_gather(adapter_down, "fsdp", axis=2, tiled=True)
    every_a, every_b = (
        lax.all_gather(widened_down, "dp", axis=0, tiled=True),
        lax.all_gather(adapter_up, "dp", axis=0, tiled=True),
    )
    group_grads = lax.all_gather(masked, "fsdp", axis=0, tiled=True)
    blocks = jnp.einsum("tk,dk->td", group_grads, value_weight, preferred_element_type=jnp.float32)
    frozen_contribution = lax.all_to_all(blocks, "fsdp", split_axis=0, concat_axis=1, tiled=True)
    x_tiles = tokens.reshape(tile_count, tile_rows, hidden_width)
    num_pol = every_a.shape[0]
    rank_width = every_a.shape[1]

    def tile_step(carried, inputs):
        down_accumulator, up_accumulator = carried
        x_tile, value_grad_tile, policy_index = inputs
        down_matrix = lax.dynamic_index_in_dim(every_a, policy_index, 0, keepdims=False)
        up_matrix = lax.dynamic_index_in_dim(every_b, policy_index, 0, keepdims=False)
        rank_activations = (
            adapter_scale
            * jnp.einsum(
                "xs,zs->xz", value_grad_tile, up_matrix, preferred_element_type=jnp.float32
            )
        ).astype(jnp.bfloat16)
        adapter_contribution = jnp.dot(
            rank_activations, down_matrix, preferred_element_type=jnp.float32
        )
        projected_rows = jnp.einsum(
            "td,rd->tr", x_tile, down_matrix, preferred_element_type=jnp.float32
        ).astype(jnp.bfloat16)
        down_accumulator = down_accumulator.at[policy_index].add(
            jnp.einsum("tr,td->rd", rank_activations, x_tile, preferred_element_type=jnp.float32)
        )
        up_accumulator = up_accumulator.at[policy_index].add(
            adapter_scale
            * jnp.einsum(
                "tr,tk->rk", projected_rows, value_grad_tile, preferred_element_type=jnp.float32
            )
        )
        return ((down_accumulator, up_accumulator), (adapter_contribution, rank_activations))

    start_a = jnp.zeros((num_pol, rank_width, hidden_width), jnp.float32)
    initial = (start_a, jnp.zeros((num_pol, rank_width, width_kv), jnp.float32))
    (down_accumulator, up_accumulator), (adapter_contributions, rank_tile_rows) = lax.scan(
        tile_step, initial, (x_tiles, masked_tiles, tile_token_policy)
    )
    input_cotangent = (
        frozen_contribution + adapter_contributions.reshape(tokens_per_device, hidden_width)
    ).astype(jnp.bfloat16)
    normalizer = 1.0 / math.sqrt(tokens_per_device * lax.axis_size("dp") * lax.axis_size("fsdp"))
    up_accumulator = up_accumulator * normalizer
    down_accumulator = down_accumulator * normalizer
    owned_a, owned_b = (
        lax.psum_scatter(down_accumulator, "dp", scatter_dimension=0, tiled=True),
        lax.psum_scatter(up_accumulator, "dp", scatter_dimension=0, tiled=True),
    )
    grad_a = lax.psum_scatter(owned_a, "fsdp", scatter_dimension=2, tiled=True)
    grad_b = lax.psum(owned_b, "fsdp")
    return (input_cotangent, grad_a, grad_b)


def solution(mesh):
    return jax.shard_map(
        body,
        mesh=mesh,
        in_specs=(
            P(("league", "dp", "fsdp"), None),
            P(("league", "dp", "fsdp"), None),
            P("fsdp", None),
            P("dp", None, "fsdp"),
            P("dp", None, None),
            P(("league", "dp", "fsdp")),
            P(("league", "dp", "fsdp")),
        ),
        out_specs=(
            P(("league", "dp", "fsdp"), None),
            P(("league", "dp"), None, "fsdp"),
            P(("league", "dp"), None, None),
        ),
        check_vma=False,
    )
```

profile of v0, /device:TPU:0, one launch (start us, length us, event | category | flops | bytes accessed | tf_op | source)
XLA Modules:
  0.0 509.1 jit_solution(10741614815432691317)
XLA Ops:
  8.7 36.3 %all-gather.9.cloned.1.call-done = bf16[2,64,5120]{2,1,0:T(8,128)(2,1)} async-done(((bf16[2,64,1280]{2,1,0:T(8,128)(2,1)}), bf16[2,64,5120]{2,1,0:T(8,128)(2,1)}) %all-gather.9.cloned.1.call-update) | async-done | bytes 1310736 | tf_op jit(solution)/shard_map/all_gather | solution.py:33
  45.8 2.4 broadcast_select_fusion
  48.3 2.5 broadcast_select_fusion.1
  50.7 11.6 %all-gather.7.cloned.1.call-done = bf16[8,64,1024]{2,1,0:T(8,128)(2,1)} async-done(((bf16[2,64,1024]{2,1,0:T(8,128)(2,1)}), bf16[8,64,1024]{2,1,0:T(8,128)(2,1)}) %all-gather.7.cloned.1.call-update) | async-done | bytes 1048592 | tf_op jit(solution)/shard_map/all_gather | solution.py:36
  62.3 42.0 %all-gather.11.cloned.1.call-done = bf16[8,64,5120]{2,1,0:T(8,128)(2,1)} async-done(((bf16[2,64,5120]{2,1,0:T(8,128)(2,1)}), bf16[8,64,5120]{2,1,0:T(8,128)(2,1)}) %all-gather.11.cloned.1.call-update) | async-done | bytes 5242896 | tf_op jit(solution)/shard_map/all_gather | solution.py:35
  104.4 5.2 %broadcast_in_dim.36 = f32[8,64,5120]{2,1,0:T(8,128)} broadcast(f32[]{:T(128)} %constant.77.clone.1), dimensions={} | broadcast | bytes 10485764 | tf_op jit(solution)/shard_map/broadcast_in_dim | solution.py:73
  109.6 1.6 broadcast_in_dim.37
  111.2 60.4 %while.16 = (s32[]{:T(128)}, f32[8,64,5120]{2,1,0:T(8,128)}, f32[8,64,1024]{2,1,0:T(8,128)}, f32[4,128,5120]{2,1,0:T(8,128)}, s32[4]{0:T(128)S(1)}, /*index=5*/b...) while((s32[]{:T(128)}, f32[8,64,5120]{2,1,0:T(8,128)}, ...), condition=%wide.region_2.3_spmd, body=%wide.region_0.2_spmd.sunk | while | flops 286089216 | bytes 10410184 | solution.py:75
  115.0 3.3 fusion.68
  118.9 3.7 fusion.66
  122.7 3.7 fusion.67
  130.1 3.1 fusion.68
  133.9 3.8 fusion.66
  137.7 3.7 fusion.67
  145.1 3.1 fusion.68
  149.0 3.8 fusion.66
  152.8 3.7 fusion.67
  160.2 3.1 fusion.68
  164.0 3.8 fusion.66
  167.9 3.7 fusion.67
  171.6 3.3 broadcast_multiply_fusion.1
  174.9 9.8 %broadcast_multiply_fusion = f32[8,64,5120]{2,1,0:T(8,128)} fusion(f32[8,64,5120]{2,1,0:T(8,128)} %get-tuple-element.77), kind=kLoop, calls=%fused_computation.36 | loop fusion | flops 2621440 | bytes 20971520 | tf_op jit(solution)/shard_map/mul | solution.py:83
  184.8 1.8 all-gather.5.cloned.1.call-done
  186.6 9.7 %fusion.38 = f32[2048,1280]{1,0:T(8,128)} fusion(bf16[2048,1024]{1,0:T(8,128)(2,1)} %all-gather.5.cloned.1.call-done, bf16[1280,1024]{1,0:T(8,128)(2,1)S(1)} %copy-done), kind=kOutput, calls=%fused_computation.42 | convolution fusion | flops 5368709120 | bytes 17301504 | tf_op jit(solution)/shard_map/tk,dk->td/dot_general | solution.py:39
  196.3 6.0 %all-to-all-start = ((f32[4,512,1280]{2,1,0:T(8,128)}), f32[4,512,1280]{2,1,0:T(8,128)}, u32[]{:S(2)}, u32[]{:S(2)}) async-start(f32[4,512,1280]{2,1,0:T(8,128)} %bitcast.91), calls=%async_computation | async-start | bytes 20971520 | tf_op jit(solution)/shard_map/all_to_all | solution.py:40
  202.4 17.2 %reduce-scatter.8.cloned.1.call-done = f32[2,64,1024]{2,1,0:T(8,128)} async-done(((f32[8,64,1024]{2,1,0:T(8,128)}), f32[2,64,1024]{2,1,0:T(8,128)}) %reduce-scatter.8.cloned.1.call-update) | async-done | bytes 524304 | tf_op jit(solution)/shard_map/reduce_scatter | solution.py:86
  219.6 87.9 %reduce-scatter.4.cloned.1.call-done = f32[2,64,5120]{2,1,0:T(8,128)} async-done(((f32[8,64,5120]{2,1,0:T(8,128)}), f32[2,64,5120]{2,1,0:T(8,128)}) %reduce-scatter.4.cloned.1.call-update) | async-done | bytes 2621456 | tf_op jit(solution)/shard_map/reduce_scatter | solution.py:85
  307.6 139.9 %all-to-all-done = f32[4,512,1280]{2,1,0:T(8,128)} async-done(((f32[4,512,1280]{2,1,0:T(8,128)}), f32[4,512,1280]{2,1,0:T(8,128)}, u32[]{:S(2)}, u32[]{:S(2)}) %all-to-all-start) | async-done | bytes 10485792 | tf_op jit(solution)/shard_map/all_to_all | solution.py:40
  447.5 9.5 %copy.12 = f32[4,64,8,1280]{3,2,0,1:T(8,128)} copy(f32[4,64,8,1280]{3,2,1,0:T(8,128)} %bitcast.15) | data formatting | bytes 20971520 | tf_op jit(solution)/shard_map/all_to_all | solution.py:40
  457.0 11.1 %fusion.36 = bf16[512,5120]{1,0:T(8,128)(2,1)} fusion(f32[512,5120]{1,0:T(8,128)} %bitcast.89, f32[4,128,5120]{2,1,0:T(8,128)} %get-tuple-element.76), kind=kLoop, calls=%fused_computation.35 | loop fusion | flops 5242880 | bytes 26214400 | tf_op jit(solution)/shard_map/convert_element_type | solution.py:80
  468.0 32.3 %reduce-scatter.6.cloned.1.call-done = f32[2,64,1280]{2,1,0:T(8,128)} async-done(((f32[2,64,5120]{2,1,0:T(8,128)}), f32[2,64,1280]{2,1,0:T(8,128)}) %reduce-scatter.6.cloned.1.call-update) | async-done | bytes 655376 | tf_op jit(solution)/shard_map/reduce_scatter | solution.py:88
  500.4 1.9 copy.29
  (39 shorter events, 12.6 us)
Async XLA Ops:
  7.2 179.4 %copy-start = (bf16[1280,1024]{1,0:T(8,128)(2,1)S(1)}, bf16[1280,1024]{1,0:T(8,128)(2,1)}, u32[]{:S(2)}) copy-start(bf16[1280,1024]{1,0:T(8,128)(2,1)} %param.15) | copy-start | bytes 7864324
  7.2 37.8 %all-gather.9.cloned.1.call-start = ((), (), s32[]{:S(2)}) async-start(), calls=%async_computation.6 | async-start | bytes 1638400 | tf_op jit(solution)/shard_map/all_gather | solution.py:33
  7.9 54.4 %all-gather.7.cloned.1.call-start = ((), (), s32[]{:S(2)}) async-start(), calls=%async_computation.5 | async-start | bytes 1310720 | tf_op jit(solution)/shard_map/all_gather | solution.py:36
  8.7 95.7 %all-gather.11.cloned.1.call-start = ((), (), s32[]{:S(2)}) async-start(), calls=%async_computation.7 | async-start | bytes 6553600 | tf_op jit(solution)/shard_map/all_gather | solution.py:35
  45.0 141.5 %all-gather.5.cloned.1.call-start = ((), (), s32[]{:S(2)}) async-start(), calls=%async_computation.4 | async-start | bytes 5242880 | tf_op jit(solution)/shard_map/all_gather | solution.py:38
  48.2 171.4 %reduce-scatter.8.cloned.1.call-start = ((), (), s32[]{:S(2)}) async-start(), calls=%async_computation.10 | async-start | bytes 2621440 | tf_op jit(solution)/shard_map/reduce_scatter | solution.py:86
  104.4 6.8 %copy-start.2 = (s32[3]{0:T(128)S(1)}, s32[3]{0:T(128)}, u32[]{:S(2)}) copy-start(s32[3]{0:T(128)} %constant.71.clone.1) | copy-start | bytes 40
  104.4 6.8 %copy-start.3 = (s32[4]{0:T(128)S(1)}, s32[4]{0:T(128)}, u32[]{:S(2)}) copy-start(s32[4]{0:T(128)} %param.18) | copy-start | bytes 52
  174.9 132.6 %reduce-scatter.4.cloned.1.call-start = ((), (), s32[]{:S(2)}) async-start(), calls=%async_computation.8 | async-start | bytes 13107200 | tf_op jit(solution)/shard_map/reduce_scatter | solution.py:85
  196.3 251.2 %all-to-all-start = ((f32[4,512,1280]{2,1,0:T(8,128)}), f32[4,512,1280]{2,1,0:T(8,128)}, u32[]{:S(2)}, u32[]{:S(2)}) async-start(f32[4,512,1280]{2,1,0:T(8,128)} %bitcast.91), calls=%async_computation | async-start | bytes 20971520 | tf_op jit(solution)/shard_map/all_to_all | solution.py:40
  202.3 265.7 %all-reduce.2.cloned.1.call-start = ((), (), s32[]{:S(2)}) async-start(), calls=%async_computation.11 | async-start | bytes 1048576 | tf_op jit(solution)/shard_map/psum | solution.py:89
  219.6 280.8 %reduce-scatter.6.cloned.1.call-start = ((), (), s32[]{:S(2)}) async-start(), calls=%async_computation.9 | async-start | bytes 3276800 | tf_op jit(solution)/shard_map/reduce_scatter | solution.py:88
  457.0 45.3 %copy-start.1 = (bf16[1280,1024]{1,0:T(8,128)(2,1)S(1)}, bf16[1280,1024]{1,0:T(8,128)(2,1)}, u32[]{:S(2)}) copy-start(bf16[1280,1024]{1,0:T(8,128)(2,1)} %param.15) | copy-start | bytes 7864324
Sparse Core Ops, SparseCore 0:
  9.6 35.3 all-gather.8
  46.6 15.7 all-gather.6
  63.9 40.4 all-gather.10
  105.8 80.7 all-gather.4
  189.5 29.9 reduce-scatter.7
  222.2 85.2 reduce-scatter.3
  310.0 100.4 all-reduce.1
  413.4 86.8 reduce-scatter.5
where the time goes:
time: 510 us; the launch traced here: 509 us
  waiting for transfers between devices  371 us (73%)
  matrix products  57.1 us (11%)
  other arithmetic  32.6 us (6%)
  local copies, waits for them, and re-layouts  20.6 us (4%)
  between operations  14.2 us (3%)
  loops' own time  7.83 us (2%)
  starting transfers between devices  6.31 us (1%)
    all_to_all x1, waiting for transfers between devices, body(): lax.all_to_all(blocks, 'fsdp', split_axis=0, concat_axis=1, tiled=True)  140 us
    reduce_scatter x1, waiting for transfers between devices, body(): lax.psum_scatter(down_accumulator, 'dp', scatter_dimension=0, tiled=True)  87.9 us
    all_gather x1, waiting for transfers between devices, body(): lax.all_gather(widened_down, 'dp', axis=0, tiled=True)  42 us
    all_gather x1, waiting for transfers between devices, body(): widened_down = lax.all_gather(adapter_down, 'fsdp', axis=2, tiled=True)  36.3 us
    reduce_scatter x1, waiting for transfers between devices, body(): grad_a = lax.psum_scatter(owned_a, 'fsdp', scatter_dimension=2, tiled=True)  32.3 us
    reduce_scatter x1, waiting for transfers between devices, body(): lax.psum_scatter(up_accumulator, 'dp', scatter_dimension=0, tiled=True)  17.2 us
    dot_general x4, matrix products, tile_step(): jnp.einsum('tr,td->rd', rank_activations, x_tile, preferred_element_type=...  15.1 us
    dot_general x4, matrix products, tile_step(): jnp.einsum('tr,tk->rk', projected_rows, value_grad_tile, preferred_elemen...  14.8 us
  transfers between devices with their start and end apart: 9, of which 8 were waited for; matrix products, arithmetic and copies ran while one was open for 21% of the time, Pallas kernels for 0%

commit v1 on v0

v1 whole, which is shorter than its diff:
```python
import math

import jax
import jax.numpy as jnp
from jax import lax
from jax.sharding import Mesh
from jax.sharding import PartitionSpec as P

adapter_scale = 2.0
cores = 2


def shift(value, axis, by):
    size = lax.axis_size(axis)
    return lax.ppermute(value, axis, [(i, (i + by) % size) for i in range(size)])


def gather_steps(value, axis):
    blocks = [value]
    for _ in range(lax.axis_size(axis) - 1):
        blocks.append(shift(blocks[-1], axis, 1))
    return blocks


def body(tokens, value_cotangent, value_weight, adapter_down, adapter_up, tile_token_policy, tile_live_length):
    y_size, x_size, c_size, z_size = (lax.axis_size(a) for a in ("league", "x", "core", "fsdp"))
    y, x, c, z = (lax.axis_index(a) for a in ("league", "x", "core", "fsdp"))
    rows, width = tokens.shape
    kv = value_cotangent.shape[1]
    tiles = tile_token_policy.shape[0]
    tile_rows = rows // tiles
    own_policies, rank, cols = adapter_down.shape
    half = own_policies * rank // y_size
    slices = y_size * x_size * c_size
    depth = kv // slices
    bf16, f32 = jnp.bfloat16, jnp.float32

    live = jnp.arange(tile_rows, dtype=jnp.int32)[None, :] < tile_live_length[:, None]
    live = live.reshape(rows, 1)
    masked = jnp.where(live, value_cotangent, jnp.zeros((), bf16))

    down_share = lax.dynamic_slice_in_dim(adapter_down.reshape(own_policies * rank, cols), y * half, half, 0)
    up_rows = adapter_up.reshape(y_size, half, kv)
    up_rows = jnp.stack([lax.dynamic_index_in_dim(up_rows, (y - s) % y_size, 0, False) for s in range(y_size)])
    up_x = jnp.stack(gather_steps(up_rows, "x"))
    up_all = jnp.stack(gather_steps(up_x, "core"))

    down_z = jnp.stack(gather_steps(down_share, "fsdp"))
    down_x = jnp.stack(gather_steps(down_z, "x"))
    down_y = jnp.stack(gather_steps(down_x, "league"))
    down_all = jnp.stack(gather_steps(down_y, "core"))

    back_c = (c - jnp.arange(c_size)) % c_size
    back_x = (x - jnp.arange(x_size)) % x_size
    back_y = (y - jnp.arange(y_size)) % y_size
    first_row = ((back_x[None, :, None] * c_size + back_c[:, None, None]) * y_size + back_y[None, None, :]) * half
    row_policy = (first_row[..., None] + jnp.arange(half)) // rank
    token_policy = jnp.repeat(tile_token_policy, tile_rows)[:, None]
    mine = token_policy == row_policy.reshape(1, -1)

    all_rows = slices * half
    low_rank = adapter_scale * jnp.einsum(
        "tk,rk->tr", masked, up_all.reshape(all_rows, kv), preferred_element_type=f32
    )
    low_rank = jnp.where(mine, low_rank, 0.0).astype(bf16)

    lr = low_rank.reshape(rows, c_size, all_rows // c_size)
    kept = jnp.einsum("tr,td->rd", lr[:, 0], tokens, preferred_element_type=f32)
    for s in range(1, c_size):
        part = jnp.einsum("tr,td->rd", lr[:, s], tokens, preferred_element_type=f32).astype(bf16)
        kept = kept + shift(part, "core", -s).astype(f32)
    kept = kept.reshape(x_size, y_size * half, width)
    own = kept[0]
    for s in range(1, x_size):
        own = own + shift(kept[s].astype(bf16), "x", -s).astype(f32)
    own = own.reshape(y_size * half, z_size, cols).swapaxes(0, 1).astype(bf16)
    parts_a = lax.all_to_all(own, "fsdp", split_axis=0, concat_axis=0, tiled=True)
    normalizer = 1.0 / math.sqrt(rows * x_size * c_size * z_size)
    grad_a = jnp.sum(parts_a.astype(f32), axis=0) * normalizer

    order = "cyxzrd,tzd->tcxyr"
    tok = tokens.reshape(rows, z_size, cols)
    tok = jnp.stack([lax.dynamic_index_in_dim(tok, (z - s) % z_size, 1, False) for s in range(z_size)])
    down_k = down_all.transpose(3, 0, 2, 1, 4, 5).reshape(z_size, all_rows, cols)
    projected = sum(
        jnp.einsum("td,rd->tr", tok[s], down_k[s], preferred_element_type=f32) for s in range(z_size)
    )
    projected = jnp.where(mine, projected, 0.0).astype(bf16)
    pr = projected.reshape(rows, c_size, all_rows // c_size)
    kept = jnp.einsum("tr,tk->rk", pr[:, 0], masked, preferred_element_type=f32)
    for s in range(1, c_size):
        part = jnp.einsum("tr,tk->rk", pr[:, s], masked, preferred_element_type=f32).astype(bf16)
        kept = kept + shift(part, "core", -s).astype(f32)
    kept = kept.reshape(x_size, y_size * half, kv)
    own = kept[0]
    for s in range(1, x_size):
        own = own + shift(kept[s].astype(bf16), "x", -s).astype(f32)
    own = own.reshape(z_size, -1, kv).astype(bf16)
    parts_b = lax.all_to_all(own, "fsdp", split_axis=0, concat_axis=0, tiled=True)
    own_b = (jnp.sum(parts_b.astype(f32), axis=0) * (adapter_scale * normalizer)).astype(bf16)
    spread = jnp.broadcast_to(own_b[None], (z_size,) + own_b.shape)
    grad_b = lax.all_to_all(spread, "fsdp", split_axis=0, concat_axis=0, tiled=True).astype(f32)
    grad_b = grad_b.reshape(y_size * half, kv)

    def unroll(value):
        value = value.reshape(y_size, half, -1)
        value = jnp.stack([lax.dynamic_index_in_dim(value, (y - k) % y_size, 0, False) for k in range(y_size)])
        return value.reshape(own_policies, rank, -1)

    me = (x * c_size + c) * y_size + y
    weight_share = lax.dynamic_slice_in_dim(value_weight, me * depth, depth, 1).T
    own_weight = value_weight
    weight = []
    held = weight_share
    for s in range(z_size):
        if s:
            held = shift(held, "fsdp", 1)
            got = jnp.stack(gather_steps(held, "x"))
            got = jnp.stack(gather_steps(got, "league"))
            got = jnp.stack(gather_steps(got, "core"))
            weight.append(got.reshape(kv, cols))
    order_k = [
        (((x - dx) % x_size) * c_size + (c - dc) % c_size) * y_size + (y - dy) % y_size
        for dc in range(c_size)
        for dy in range(y_size)
        for dx in range(x_size)
    ]
    masked_k = jnp.concatenate([lax.dynamic_slice_in_dim(masked, k * depth, depth, 1) for k in order_k], axis=1)
    out = jnp.zeros((rows, width), bf16)
    for s in range(z_size):
        if s == 0:
            block = jnp.einsum("tk,dk->td", masked, value_weight, preferred_element_type=f32)
        else:
            block = jnp.dot(masked_k, weight[s - 1], preferred_element_type=f32)
        block = block + jnp.dot(low_rank, down_k[s], preferred_element_type=f32)
        out = lax.dynamic_update_slice_in_dim(out, block.astype(bf16), ((z - s) % z_size) * cols, 1)
    return out, unroll(grad_a), unroll(grad_b)


def solution(mesh):
    league, dp, fsdp = mesh.devices.shape
    fine = Mesh(mesh.devices.reshape(league, dp // cores, cores, fsdp), ("league", "x", "core", "fsdp"))
    every = ("league", "x", "core", "fsdp")
    return jax.shard_map(
        body,
        mesh=fine,
        in_specs=(
            P(every, None),
            P(every, None),
            P("fsdp", None),
            P(("x", "core"), None, "fsdp"),
            P(("x", "core"), None, None),
            P(every),
            P(every),
        ),
        out_specs=(
            P(every, None),
            P(("league", "x", "core"), None, "fsdp"),
            P(("league", "x", "core"), None, None),
        ),
        check_vma=False,
    )
```

time: 510 us -> 232 us (0.45)
  waiting for transfers between devices: 371 us -> 106 us
  matrix products: 57.1 us -> 29.6 us
  starting transfers between devices: 6.31 us -> 31.8 us
  local copies, waits for them, and re-layouts: 20.6 us -> 36.1 us
  between operations: 14.2 us -> 1.13 us
  loops' own time: 7.83 us -> 0 us
  other arithmetic: 32.6 us -> 26.6 us
    reduce_scatter x3 -> x0, waiting for transfers between devices: 137 us -> none  [the longest x1 87.9 us: body(): lax.psum_scatter(down_accumulator, 'dp', scatter_dimension=0, tiled=True)]
    all_to_all x1 -> x3, waiting for transfers between devices: 140 us -> 22 us  [the longest x2 18.5 us: body(): lax.all_to_all(own, 'fsdp', split_axis=0, concat_axis=0, tiled=True)]
    all_gather x4 -> x0, waiting for transfers between devices: 91.8 us -> none  [the longest x1 42 us: body(): lax.all_gather(widened_down, 'dp', axis=0, tiled=True)]
    ppermute x0 -> x24, waiting for transfers between devices: none -> 83.9 us  [shift(): lax.ppermute(value, axis, [(i, (i + by) % size) for i in range(size)])]
    dot_general x17, matrix products: 57.1 us -> 29.6 us  [the longest x3 12.5 us: body(): block = jnp.dot(masked_k, weight[s - 1], preferred_element_type=f32)]
    unnamed x9 -> x53, local copies, waits for them, and re-layouts: 1.91 us -> 25 us
    ppermute x0 -> x24, starting transfers between devices: none -> 18.9 us  [shift(): lax.ppermute(value, axis, [(i, (i + by) % size) for i in range(size)])]
    another operation x4 -> x18, other arithmetic: 2.88 us -> 19.4 us  [the longest x6 10.6 us: body(): got = jnp.stack(gather_steps(got, 'core'))]
  transfers between devices with their start and end apart: 9 -> 27, of which waited for: 8 -> 15; matrix products, arithmetic and copies ran while one was open for 21% -> 35% of each run, Pallas kernels for 0% -> 0%
where the time goes in v1:
time: 232 us; the launch traced here: 231 us
  waiting for transfers between devices  106 us (46%)
  local copies, waits for them, and re-layouts  36.1 us (16%)
  starting transfers between devices  31.8 us (14%)
  matrix products  29.6 us (13%)
  other arithmetic  26.6 us (11%)
    ppermute x24, waiting for transfers between devices, shift(): lax.ppermute(value, axis, [(i, (i + by) % size) for i in range(size)])  83.9 us
    unnamed x53, local copies, waits for them, and re-layouts  25 us
    ppermute x24, starting transfers between devices, shift(): lax.ppermute(value, axis, [(i, (i + by) % size) for i in range(size)])  18.9 us
    all_to_all x2, waiting for transfers between devices, body(): lax.all_to_all(own, 'fsdp', split_axis=0, concat_axis=0, tiled=True)  18.5 us
    dot_general x3, matrix products, body(): block = jnp.dot(masked_k, weight[s - 1], preferred_element_type=f32)  12.5 us
    another operation x6, other arithmetic, body(): got = jnp.stack(gather_steps(got, 'core'))  10.6 us
    all_to_all x2, starting transfers between devices, body(): lax.all_to_all(own, 'fsdp', split_axis=0, concat_axis=0, tiled=True)  9.09 us
    dot_general x4, matrix products, body(): block = block + jnp.dot(low_rank, down_k[s], preferred_element_type=f32)  5.9 us
  transfers between devices with their start and end apart: 27, of which 15 were waited for; matrix products, arithmetic and copies ran while one was open for 35% of the time, Pallas kernels for 0%

profile of v1, /device:TPU:0, one launch (start us, length us, event | category | flops | bytes accessed | tf_op | source)
XLA Modules:
  0.0 231.2 jit_solution(7858101624132889010)
XLA Ops:
  0.7 1.7 constant_dynamic-slice_fusion.5
  2.4 3.0 %collective-permute-start.2 = (bf16[64,1280]{1,0:T(8,128)(2,1)}, bf16[64,1280]{1,0:T(8,128)(2,1)}, u32[]{:S(2)}, u32[]{:S(2)}) collective-permute-start(bf16[64,1280]{1,0:T(8,128)(2,1)} %constant_dynamic-slice_fusion.5), channel_id=1, source_target_pairs={{0,1},{1,2},{2,3},{3,0},{4,5},{5,6},{6,7},{7,4},{8,9},{9,10},{10,1... | collective-permute-start | bytes 491528 | tf_op jit(solution)/shard_map/ppermute | solution.py:15
  12.2 2.4 %broadcast_select_fusion = bf16[512,1024]{1,0:T(8,128)(2,1)} fusion(bf16[512,1024]{1,0:T(8,128)(2,1)} %param.8, pred[512]{0:T(512)(128)(4,1)S(1)} %fusion.32), kind=kLoop, calls=%fused_computation.48 | loop fusion | flops 524288 | bytes 2097664 | tf_op jit(solution)/shard_map/jit(_where)/select_n | solution.py:40
  21.0 3.1 %collective-permute-done.3 = bf16[64,1280]{1,0:T(8,128)(2,1)S(1)} collective-permute-done((bf16[64,1280]{1,0:T(8,128)(2,1)}, bf16[64,1280]{1,0:T(8,128)(2,1)S(1)}, u32[]{:S(2)}, u32[]{:S(2)}) %collective-permute-start.3) | collective-permute-done | bytes 163872 | tf_op jit(solution)/shard_map/ppermute | solution.py:15
  27.3 3.9 %collective-permute-done.4 = bf16[64,1280]{1,0:T(8,128)(2,1)S(1)} collective-permute-done((bf16[64,1280]{1,0:T(8,128)(2,1)S(1)}, bf16[64,1280]{1,0:T(8,128)(2,1)S(1)}, u32[]{:S(2)}, u32[]{:S(2)}) %collective-permute-start.4) | collective-permute-done | bytes 163872 | tf_op jit(solution)/shard_map/ppermute | solution.py:15
  31.9 2.1 fusion.47
  36.2 7.9 %copy.28 = bf16[512,5120]{0,1:T(8,128)(2,1)} copy(bf16[512,5120]{1,0:T(8,128)(2,1)} %param.7) | data formatting | bytes 10485760 | tf_op args[0]
  47.1 4.9 %collective-permute-done.5 = bf16[4,64,1280]{2,1,0:T(8,128)(2,1)} collective-permute-done((bf16[4,64,1280]{2,1,0:T(8,128)(2,1)}, bf16[4,64,1280]{2,1,0:T(8,128)(2,1)}, u32[]{:S(2)}, u32[]{:S(2)}) %collective-permute-start.5) | collective-permute-done | bytes 655392 | tf_op jit(solution)/shard_map/ppermute | solution.py:15
  63.7 6.5 %collective-permute-done.16 = bf16[128,1280]{1,0:T(8,128)(2,1)S(1)} collective-permute-done((bf16[128,1280]{1,0:T(8,128)(2,1)S(1)}, bf16[128,1280]{1,0:T(8,128)(2,1)S(1)}, u32[]{:S(2)}, u32[]{:S(2)}) %collective-permute-start.16) | collective-permute-done | bytes 327712 | tf_op jit(solution)/shard_map/ppermute | solution.py:15
  70.7 14.3 %collective-permute-done.6 = bf16[2,4,64,1280]{3,2,0,1:T(8,128)(2,1)S(1)} collective-permute-done((bf16[2,4,64,1280]{3,2,0,1:T(8,128)(2,1)S(1)}, bf16[2,4,64,1280]{3,2,0,1:T(8,128)(2,1)S(1)}, u32[]{:S(2)}, u32[]{:S(2)}) %collective-permute-start.6) | collective-permute-done | bytes 1310752 | tf_op jit(solution)/shard_map/ppermute | solution.py:15
  85.4 8.1 %collective-permute-done.10 = bf16[2,128,1280]{2,1,0:T(8,128)(2,1)S(1)} collective-permute-done((bf16[2,128,1280]{2,1,0:T(8,128)(2,1)S(1)}, bf16[2,128,1280]{2,1,0:T(8,128)(2,1)S(1)}, u32[]{:S(2)}, u32[]{:S(2)}) %collective-permute-start.10) | collective-permute-done | bytes 655392 | tf_op jit(solution)/shard_map/ppermute | solution.py:15
  96.2 3.0 %fusion.50 = f32[512,1280]{1,0:T(8,128)} fusion(bf16[512,1024]{1,0:T(8,128)(2,1)S(1)} %copy-done.2, bf16[1280,1024]{1,0:T(8,128)(2,1)S(1)} %copy-done), kind=kOutput, calls=%fused_computation.128 | convolution fusion | flops 1342177280 | bytes 6291456 | tf_op jit(solution)/shard_map/tk,dk->td/dot_general | solution.py:132
  99.2 12.3 %collective-permute-done.14 = bf16[2,128,1280]{2,1,0:T(8,128)(2,1)S(1)} collective-permute-done((bf16[2,128,1280]{2,1,0:T(8,128)(2,1)S(1)}, bf16[2,128,1280]{2,1,0:T(8,128)(2,1)S(1)}, u32[]{:S(2)}, u32[]{:S(2)}) %collective-permute-start.14) | collective-permute-done | bytes 655392 | tf_op jit(solution)/shard_map/ppermute | solution.py:15
  112.8 12.4 %collective-permute-done.18 = bf16[2,128,1280]{2,1,0:T(8,128)(2,1)S(1)} collective-permute-done((bf16[2,128,1280]{2,1,0:T(8,128)(2,1)S(1)}, bf16[2,128,1280]{2,1,0:T(8,128)(2,1)S(1)}, u32[]{:S(2)}, u32[]{:S(2)}) %collective-permute-start.18) | collective-permute-done | bytes 655392 | tf_op jit(solution)/shard_map/ppermute | solution.py:15
  126.4 1.7 pad_maximum_fusion.1
  128.1 1.6 convert_add_fusion
  132.8 3.3 %slice-done.3 = s8[4194304]{0:T(1024)(128)(4,1)S(1)} async-done(((s8[5242880]{0:T(1024)(128)(4,1)}), s8[4194304]{0:T(1024)(128)(4,1)S(1)}, s32[]{:S(2)}) %slice-start.3) | async-done | bytes 4194328
  140.2 3.1 %pad_maximum_fusion.2 = bf16[2,2,2,128,1280]{4,3,2,1,0:T(8,128)(2,1)} fusion(bf16[1,2,2,128,1280]{4,3,2,1,0:T(8,128)(2,1)} %bitcast.37, bf16[1,2,2,128,1280]{4,3,2,1,0:T(8,128)(2,1)S(1)} %get-tuple-element.11), kind=kLoop, calls=%fused_computation.20 | loop fusion | flops 1310720 | bytes 5242880 | tf_op jit(solution)/shard_map/stack | solution.py:120
  143.3 3.1 %pad_maximum_fusion.3 = bf16[2,2,2,128,1280]{4,3,2,1,0:T(8,128)(2,1)} fusion(bf16[1,2,2,128,1280]{4,3,2,1,0:T(8,128)(2,1)} %bitcast.45, bf16[1,2,2,128,1280]{4,3,2,1,0:T(8,128)(2,1)S(1)} %get-tuple-element.9), kind=kLoop, calls=%fused_computation.21 | loop fusion | flops 1310720 | bytes 5242880 | tf_op jit(solution)/shard_map/stack | solution.py:120
  148.5 14.4 %collective-permute-done.21 = bf16[128,5120]{1,0:T(8,128)(2,1)} collective-permute-done((bf16[128,5120]{1,0:T(8,128)(2,1)}, bf16[128,5120]{1,0:T(8,128)(2,1)}, u32[]{:S(2)}, u32[]{:S(2)}) %collective-permute-start.21) | collective-permute-done | bytes 1310752 | tf_op jit(solution)/shard_map/ppermute | solution.py:15
  165.6 2.4 %collective-permute-done.23 = bf16[128,1024]{1,0:T(8,128)(2,1)S(1)} collective-permute-done((bf16[128,1024]{1,0:T(8,128)(2,1)S(1)}, bf16[128,1024]{1,0:T(8,128)(2,1)S(1)}, u32[]{:S(2)}, u32[]{:S(2)}) %collective-permute-start.23) | collective-permute-done | bytes 262176 | tf_op jit(solution)/shard_map/ppermute | solution.py:15
  168.8 4.8 %all-to-all-start.1 = ((bf16[4,32,1024]{2,1,0:T(8,128)(2,1)}), bf16[4,32,1024]{2,1,0:T(8,128)(2,1)S(1)}, u32[]{:S(2)}, u32[]{:S(2)}) async-start(bf16[4,32,1024]{2,1,0:T(8,128)(2,1)} %bitcast.61), calls=%async_computation.1 | async-start | bytes 524288 | tf_op jit(solution)/shard_map/all_to_all | solution.py:99
  173.6 2.2 fusion.51
  175.8 3.0 %broadcast_in_dim.36 = bf16[512,5120]{1,0:T(8,128)(2,1)} broadcast(bf16[]{:T(256)} %constant.197.clone.1), dimensions={} | broadcast | bytes 5242882 | tf_op jit(solution)/shard_map/broadcast_in_dim | solution.py:129
  179.2 2.0 fusion.7
  183.2 3.9 %all-to-all-start.2 = ((bf16[4,32,1024]{2,1,0:T(8,128)(2,1)}), bf16[4,32,1024]{2,1,0:T(8,128)(2,1)S(1)}, u32[]{:S(2)}, u32[]{:S(2)}) async-start(bf16[4,32,1024]{2,1,0:T(8,128)(2,1)} %broadcast_in_dim.41), calls=%async_computation.2 | async-start | bytes 524288 | tf_op jit(solution)/shard_map/all_to_all | solution.py:102
  187.1 4.6 %fusion.1 = bf16[512,5120]{1,0:T(8,128)(2,1)} fusion(bf16[512,5120]{1,0:T(8,128)(2,1)} %fusion.7, s32[]{:T(128)S(6)} %select_n.240, f32[512,1280]{1,0:T(8,128)S(1)} %fusion.51, bf16[512,1024]{1,0:T(8,128)(2,1)} %dynamic-slice_dynamic-update-slice_fusion, bf16[1024,1280]{1,0:T(8,128)(2,1)} %bitcast.163), kind=kOutput, calls=%fused_computation.8 | convolution fusion | flops 1343488000 | bytes 7602180 | tf_op jit(solution)/shard_map/dot_general | solution.py:134
  191.7 3.6 %all-to-all-done.2 = bf16[4,32,1024]{2,1,0:T(8,128)(2,1)S(1)} async-done(((bf16[4,32,1024]{2,1,0:T(8,128)(2,1)}), bf16[4,32,1024]{2,1,0:T(8,128)(2,1)S(1)}, u32[]{:S(2)}, u32[]{:S(2)}) %all-to-all-start.2) | async-done | bytes 262176 | tf_op jit(solution)/shard_map/all_to_all | solution.py:102
  195.3 4.3 %all-to-all-start = ((bf16[4,128,1280]{2,1,0:T(8,128)(2,1)}), bf16[4,128,1280]{2,1,0:T(8,128)(2,1)}, u32[]{:S(2)}, u32[]{:S(2)}) async-start(bf16[4,128,1280]{2,1,0:T(8,128)(2,1)} %bitcast.159), calls=%async_computation | async-start | bytes 2621440 | tf_op jit(solution)/shard_map/all_to_all | solution.py:77
  202.6 4.0 %fusion.3 = bf16[512,5120]{1,0:T(8,128)(2,1)} fusion(bf16[512,5120]{1,0:T(8,128)(2,1)} %fusion.1, s32[]{:T(128)S(6)} %select_n.242, f32[512,1280]{1,0:T(8,128)S(1)} %fusion.52, bf16[512,1024]{1,0:T(8,128)(2,1)} %dynamic-slice_dynamic-update-slice_fusion, bf16[1024,1280]{1,0:T(8,128)(2,1)S(1)} %bitcast.164), kind=kOutput, calls=%fused_computation.10 | convolution fusion | flops 1343488000 | bytes 7602180 | tf_op jit(solution)/shard_map/dot_general | solution.py:134
  206.6 3.8 %fusion.5 = bf16[512,5120]{1,0:T(8,128)(2,1)} fusion(bf16[512,5120]{1,0:T(8,128)(2,1)} %fusion.3, s32[]{:T(128)S(6)} %select_n.244, f32[512,1280]{1,0:T(8,128)S(1)} %fusion.53, bf16[512,1024]{1,0:T(8,128)(2,1)} %dynamic-slice_dynamic-update-slice_fusion, bf16[1024,1280]{1,0:T(8,128)(2,1)S(1)} %bitcast.165), kind=kOutput, calls=%fused_computation.12 | convolution fusion | flops 1343488000 | bytes 7602180 | tf_op jit(solution)/shard_map/dot_general | solution.py:134
  211.4 17.3 %all-to-all-done = bf16[4,128,1280]{2,1,0:T(8,128)(2,1)} async-done(((bf16[4,128,1280]{2,1,0:T(8,128)(2,1)}), bf16[4,128,1280]{2,1,0:T(8,128)(2,1)}, u32[]{:S(2)}, u32[]{:S(2)}) %all-to-all-start) | async-done | bytes 1310752 | tf_op jit(solution)/shard_map/all_to_all | solution.py:77
  (142 shorter events, 61.4 us)
Async XLA Ops:
  0.6 10.6 %copy-start.13 = (bf16[2,64,1280]{2,1,0:T(8,128)(2,1)S(1)}, bf16[2,64,1280]{2,1,0:T(8,128)(2,1)}, u32[]{:S(2)}) copy-start(bf16[2,64,1280]{2,1,0:T(8,128)(2,1)} %param.10) | copy-start | bytes 983044
  0.7 11.3 %copy-start.17 = (s32[4]{0:T(128)S(1)}, s32[4]{0:T(128)}, u32[]{:S(2)}) copy-start(s32[4]{0:T(128)} %param.13) | copy-start | bytes 52
  2.4 13.8 %collective-permute-start.2 = (bf16[64,1280]{1,0:T(8,128)(2,1)}, bf16[64,1280]{1,0:T(8,128)(2,1)}, u32[]{:S(2)}, u32[]{:S(2)}) collective-permute-start(bf16[64,1280]{1,0:T(8,128)(2,1)} %constant_dynamic-slice_fusion.5), channel_id=1, source_target_pairs={{0,1},{1,2},{2,3},{3,0},{4,5},{5,6},{6,7},{7,4},{8,9},{9,10},{10,1... | collective-permute-start | bytes 491528 | tf_op jit(solution)/shard_map/ppermute | solution.py:15
  7.2 38.6 %collective-permute-start = (bf16[2,64,1024]{2,1,0:T(8,128)(2,1)}, bf16[2,64,1024]{2,1,0:T(8,128)(2,1)}, u32[]{:S(2)}, u32[]{:S(2)}) collective-permute-start(bf16[2,64,1024]{2,1,0:T(8,128)(2,1)} %get-tuple-element.32), channel_id=1, source_target_pairs={{0,8},{8,0},{1,9},{9,1},{2,10},{10,2},{3,11},{11,3},{4,12},{12,4},... | collective-permute-start | bytes 786440 | tf_op jit(solution)/shard_map/ppermute | solution.py:15
  9.7 34.5 %collective-permute-start.8 = (bf16[128,1280]{1,0:T(8,128)(2,1)}, bf16[128,1280]{1,0:T(8,128)(2,1)}, u32[]{:S(2)}, u32[]{:S(2)}) collective-permute-start(bf16[128,1280]{1,0:T(8,128)(2,1)} %bitcast.179), channel_id=1, source_target_pairs={{0,1},{1,2},{2,3},{3,0},{4,5},{5,6},{6,7},{7,4},{8,9},{9,10},{10,1... | collective-permute-start | bytes 983048 | tf_op jit(solution)/shard_map/ppermute | solution.py:15
  12.2 22.3 %copy-start.16 = (s32[4]{0:T(128)S(1)}, s32[4]{0:T(128)}, u32[]{:S(2)}) copy-start(s32[4]{0:T(128)} %param.12) | copy-start | bytes 52
  16.3 7.8 %collective-permute-start.3 = (bf16[64,1280]{1,0:T(8,128)(2,1)}, bf16[64,1280]{1,0:T(8,128)(2,1)S(1)}, u32[]{:S(2)}, u32[]{:S(2)}) collective-permute-start(bf16[64,1280]{1,0:T(8,128)(2,1)} %collective-permute-done.2), channel_id=1, source_target_pairs={{0,1},{1,2},{2,3},{3,0},{4,5},{5,6},{6,7},{7,4},{8,9},{9,10},{10,1... | collective-permute-start | bytes 491528 | tf_op jit(solution)/shard_map/ppermute | solution.py:15
  24.1 7.1 %collective-permute-start.4 = (bf16[64,1280]{1,0:T(8,128)(2,1)S(1)}, bf16[64,1280]{1,0:T(8,128)(2,1)S(1)}, u32[]{:S(2)}, u32[]{:S(2)}) collective-permute-start(bf16[64,1280]{1,0:T(8,128)(2,1)S(1)} %collective-permute-done.3), channel_id=1, source_target_pairs={{0,1},{1,2},{2,3},{3,0},{4,5},{5,6},{6,7},{7,4},{8,9},{9,10},{10,1... | collective-permute-start | bytes 491528 | tf_op jit(solution)/shard_map/ppermute | solution.py:15
  34.0 18.0 %collective-permute-start.5 = (bf16[4,64,1280]{2,1,0:T(8,128)(2,1)}, bf16[4,64,1280]{2,1,0:T(8,128)(2,1)}, u32[]{:S(2)}, u32[]{:S(2)}) collective-permute-start(bf16[4,64,1280]{2,1,0:T(8,128)(2,1)} %get-tuple-element.26), channel_id=1, source_target_pairs={{0,8},{8,0},{1,9},{9,1},{2,10},{10,2},{3,11},{11,3},{4,12},{12,4},... | collective-permute-start | bytes 1966088 | tf_op jit(solution)/shard_map/ppermute | solution.py:15
  44.2 11.3 %collective-permute-start.9 = (bf16[128,1280]{1,0:T(8,128)(2,1)}, bf16[128,1280]{1,0:T(8,128)(2,1)S(1)}, u32[]{:S(2)}, u32[]{:S(2)}) collective-permute-start(bf16[128,1280]{1,0:T(8,128)(2,1)} %collective-permute-done.8), channel_id=1, source_target_pairs={{0,8},{8,0},{1,9},{9,1},{2,10},{10,2},{3,11},{11,3},{4,12},{12,4},... | collective-permute-start | bytes 983048 | tf_op jit(solution)/shard_map/ppermute | solution.py:15
  45.8 14.2 %slice-start = ((s8[5242880]{0:T(1024)(128)(4,1)}), s8[4194304]{0:T(1024)(128)(4,1)S(1)}, s32[]{:S(2)}) async-start(s8[5242880]{0:T(1024)(128)(4,1)} %bitcast.142), calls=%async_computation.3 | async-start | bytes 8388608
  46.9 12.2 %collective-permute-start.1 = (bf16[2,2,64,1024]{3,2,1,0:T(8,128)(2,1)S(1)}, bf16[2,2,64,1024]{3,2,1,0:T(8,128)(2,1)S(1)}, u32[]{:S(2)}, u32[]{:S(2)}) collective-permute-start(bf16[2,2,64,1024]{3,2,1,0:T(8,128)(2,1)S(1)} %get-tuple-element.30), channel_id=1, source_target_pairs={{0,4},{4,0},{1,5},{5,1},{2,6},{6,2},{3,7},{7,3},{8,12},{12,8},{9,1... | collective-permute-start | bytes 1572872 | tf_op jit(solution)/shard_map/ppermute | solution.py:15
  47.0 12.1 %collective-permute-start.12 = (bf16[128,1280]{1,0:T(8,128)(2,1)}, bf16[128,1280]{1,0:T(8,128)(2,1)S(1)}, u32[]{:S(2)}, u32[]{:S(2)}) collective-permute-start(bf16[128,1280]{1,0:T(8,128)(2,1)} %collective-permute-done.8), channel_id=1, source_target_pairs={{0,1},{1,2},{2,3},{3,0},{4,5},{5,6},{6,7},{7,4},{8,9},{9,10},{10,1... | collective-permute-start | bytes 983048 | tf_op jit(solution)/shard_map/ppermute | solution.py:15
  53.2 31.8 %collective-permute-start.6 = (bf16[2,4,64,1280]{3,2,0,1:T(8,128)(2,1)S(1)}, bf16[2,4,64,1280]{3,2,0,1:T(8,128)(2,1)S(1)}, u32[]{:S(2)}, u32[]{:S(2)}) collective-permute-start(bf16[2,4,64,1280]{3,2,0,1:T(8,128)(2,1)S(1)} %get-tuple-element.16), channel_id=1, source_target_pairs={{0,16},{16,0},{1,17},{17,1},{2,18},{18,2},{3,19},{19,3},{4,20},{20... | collective-permute-start | bytes 3932168 | tf_op jit(solution)/shard_map/ppermute | solution.py:15
  56.6 36.9 %collective-permute-start.10 = (bf16[2,128,1280]{2,1,0:T(8,128)(2,1)S(1)}, bf16[2,128,1280]{2,1,0:T(8,128)(2,1)S(1)}, u32[]{:S(2)}, u32[]{:S(2)}) collective-permute-start(bf16[2,128,1280]{2,1,0:T(8,128)(2,1)S(1)} %get-tuple-element.24), channel_id=1, source_target_pairs={{0,16},{16,0},{1,17},{17,1},{2,18},{18,2},{3,19},{19,3},{4,20},{20... | collective-permute-start | bytes 1966088 | tf_op jit(solution)/shard_map/ppermute | solution.py:15
  59.1 11.1 %collective-permute-start.16 = (bf16[128,1280]{1,0:T(8,128)(2,1)S(1)}, bf16[128,1280]{1,0:T(8,128)(2,1)S(1)}, u32[]{:S(2)}, u32[]{:S(2)}) collective-permute-start(bf16[128,1280]{1,0:T(8,128)(2,1)S(1)} %collective-permute-done.12), channel_id=1, source_target_pairs={{0,1},{1,2},{2,3},{3,0},{4,5},{5,6},{6,7},{7,4},{8,9},{9,10},{10,1... | collective-permute-start | bytes 983048 | tf_op jit(solution)/shard_map/ppermute | solution.py:15
  61.6 66.5 %collective-permute-start.20 = (bf16[256,5120]{1,0:T(8,128)(2,1)S(1)}, bf16[256,5120]{1,0:T(8,128)(2,1)S(1)}, u32[]{:S(2)}, u32[]{:S(2)}) collective-permute-start(bf16[256,5120]{1,0:T(8,128)(2,1)S(1)} %convolution_convert_fusion), channel_id=1, source_target_pairs={{0,4},{4,0},{1,5},{5,1},{2,6},{6,2},{3,7},{7,3},{8,12},{12,8},{9,1... | collective-permute-start | bytes 7864328 | tf_op jit(solution)/shard_map/ppermute | solution.py:15
  63.1 30.7 %collective-permute-start.13 = (bf16[128,1280]{1,0:T(8,128)(2,1)S(1)}, bf16[128,1280]{1,0:T(8,128)(2,1)S(1)}, u32[]{:S(2)}, u32[]{:S(2)}) collective-permute-start(bf16[128,1280]{1,0:T(8,128)(2,1)S(1)} %collective-permute-done.12), channel_id=1, source_target_pairs={{0,8},{8,0},{1,9},{9,1},{2,10},{10,2},{3,11},{11,3},{4,12},{12,4},... | collective-permute-start | bytes 983048 | tf_op jit(solution)/shard_map/ppermute | solution.py:15
  70.2 25.3 %collective-permute-start.17 = (bf16[128,1280]{1,0:T(8,128)(2,1)S(1)}, bf16[128,1280]{1,0:T(8,128)(2,1)S(1)}, u32[]{:S(2)}, u32[]{:S(2)}) collective-permute-start(bf16[128,1280]{1,0:T(8,128)(2,1)S(1)} %collective-permute-done.16), channel_id=1, source_target_pairs={{0,8},{8,0},{1,9},{9,1},{2,10},{10,2},{3,11},{11,3},{4,12},{12,4},... | collective-permute-start | bytes 983048 | tf_op jit(solution)/shard_map/ppermute | solution.py:15
  85.4 46.2 %collective-permute-start.7 = (bf16[2,2,4,64,1280]{4,3,0,1,2:T(8,128)(2,1)S(1)}, bf16[2,2,4,64,1280]{4,3,0,1,2:T(8,128)(2,1)S(1)}, u32[]{:S(2)}, u32[]{:S(2)}) collective-permute-start(bf16[2,2,4,64,1280]{4,3,0,1,2:T(8,128)(2,1)S(1)} %get-tuple-element.8), channel_id=1, source_target_pairs={{0,4},{4,0},{1,5},{5,1},{2,6},{6,2},{3,7},{7,3},{8,12},{12,8},{9,1... | collective-permute-start | bytes 7864328 | tf_op jit(solution)/shard_map/ppermute | solution.py:15
  93.7 32.6 %collective-permute-start.11 = (bf16[2,2,128,1280]{3,2,1,0:T(8,128)(2,1)S(1)}, bf16[2,2,128,1280]{3,2,1,0:T(8,128)(2,1)S(1)}, u32[]{:S(2)}, u32[]{:S(2)}) collective-permute-start(bf16[2,2,128,1280]{3,2,1,0:T(8,128)(2,1)S(1)} %get-tuple-element.14), channel_id=1, source_target_pairs={{0,4},{4,0},{1,5},{5,1},{2,6},{6,2},{3,7},{7,3},{8,12},{12,8},{9,1... | collective-permute-start | bytes 3932168 | tf_op jit(solution)/shard_map/ppermute | solution.py:15
  93.9 17.6 %collective-permute-start.14 = (bf16[2,128,1280]{2,1,0:T(8,128)(2,1)S(1)}, bf16[2,128,1280]{2,1,0:T(8,128)(2,1)S(1)}, u32[]{:S(2)}, u32[]{:S(2)}) collective-permute-start(bf16[2,128,1280]{2,1,0:T(8,128)(2,1)S(1)} %get-tuple-element.22), channel_id=1, source_target_pairs={{0,16},{16,0},{1,17},{17,1},{2,18},{18,2},{3,19},{19,3},{4,20},{20... | collective-permute-start | bytes 1966088 | tf_op jit(solution)/shard_map/ppermute | solution.py:15
  95.6 29.6 %collective-permute-start.18 = (bf16[2,128,1280]{2,1,0:T(8,128)(2,1)S(1)}, bf16[2,128,1280]{2,1,0:T(8,128)(2,1)S(1)}, u32[]{:S(2)}, u32[]{:S(2)}) collective-permute-start(bf16[2,128,1280]{2,1,0:T(8,128)(2,1)S(1)} %get-tuple-element.20), channel_id=1, source_target_pairs={{0,16},{16,0},{1,17},{17,1},{2,18},{18,2},{3,19},{19,3},{4,20},{20... | collective-permute-start | bytes 1966088 | tf_op jit(solution)/shard_map/ppermute | solution.py:15
  112.8 27.5 %collective-permute-start.15 = (bf16[2,2,128,1280]{3,2,1,0:T(8,128)(2,1)}, bf16[2,2,128,1280]{3,2,1,0:T(8,128)(2,1)}, u32[]{:S(2)}, u32[]{:S(2)}) collective-permute-start(bf16[2,2,128,1280]{3,2,1,0:T(8,128)(2,1)} %get-tuple-element.12), channel_id=1, source_target_pairs={{0,4},{4,0},{1,5},{5,1},{2,6},{6,2},{3,7},{7,3},{8,12},{12,8},{9,1... | collective-permute-start | bytes 3932168 | tf_op jit(solution)/shard_map/ppermute | solution.py:15
  126.4 17.0 %collective-permute-start.19 = (bf16[2,2,128,1280]{3,2,1,0:T(8,128)(2,1)}, bf16[2,2,128,1280]{3,2,1,0:T(8,128)(2,1)}, u32[]{:S(2)}, u32[]{:S(2)}) collective-permute-start(bf16[2,2,128,1280]{3,2,1,0:T(8,128)(2,1)} %get-tuple-element.10), channel_id=1, source_target_pairs={{0,4},{4,0},{1,5},{5,1},{2,6},{6,2},{3,7},{7,3},{8,12},{12,8},{9,1... | collective-permute-start | bytes 3932168 | tf_op jit(solution)/shard_map/ppermute | solution.py:15
  131.0 31.9 %collective-permute-start.21 = (bf16[128,5120]{1,0:T(8,128)(2,1)}, bf16[128,5120]{1,0:T(8,128)(2,1)}, u32[]{:S(2)}, u32[]{:S(2)}) collective-permute-start(bf16[128,5120]{1,0:T(8,128)(2,1)} %slice.94), channel_id=1, source_target_pairs={{0,8},{8,0},{1,9},{9,1},{2,10},{10,2},{3,11},{11,3},{4,12},{12,4},... | collective-permute-start | bytes 3932168 | tf_op jit(solution)/shard_map/ppermute | solution.py:15
  139.9 6.5 %collective-permute-start.22 = (bf16[256,1024]{1,0:T(8,128)(2,1)S(1)}, bf16[256,1024]{1,0:T(8,128)(2,1)S(1)}, u32[]{:S(2)}, u32[]{:S(2)}) collective-permute-start(bf16[256,1024]{1,0:T(8,128)(2,1)S(1)} %convolution_convert_fusion.1), channel_id=1, source_target_pairs={{0,4},{4,0},{1,5},{5,1},{2,6},{6,2},{3,7},{7,3},{8,12},{12,8},{9,1... | collective-permute-start | bytes 1572872 | tf_op jit(solution)/shard_map/ppermute | solution.py:15
  146.9 21.1 %collective-permute-start.23 = (bf16[128,1024]{1,0:T(8,128)(2,1)S(1)}, bf16[128,1024]{1,0:T(8,128)(2,1)S(1)}, u32[]{:S(2)}, u32[]{:S(2)}) collective-permute-start(bf16[128,1024]{1,0:T(8,128)(2,1)S(1)} %slice.95), channel_id=1, source_target_pairs={{0,8},{8,0},{1,9},{9,1},{2,10},{10,2},{3,11},{11,3},{4,12},{12,4},... | collective-permute-start | bytes 786440 | tf_op jit(solution)/shard_map/ppermute | solution.py:15
  168.8 13.6 %all-to-all-start.1 = ((bf16[4,32,1024]{2,1,0:T(8,128)(2,1)}), bf16[4,32,1024]{2,1,0:T(8,128)(2,1)S(1)}, u32[]{:S(2)}, u32[]{:S(2)}) async-start(bf16[4,32,1024]{2,1,0:T(8,128)(2,1)} %bitcast.61), calls=%async_computation.1 | async-start | bytes 524288 | tf_op jit(solution)/shard_map/all_to_all | solution.py:99
  183.2 12.1 %all-to-all-start.2 = ((bf16[4,32,1024]{2,1,0:T(8,128)(2,1)}), bf16[4,32,1024]{2,1,0:T(8,128)(2,1)S(1)}, u32[]{:S(2)}, u32[]{:S(2)}) async-start(bf16[4,32,1024]{2,1,0:T(8,128)(2,1)} %broadcast_in_dim.41), calls=%async_computation.2 | async-start | bytes 524288 | tf_op jit(solution)/shard_map/all_to_all | solution.py:102
  195.3 33.4 %all-to-all-start = ((bf16[4,128,1280]{2,1,0:T(8,128)(2,1)}), bf16[4,128,1280]{2,1,0:T(8,128)(2,1)}, u32[]{:S(2)}, u32[]{:S(2)}) async-start(bf16[4,128,1280]{2,1,0:T(8,128)(2,1)} %bitcast.159), calls=%async_computation | async-start | bytes 2621440 | tf_op jit(solution)/shard_map/all_to_all | solution.py:77
  210.5 20.7 %copy-start.1 = (bf16[1280,1024]{1,0:T(8,128)(2,1)S(1)}, bf16[1280,1024]{1,0:T(8,128)(2,1)}, u32[]{:S(2)}) copy-start(bf16[1280,1024]{1,0:T(8,128)(2,1)} %param.9) | copy-start | bytes 7864324
  (17 other events, 74.6 us)

commit v2 on v1

v2 whole, which is shorter than its diff:
```python
import functools
import math

import jax
import jax.numpy as jnp
from jax import lax
from jax.experimental import pallas as pl
from jax.experimental.pallas import tpu as pltpu
from jax.sharding import Mesh
from jax.sharding import PartitionSpec as P

adapter_scale = 2.0
cores = 2
bf16, f32 = jnp.bfloat16, jnp.float32
vmem_bytes = 40 * 1024 * 1024
nt = (((1,), (1,)), ((), ()))


def shift(value, axis, by):
    size = lax.axis_size(axis)
    return lax.ppermute(value, axis, [(i, (i + by) % size) for i in range(size)])


def gather_steps(value, axis):
    blocks = [value]
    for _ in range(lax.axis_size(axis) - 1):
        blocks.append(shift(blocks[-1], axis, 1))
    return blocks


def column_block(cols):
    for size in (640, 512, 384, 256, 128):
        if cols % size == 0:
            return size
    return cols


def column_spec(rows, cols, place):
    bc = column_block(cols)
    per = cols // bc
    if cols % 128 == 0:
        def index(*at):
            owner, block = place(*at)
            return 0, owner * per + block

        return pl.BlockSpec((rows, bc), index)

    def index(*at):
        owner, block = place(*at)
        return owner, 0, block

    return pl.BlockSpec((None, rows, bc), index)


def by_owner(value, cols):
    if cols % 128 == 0:
        return value
    return value.reshape(value.shape[0], -1, cols).swapaxes(0, 1)


def call(kernel, name, grid, in_specs, out_specs, out_shape, scratch, scalars, args, flops, aliases=None):
    moved = sum(math.prod(a.shape) * a.dtype.itemsize for a in args)
    return pl.pallas_call(
        kernel,
        grid_spec=pltpu.PrefetchScalarGridSpec(
            num_scalar_prefetch=len(scalars), grid=grid, in_specs=in_specs, out_specs=out_specs, scratch_shapes=scratch
        ),
        out_shape=out_shape,
        compiler_params=pltpu.CompilerParams(vmem_limit_bytes=vmem_bytes),
        cost_estimate=pl.CostEstimate(flops=flops, bytes_accessed=moved, transcendentals=0),
        input_output_aliases=aliases or {},
        name=name,
    )(*scalars, *args)


def whole(array):
    zeros = (0,) * array.ndim
    return pl.BlockSpec(array.shape, lambda *_: zeros)


def columns_policy(first, count, group, rank):
    parts = []
    for g in range(count):
        parts.append(first[g] + lax.broadcasted_iota(jnp.int32, (1, group), 1) // rank)
    return jnp.concatenate(parts, axis=1)


def low_rank_kernel(count, group, rank, first, policy, live, cot_ref, *refs):
    up_refs, (masked_ref, low_ref, low_t_ref) = refs[:count], refs[count:]
    tile = pl.program_id(0)
    rows, kv = cot_ref.shape
    keep = lax.broadcasted_iota(jnp.int32, (rows, kv), 0) < live[tile]
    masked = jnp.where(keep, cot_ref[...].astype(f32), 0.0).astype(bf16)
    masked_ref[...] = masked
    up = jnp.concatenate([r[...] for r in up_refs], axis=0)
    low = adapter_scale * lax.dot_general(masked, up, nt, preferred_element_type=f32)
    mine = columns_policy(first, count, group, rank) == policy[tile]
    low = jnp.where(mine, low, 0.0)
    low_ref[...] = low.astype(bf16)
    low_t_ref[...] = low.T.astype(bf16)


def low_rank_call(first, policy, live, cotangent, ups, rank):
    rows, kv = cotangent.shape
    tiles = policy.shape[0]
    group = ups[0].shape[0]
    total = group * len(ups)
    tile_rows = rows // tiles
    return call(
        functools.partial(low_rank_kernel, len(ups), group, rank),
        "low_rank",
        (tiles,),
        [pl.BlockSpec((tile_rows, kv), lambda i, *_: (i, 0))] + [whole(u) for u in ups],
        [
            pl.BlockSpec((tile_rows, kv), lambda i, *_: (i, 0)),
            pl.BlockSpec((tile_rows, total), lambda i, *_: (i, 0)),
            pl.BlockSpec((total, tile_rows), lambda i, *_: (0, i)),
        ],
        [
            jax.ShapeDtypeStruct((rows, kv), bf16),
            jax.ShapeDtypeStruct((rows, total), bf16),
            jax.ShapeDtypeStruct((total, rows), bf16),
        ],
        [],
        (first, policy, live),
        [cotangent, *ups],
        2 * rows * kv * total,
    )


def partial_kernel(adds, blocks, low_t_ref, tok_ref, *refs):
    value = jnp.dot(low_t_ref[...], tok_ref[...], preferred_element_type=f32)
    if adds:
        value = value + refs[0][0].astype(f32)
    refs[-1][0] = value.astype(refs[-1].dtype)


def partial_call(low_t, tokens, blocks, cols, added, dtype):
    rows = low_t.shape[0]
    count = blocks.shape[0]
    bc = column_block(cols)
    per = cols // bc
    in_specs = [whole(low_t), column_spec(low_t.shape[1], cols, lambda i, j, b: (b[i], j))]
    args = [low_t, tokens]
    if added is not None:
        in_specs.append(pl.BlockSpec((1, rows, bc), lambda i, j, b: (i, 0, j)))
        args.append(added)
    return call(
        functools.partial(partial_kernel, added is not None),
        "down_partial",
        (count, per),
        in_specs,
        pl.BlockSpec((1, rows, bc), lambda i, j, b: (i, 0, j)),
        jax.ShapeDtypeStruct((count, rows, cols), dtype),
        [],
        (blocks,),
        args,
        2 * rows * low_t.shape[1] * cols * count,
    )


def place_down(store, refs, half, back, scalars, at):
    y_size = len(back)
    for n, ref in enumerate(refs):
        g, s = divmod(n, y_size)
        row = pl.multiple_of(scalars[at + s] * half, half) + g * y_size * half
        store[pl.ds(row, half), :] = ref[0]


def projected_first_kernel(count, blocks, tok_ref, *refs):
    out_ref = refs[-1]
    down = jnp.concatenate([r[...] for r in refs[:count]], axis=0)

    @pl.when(pl.program_id(0) == 0)
    def _():
        out_ref[...] = jnp.zeros_like(out_ref)

    out_ref[...] += lax.dot_general(tok_ref[...], down, nt, preferred_element_type=f32)


def projected_first(tokens, downs, blocks, rows):
    group, cols = downs[0].shape
    total = group * len(downs)
    bc = column_block(cols)
    per = cols // bc
    return call(
        functools.partial(projected_first_kernel, len(downs)),
        "projected_own",
        (per,),
        [column_spec(rows, cols, lambda j, b: (b[0], j))]
        + [pl.BlockSpec((group, bc), lambda j, b: (0, j)) for _ in downs],
        pl.BlockSpec((rows, total), lambda j, b: (0, 0)),
        jax.ShapeDtypeStruct((rows, total), f32),
        [],
        (blocks,),
        [tokens, *downs],
        2 * rows * cols * total,
    )


def projected_kernel(pieces, y_size, half, tiles, rank, split, scalars, first, policy, tok_ref, base_ref, masked_ref, *refs):
    piece_refs, (send_ref, keep_ref, store, total) = refs[:pieces], refs[pieces:]
    step = pl.program_id(0) * pl.num_programs(1) + pl.program_id(1)

    @pl.when(step == 0)
    def _():
        total[...] = base_ref[...]

    place_down(store, piece_refs, half, range(y_size), scalars, 0)
    total[...] += lax.dot_general(tok_ref[...], store[...], nt, preferred_element_type=f32)

    @pl.when(step == pl.num_programs(0) * pl.num_programs(1) - 1)
    def _():
        count = pieces // y_size
        columns = columns_policy(first, count, half * y_size, rank)
        tile_rows = total.shape[0] // tiles
        chosen = []
        for i in range(tiles):
            part = total[i * tile_rows : (i + 1) * tile_rows, :]
            chosen.append(jnp.where(columns == policy[i], part, 0.0).T)
        projected = jnp.concatenate(chosen, axis=1).astype(bf16)
        value = jnp.dot(projected, masked_ref[...], preferred_element_type=f32)
        keep_ref[...] = value[:split]
        send_ref[...] = value[split:]


def projected_call(scalars, first, policy, blocks_at, tokens, base, masked, pieces, y_size, half, rank, split):
    rows, kv = masked.shape
    steps, _, cols = pieces[0].shape
    total = half * len(pieces)
    bc = column_block(cols)
    per = cols // bc
    return call(
        functools.partial(projected_kernel, len(pieces), y_size, half, policy.shape[0], rank, split),
        "projected",
        (steps, per),
        [
            column_spec(rows, cols, lambda i, j, s, *_: (s[blocks_at + i], j)),
            whole(base),
            whole(masked),
        ]
        + [pl.BlockSpec((1, half, bc), lambda i, j, *_: (i, 0, j)) for _ in pieces],
        [
            pl.BlockSpec((total - split, kv), lambda *_: (0, 0)),
            pl.BlockSpec((split, kv), lambda *_: (0, 0)),
        ],
        [jax.ShapeDtypeStruct((total - split, kv), f32), jax.ShapeDtypeStruct((split, kv), f32)],
        [pltpu.VMEM((total, bc), bf16), pltpu.VMEM((rows, total), f32)],
        (scalars, first, policy),
        [tokens, base, masked, *pieces],
        2 * rows * cols * steps * total + 2 * rows * kv * total,
    )


def input_kernel(views, pieces, y_size, half, has_out, scalars, low_ref, *refs):
    masked_refs, refs = refs[:views], refs[views:]
    weight_refs, refs = refs[:views], refs[views:]
    down_refs, refs = refs[:pieces], refs[pieces:]
    if has_out:
        refs = refs[1:]
    out_ref = refs[0]
    masked = jnp.concatenate([r[...] for r in masked_refs], axis=1)
    weight = jnp.concatenate([r[...] for r in weight_refs], axis=1)
    value = lax.dot_general(masked, weight, nt, preferred_element_type=f32)
    if y_size:
        place_down(refs[1], down_refs, half, range(y_size), scalars, 1 + views)
        down = refs[1][...]
    else:
        down = jnp.concatenate([r[...] for r in down_refs], axis=0)
    value = value + jnp.dot(low_ref[...], down, preferred_element_type=f32)
    out_ref[...] = value.astype(bf16)


def input_call(scalars, low, masked, weights, downs, step, y_size, out, width):
    rows, kv = masked.shape
    cols = weights[0].shape[0]
    depth = weights[0].shape[1]
    half = downs[0].shape[-2]
    total = low.shape[1]
    bc = column_block(cols)
    per = cols // bc
    if y_size:
        down_specs = [pl.BlockSpec((1, half, bc), lambda j, s: (step, 0, j)) for _ in downs]
    else:
        down_specs = [pl.BlockSpec((half, bc), lambda j, s: (0, j)) for _ in downs]
    in_specs = [whole(low)]
    for v in range(len(weights)):
        in_specs.append(pl.BlockSpec((rows, depth), functools.partial(lambda v, j, s: (0, s[1 + v]), v)))
    in_specs += [pl.BlockSpec((bc, depth), lambda j, s: (j, 0)) for _ in weights] + down_specs
    args = [low] + [masked] * len(weights) + list(weights) + list(downs)
    aliases = {}
    if out is not None:
        in_specs.append(pl.BlockSpec(memory_space=pl.ANY))
        aliases = {1 + len(args): 0}
        args.append(out)
    return call(
        functools.partial(input_kernel, len(weights), len(downs), y_size, half, out is not None),
        "input_cotangent",
        (per,),
        in_specs,
        column_spec(rows, cols, lambda j, s: (s[0], j)),
        jax.ShapeDtypeStruct((rows, width) if cols % 128 == 0 else (width // cols, rows, cols), bf16),
        [pltpu.VMEM((total, bc), bf16)] if y_size else [],
        (scalars,),
        args,
        2 * rows * cols * (kv + total),
        aliases,
    )


def body(tokens, value_cotangent, value_weight, adapter_down, adapter_up, tile_token_policy, tile_live_length):
    y_size, x_size, c_size, z_size = (lax.axis_size(a) for a in ("league", "x", "core", "fsdp"))
    y, x, c, z = (lax.axis_index(a) for a in ("league", "x", "core", "fsdp"))
    rows, width = tokens.shape
    kv = value_cotangent.shape[1]
    own_policies, rank, cols = adapter_down.shape
    group = own_policies * rank
    half = group // y_size
    depth = kv // (y_size * c_size)

    def ints(*values):
        return jnp.stack([jnp.asarray(v, jnp.int32) for v in values])

    up_x = gather_steps(adapter_up.reshape(group, kv), "x")
    ups = [piece for s in zip(*[gather_steps(u, "core") for u in up_x]) for piece in s]
    groups = [(dc, dx) for dc in range(c_size) for dx in range(x_size)]
    first = ints(*[(((x - dx) % x_size) * c_size + (c - dc) % c_size) * own_policies for dc, dx in groups])

    own_down = adapter_down.reshape(group, cols)
    down_x = gather_steps(own_down, "x")
    own_downs = [piece for s in zip(*[gather_steps(u, "core") for u in down_x]) for piece in s]
    down_half = lax.dynamic_slice_in_dim(own_down, y * half, half, 0)
    down_z = jnp.stack([shift(down_half, "fsdp", s) for s in range(1, z_size)])
    down_pieces = {}
    for dx, piece in enumerate(gather_steps(down_z, "x")):
        for dy, got in enumerate(gather_steps(piece, "league")):
            for dc, last in enumerate(gather_steps(got, "core")):
                down_pieces[dc, dx, dy] = last
    downs = [down_pieces[dc, dx, dy] for dc, dx in groups for dy in range(y_size)]
    league_back = [(y - s) % y_size for s in range(y_size)]

    masked, low, low_t = low_rank_call(first, tile_token_policy, tile_live_length, value_cotangent, ups, rank)

    tokens = by_owner(tokens, cols)

    split = x_size * group
    normalizer = 1.0 / math.sqrt(rows * x_size * c_size * z_size)
    order = [(z + s) % z_size for s in range(z_size)]
    chunks = [list(range(z_size // 2, z_size)), list(range(z_size // 2))]
    got_a = []
    for chunk in chunks:
        places = ints(*[order[s] for s in chunk])
        sent = [
            shift(partial_call(low_t[s * split : (s + 1) * split], tokens, places, cols, None, bf16), "core", -s)
            for s in range(1, c_size)
        ]
        added = sent[0] if len(sent) == 1 else sum(v.astype(f32) for v in sent)
        for_x = [
            shift(partial_call(low_t[s * group : (s + 1) * group], tokens, places, cols, added[:, s * group : (s + 1) * group], bf16), "x", -s)
            for s in range(1, x_size)
        ]
        kept = partial_call(low_t[:group], tokens, places, cols, added[:, :group], f32)
        for value in for_x:
            kept = kept + value.astype(f32)
        for n, s in enumerate(chunk):
            got_a.append(shift(kept[n].astype(bf16), "fsdp", s).astype(f32) if s else kept[n])
    grad_a = sum(got_a[1:], got_a[0]) * normalizer

    blocks = ints(*[(z - s) % z_size for s in range(z_size)])
    base = projected_first(tokens, own_downs, blocks, rows)
    scalars = jnp.concatenate([ints(*league_back), blocks[1:]])
    sent_b, kept_b = projected_call(
        scalars, first, tile_token_policy, y_size, tokens, base, masked, downs, y_size, half, rank, split
    )
    for s in range(1, c_size):
        kept_b = kept_b + shift(sent_b[(s - 1) * split : s * split], "core", -s)
    kept_b = kept_b.reshape(x_size, group, kv)
    own_b = kept_b[0]
    for s in range(1, x_size):
        own_b = own_b + shift(kept_b[s].astype(bf16), "x", -s).astype(f32)
    own_b = own_b.reshape(z_size, -1, kv).astype(bf16)
    parts_b = lax.all_to_all(own_b, "fsdp", split_axis=0, concat_axis=0, tiled=True)
    share_b = (jnp.sum(parts_b.astype(f32), axis=0) * (adapter_scale * normalizer)).astype(bf16)
    spread = jnp.broadcast_to(share_b[None], (z_size,) + share_b.shape)
    grad_b = lax.all_to_all(spread, "fsdp", split_axis=0, concat_axis=0, tiled=True).astype(f32)

    out = input_call(ints(z, 0), low, masked, [value_weight], own_downs, 0, 0, None, width)
    held = lax.dynamic_slice_in_dim(value_weight, (y * c_size + c) * depth, depth, 1)
    for s in range(1, z_size):
        held = shift(held, "fsdp", 1)
        weights, places = [], []
        for dy, piece in enumerate(gather_steps(held, "league")):
            for dc, got in enumerate(gather_steps(piece, "core")):
                weights.append(got)
                places.append(league_back[dy] * c_size + (c - dc) % c_size)
        out = input_call(
            ints((z - s) % z_size, *places, *league_back), low, masked, weights, downs, s - 1, y_size, out, width
        )
    if cols % 128:
        out = out.swapaxes(0, 1).reshape(rows, width)
    return out, grad_a.reshape(own_policies, rank, cols), grad_b.reshape(own_policies, rank, kv)


def solution(mesh):
    league, dp, fsdp = mesh.devices.shape
    fine = Mesh(mesh.devices.reshape(league, dp // cores, cores, fsdp), ("league", "x", "core", "fsdp"))
    every = ("league", "x", "core", "fsdp")
    return jax.shard_map(
        body,
        mesh=fine,
        in_specs=(
            P(every, None),
            P(every, None),
            P("fsdp", None),
            P(("x", "core"), None, "fsdp"),
            P(("x", "core"), None, None),
            P(every),
            P(every),
        ),
        out_specs=(
            P(every, None),
            P(("league", "x", "core"), None, "fsdp"),
            P(("league", "x", "core"), None, None),
        ),
        check_vma=False,
    )
```

time: 232 us -> 176 us (0.76)
  waiting for transfers between devices: 106 us -> 36.9 us
  Pallas kernels: 0 us -> 51.9 us
  matrix products: 29.6 us -> 0 us
  other arithmetic: 26.6 us -> 8.61 us
  starting transfers between devices: 31.8 us -> 46.2 us
  local copies, waits for them, and re-layouts: 36.1 us -> 29.7 us
    ppermute x24 -> x37, waiting for transfers between devices: 83.9 us -> 30.8 us  [shift(): lax.ppermute(value, axis, [(i, (i + by) % size) for i in range(size)])]
    pallas_call x0 -> x13, Pallas kernels: none -> 51.9 us  [call(): pl.pallas_call(kernel, grid_spec=pltpu.PrefetchScalarGridSpec(num_scalar_...]
    dot_general x17 -> x0, matrix products: 29.6 us -> none  [the longest x3 12.5 us: body(): block = jnp.dot(masked_k, weight[s - 1], preferred_element_type=f32)]
    another operation x18 -> x7, other arithmetic: 19.4 us -> 2.4 us  [the longest x5 1.38 us: ints(): return jnp.stack([jnp.asarray(v, jnp.int32) for v in values])]
    all_to_all x2 -> x1, waiting for transfers between devices: 18.5 us -> 6.18 us  [body(): lax.all_to_all(own_b, 'fsdp', split_axis=0, concat_axis=0, tiled=True)]
    ppermute x24 -> x37, starting transfers between devices: 18.9 us -> 31 us  [shift(): lax.ppermute(value, axis, [(i, (i + by) % size) for i in range(size)])]
    unnamed x53 -> x58, local copies, waits for them, and re-layouts: 25 us -> 17.6 us
    all_to_all x1, starting transfers between devices: 3.87 us -> 11 us  [body(): lax.all_to_all(spread, 'fsdp', split_axis=0, concat_axis=0, tiled=True)]
  transfers between devices with their start and end apart: 27 -> 39, of which waited for: 15 -> 8; matrix products, arithmetic and copies ran while one was open for 35% -> 11% of each run, Pallas kernels for 0% -> 30%
where the time goes in v2:
time: 176 us; the launch traced here: 174 us
  Pallas kernels  51.9 us (29%)
  starting transfers between devices  46.2 us (26%)
  waiting for transfers between devices  36.9 us (21%)
  local copies, waits for them, and re-layouts  29.7 us (17%)
  other arithmetic  8.61 us (5%)
    pallas_call x13, Pallas kernels, call(): pl.pallas_call(kernel, grid_spec=pltpu.PrefetchScalarGridSpec(num_scalar_...  51.9 us
    ppermute x37, starting transfers between devices, shift(): lax.ppermute(value, axis, [(i, (i + by) % size) for i in range(size)])  31 us
    ppermute x37, waiting for transfers between devices, shift(): lax.ppermute(value, axis, [(i, (i + by) % size) for i in range(size)])  30.8 us
    unnamed x58, local copies, waits for them, and re-layouts  17.6 us
    all_to_all x1, starting transfers between devices, body(): lax.all_to_all(spread, 'fsdp', split_axis=0, concat_axis=0, tiled=True)  11 us
    all_to_all x1, waiting for transfers between devices, body(): lax.all_to_all(own_b, 'fsdp', split_axis=0, concat_axis=0, tiled=True)  6.18 us
    all_to_all x1, starting transfers between devices, body(): lax.all_to_all(own_b, 'fsdp', split_axis=0, concat_axis=0, tiled=True)  4.14 us
  transfers between devices with their start and end apart: 39, of which 8 were waited for; matrix products, arithmetic and copies ran while one was open for 11% of the time, Pallas kernels for 30%

profile of v2, /device:TPU:0, one launch (start us, length us, event | category | flops | bytes accessed | tf_op | source)
XLA Modules:
  0.0 174.3 jit_solution(14900342675164279423)
XLA Ops:
  0.6 3.0 %collective-permute-start = (bf16[128,1024]{1,0:T(8,128)(2,1)}, bf16[128,1024]{1,0:T(8,128)(2,1)S(1)}, u32[]{:S(2)}, u32[]{:S(2)}) collective-permute-start(bf16[128,1024]{1,0:T(8,128)(2,1)} %bitcast.50), channel_id=1, source_target_pairs={{0,8},{8,0},{1,9},{9,1},{2,10},{10,2},{3,11},{11,3},{4,12},{12,4},... | collective-permute-start | bytes 786440 | tf_op jit(solution)/shard_map/ppermute | solution.py:21
  6.2 2.6 %collective-permute-start.10 = (bf16[64,1280]{1,0:T(8,128)(2,1)S(1)}, bf16[64,1280]{1,0:T(8,128)(2,1)S(1)}, u32[]{:S(2)}, u32[]{:S(2)}) collective-permute-start(bf16[64,1280]{1,0:T(8,128)(2,1)S(1)} %constant_dynamic-slice_fusion), channel_id=1, source_target_pairs={{0,2},{1,3},{2,0},{3,1},{4,6},{5,7},{6,4},{7,5},{8,10},{9,11},{10,... | collective-permute-start | bytes 491528 | tf_op jit(solution)/shard_map/ppermute | solution.py:21
  10.7 3.0 %collective-permute-done.9 = bf16[64,1280]{1,0:T(8,128)(2,1)S(1)} collective-permute-done((bf16[64,1280]{1,0:T(8,128)(2,1)S(1)}, bf16[64,1280]{1,0:T(8,128)(2,1)S(1)}, u32[]{:S(2)}, u32[]{:S(2)}) %collective-permute-start.9) | collective-permute-done | bytes 163872 | tf_op jit(solution)/shard_map/ppermute | solution.py:21
  13.7 5.6 %collective-permute-done.10 = bf16[64,1280]{1,0:T(8,128)(2,1)S(1)} collective-permute-done((bf16[64,1280]{1,0:T(8,128)(2,1)S(1)}, bf16[64,1280]{1,0:T(8,128)(2,1)S(1)}, u32[]{:S(2)}, u32[]{:S(2)}) %collective-permute-start.10) | collective-permute-done | bytes 163872 | tf_op jit(solution)/shard_map/ppermute | solution.py:21
  23.8 2.0 %constant_dynamic-slice_fusion.1 = bf16[1280,256]{1,0:T(8,128)(2,1)} fusion(bf16[1280,1024]{1,0:T(8,128)(2,1)} %refs_1_.1, s32[]{:T(128)S(6)} %select_n.108), kind=kLoop, calls=%fused_computation.23 | loop fusion | bytes 1310724 | tf_op jit(solution)/shard_map/dynamic_slice | solution.py:388
  26.4 2.9 %collective-permute-start.3 = (bf16[1280,256]{1,0:T(8,128)(2,1)}, bf16[1280,256]{1,0:T(8,128)(2,1)}, u32[]{:S(2)}, u32[]{:S(2)}) collective-permute-start(bf16[1280,256]{1,0:T(8,128)(2,1)} %constant_dynamic-slice_fusion.1), channel_id=1, source_target_pairs={{0,1},{1,2},{2,3},{3,0},{4,5},{5,6},{6,7},{7,4},{8,9},{9,10},{10,1... | collective-permute-start | bytes 1966088 | tf_op jit(solution)/shard_map/ppermute | solution.py:21
  34.5 2.9 %low_rank.1 = (bf16[512,1024]{1,0:T(8,128)(2,1)S(1)}, bf16[512,512]{1,0:T(8,128)(2,1)S(1)}, bf16[512,512]{1,0:T(8,128)(2,1)S(1)}) custom-call(s32[4]{0:T(128)S(1)} %pad_add_fusion.first, s32[4]{0:T(128)S(1)} %copy-done.20, s32[4]{0:T(128)S(1)} %copy-done.24, bf16[512,1024]{1,0:T(8,128)(2,1)S(1)} %copy-done.9, bf16[128,1024]{1,0:T(8,128)(2,1)S(1)} %bitcast.52, ...), custom_call_target="tpu_custom_call" | custom-call | flops 536870912 | bytes 2097152 | tf_op jit(solution)/shard_map/low_rank/pallas_call | solution.py:63
  38.2 2.5 %copy-done = bf16[512,5120]{1,0:T(8,128)(2,1)S(1)} copy-done((bf16[512,5120]{1,0:T(8,128)(2,1)S(1)}, bf16[512,5120]{1,0:T(8,128)(2,1)}, u32[]{:S(2)}) %copy-start) | copy-done | bytes 5242904
  40.7 3.5 %down_partial.6 = bf16[2,256,1280]{2,1,0:T(8,128)(2,1)} custom-call(s32[2]{0:T(128)S(1)} %pad_add_fusion.2.blocks, bf16[256,512]{1,0:T(8,128)(2,1)S(1)} %slice.51.low_t_ref, bf16[512,5120]{1,0:T(8,128)(2,1)S(1)} %copy-done), custom_call_target="tpu_custom_call" | custom-call | flops 671088640 | bytes 5505024 | tf_op jit(solution)/shard_map/down_partial/pallas_call | solution.py:63
  46.8 2.5 %copy-done.1 = bf16[512,5120]{1,0:T(8,128)(2,1)S(1)} copy-done((bf16[512,5120]{1,0:T(8,128)(2,1)S(1)}, bf16[512,5120]{1,0:T(8,128)(2,1)}, u32[]{:S(2)}) %copy-start.1) | copy-done | bytes 5242904
  50.3 3.5 %down_partial.9 = bf16[2,256,1280]{2,1,0:T(8,128)(2,1)} custom-call(s32[2]{0:T(128)S(1)} %pad_add_fusion.3.blocks, bf16[256,512]{1,0:T(8,128)(2,1)S(1)} %copy-done.5, bf16[512,5120]{1,0:T(8,128)(2,1)S(1)} %copy-done.1), custom_call_target="tpu_custom_call" | custom-call | flops 671088640 | bytes 5505024 | tf_op jit(solution)/shard_map/down_partial/pallas_call | solution.py:63
  58.3 2.5 %copy-done.2 = bf16[512,5120]{1,0:T(8,128)(2,1)S(1)} copy-done((bf16[512,5120]{1,0:T(8,128)(2,1)S(1)}, bf16[512,5120]{1,0:T(8,128)(2,1)}, u32[]{:S(2)}) %copy-start.2) | copy-done | bytes 5242904
  63.3 3.2 %projected_own.1.base_ref = f32[512,512]{1,0:T(8,128)S(1)} custom-call(s32[4]{0:T(128)S(1)} %copy-done.22, bf16[512,5120]{1,0:T(8,128)(2,1)S(1)} %copy-done.2, bf16[128,1280]{1,0:T(8,128)(2,1)S(1)} %bitcast.48, bf16[128,1280]{1,0:T(8,128)(2,1)} %collective-permute-done.25.refs_3_.refs_1_, bf16[128,1280]{1,0:T(8,128)(2,1)S(1)} %copy-done.8, ...), custom_call_target="tpu_custom_call" | custom-call | flops 671088640 | bytes 6553600 | tf_op jit(solution)/shard_map/projected_own/pallas_call | solution.py:63
  66.6 5.5 %input_cotangent.4.refs_16_ = bf16[512,5120]{1,0:T(8,128)(2,1)} custom-call(s32[2]{0:T(128)S(1)} %copy-done.25, bf16[512,512]{1,0:T(8,128)(2,1)S(1)} %get-tuple-element.8.low_ref, bf16[512,1024]{1,0:T(8,128)(2,1)S(1)} %get-tuple-element.9.refs_0_.refs_1_.refs_2_.refs_3_.masked_ref, bf16[1280,1024]{1,0:T(8,128)(2,1)S(1)} %copy-done.3, ...), custom_call_target="tpu_custom_call" | custom-call | flops 2013265920 | bytes 5505024 | tf_op jit(solution)/shard_map/input_cotangent/pallas_call | solution.py:63
  73.8 7.7 %projected.1 = (f32[256,1024]{1,0:T(8,128)S(1)}, f32[256,1024]{1,0:T(8,128)S(1)}) custom-call(s32[5]{0:T(128)S(1)} %copy-done.23, s32[4]{0:T(128)S(1)} %pad_add_fusion.first, s32[4]{0:T(128)S(1)} %copy-done.21, bf16[512,5120]{1,0:T(8,128)(2,1)S(1)} %bitcast.44, f32[512,512]{1,0:T(8,128)S(1)} %projected_own.1.base_ref, ...), custom_call_target="tpu_custom_call" | custom-call | flops 2550136832 | bytes 11272192 | tf_op jit(solution)/shard_map/projected/pallas_call | solution.py:63
  81.5 2.0 %collective-permute-start.5 = (bf16[1280,256]{1,0:T(8,128)(2,1)}, bf16[1280,256]{1,0:T(8,128)(2,1)}, u32[]{:S(2)}, u32[]{:S(2)}) collective-permute-start(bf16[1280,256]{1,0:T(8,128)(2,1)} %collective-permute-done.4.refs_4_), channel_id=1, source_target_pairs={{0,1},{1,2},{2,3},{3,0},{4,5},{5,6},{6,7},{7,4},{8,9},{9,10},{10,1... | collective-permute-start | bytes 1966088 | tf_op jit(solution)/shard_map/ppermute | solution.py:21
  84.9 2.2 %down_partial.8 = bf16[2,128,1280]{2,1,0:T(8,128)(2,1)S(1)} custom-call(s32[2]{0:T(128)S(1)} %pad_add_fusion.2.blocks, bf16[128,512]{1,0:T(8,128)(2,1)S(1)} %get-tuple-element.19.low_t_ref, bf16[512,5120]{1,0:T(8,128)(2,1)S(1)} %bitcast.44, bf16[2,128,1280]{2,1,0:T(8,128)(2,1)S(1)} %get-tuple-element.13.refs_0_), custom_call_target="tpu_custom_call" | custom-call | flops 335544320 | bytes 6029312 | tf_op jit(solution)/shard_map/down_partial/pallas_call | solution.py:63
  89.4 2.1 %down_partial.11 = bf16[2,128,1280]{2,1,0:T(8,128)(2,1)S(1)} custom-call(s32[2]{0:T(128)S(1)} %pad_add_fusion.3.blocks, bf16[128,512]{1,0:T(8,128)(2,1)S(1)} %get-tuple-element.19.low_t_ref, bf16[512,5120]{1,0:T(8,128)(2,1)S(1)} %bitcast.44, bf16[2,128,1280]{2,1,0:T(8,128)(2,1)S(1)} %get-tuple-element.15.refs_0_), custom_call_target="tpu_custom_call" | custom-call | flops 335544320 | bytes 6029312 | tf_op jit(solution)/shard_map/down_partial/pallas_call | solution.py:63
  91.6 2.2 %down_partial.10 = f32[2,128,1280]{2,1,0:T(8,128)S(1)} custom-call(s32[2]{0:T(128)S(1)} %pad_add_fusion.3.blocks, bf16[128,512]{1,0:T(8,128)(2,1)S(1)} %get-tuple-element.20.low_t_ref, bf16[512,5120]{1,0:T(8,128)(2,1)S(1)} %bitcast.44, bf16[2,128,1280]{2,1,0:T(8,128)(2,1)S(1)} %get-tuple-element.16.refs_0_), custom_call_target="tpu_custom_call" | custom-call | flops 335544320 | bytes 6029312 | tf_op jit(solution)/shard_map/down_partial/pallas_call | solution.py:63
  93.7 2.2 %down_partial.7 = f32[2,128,1280]{2,1,0:T(8,128)S(1)} custom-call(s32[2]{0:T(128)S(1)} %pad_add_fusion.2.blocks, bf16[128,512]{1,0:T(8,128)(2,1)S(1)} %get-tuple-element.20.low_t_ref, bf16[512,5120]{1,0:T(8,128)(2,1)S(1)} %bitcast.44, bf16[2,128,1280]{2,1,0:T(8,128)(2,1)S(1)} %get-tuple-element.14.refs_0_), custom_call_target="tpu_custom_call" | custom-call | flops 335544320 | bytes 6029312 | tf_op jit(solution)/shard_map/down_partial/pallas_call | solution.py:63
  97.3 5.5 %input_cotangent.5.refs_16_ = bf16[512,5120]{1,0:T(8,128)(2,1)} custom-call(s32[7]{0:T(128)S(1)} %copy-done.19, bf16[512,512]{1,0:T(8,128)(2,1)S(1)} %get-tuple-element.8.low_ref, bf16[512,1024]{1,0:T(8,128)(2,1)S(1)} %get-tuple-element.9.refs_0_.refs_1_.refs_2_.refs_3_.masked_ref, ...), custom_call_target="tpu_custom_call", output_to_operand_aliasing={{}: (18, {})} | custom-call | flops 2013265920 | bytes 16515072 | tf_op jit(solution)/shard_map/input_cotangent/pallas_call | solution.py:63
  102.8 1.8 %collective-permute-done.29 = bf16[2,128,1280]{2,1,0:T(8,128)(2,1)S(1)} collective-permute-done((bf16[2,128,1280]{2,1,0:T(8,128)(2,1)S(1)}, bf16[2,128,1280]{2,1,0:T(8,128)(2,1)S(1)}, u32[]{:S(2)}, u32[]{:S(2)}) %collective-permute-start.29) | collective-permute-done | bytes 655392 | tf_op jit(solution)/shard_map/ppermute | solution.py:21
  107.0 11.3 %collective-permute-done.33 = bf16[2,128,1280]{2,1,0:T(8,128)(2,1)S(1)} collective-permute-done((bf16[2,128,1280]{2,1,0:T(8,128)(2,1)S(1)}, bf16[2,128,1280]{2,1,0:T(8,128)(2,1)S(1)}, u32[]{:S(2)}, u32[]{:S(2)}) %collective-permute-start.33) | collective-permute-done | bytes 655392 | tf_op jit(solution)/shard_map/ppermute | solution.py:21
  120.4 7.0 %collective-permute-done.36 = bf16[128,1024]{1,0:T(8,128)(2,1)S(1)} collective-permute-done((bf16[128,1024]{1,0:T(8,128)(2,1)S(1)}, bf16[128,1024]{1,0:T(8,128)(2,1)S(1)}, u32[]{:S(2)}, u32[]{:S(2)}) %collective-permute-start.36) | collective-permute-done | bytes 262176 | tf_op jit(solution)/shard_map/ppermute | solution.py:21
  129.2 4.1 %all-to-all-start = ((bf16[4,32,1024]{2,1,0:T(8,128)(2,1)}), bf16[4,32,1024]{2,1,0:T(8,128)(2,1)}, u32[]{:S(2)}, u32[]{:S(2)}) async-start(bf16[4,32,1024]{2,1,0:T(8,128)(2,1)} %bitcast.53), calls=%async_computation | async-start | bytes 524288 | tf_op jit(solution)/shard_map/all_to_all | solution.py:382
  133.3 2.0 %slice_bitcast_fusion.2 = (bf16[128,1280]{1,0:T(8,128)(2,1)}, bf16[128,1280]{1,0:T(8,128)(2,1)}) fusion(bf16[2,128,1280]{2,1,0:T(8,128)(2,1)} %add_convert_fusion), kind=kLoop, calls=%fused_computation.14 | loop fusion | bytes 1310720 | tf_op jit(solution)/shard_map/convert_element_type | solution.py:366
  135.3 2.9 %collective-permute-start.30 = (bf16[128,1280]{1,0:T(8,128)(2,1)}, bf16[128,1280]{1,0:T(8,128)(2,1)}, u32[]{:S(2)}, u32[]{:S(2)}) collective-permute-start(bf16[128,1280]{1,0:T(8,128)(2,1)} %get-tuple-element.17), channel_id=1, source_target_pairs={{0,2},{1,3},{2,0},{3,1},{4,6},{5,7},{6,4},{7,5},{8,10},{9,11},{10,... | collective-permute-start | bytes 983048 | tf_op jit(solution)/shard_map/ppermute | solution.py:21
  139.7 5.8 %input_cotangent.6.refs_16_ = bf16[512,5120]{1,0:T(8,128)(2,1)} custom-call(s32[7]{0:T(128)S(1)} %copy-done.18, bf16[512,512]{1,0:T(8,128)(2,1)S(1)} %get-tuple-element.8.low_ref, bf16[512,1024]{1,0:T(8,128)(2,1)S(1)} %get-tuple-element.9.refs_0_.refs_1_.refs_2_.refs_3_.masked_ref, ...), custom_call_target="tpu_custom_call", output_to_operand_aliasing={{}: (18, {})} | custom-call | flops 2013265920 | bytes 16515072 | tf_op jit(solution)/shard_map/input_cotangent/pallas_call | solution.py:63
  145.5 6.2 %all-to-all-done = bf16[4,32,1024]{2,1,0:T(8,128)(2,1)} async-done(((bf16[4,32,1024]{2,1,0:T(8,128)(2,1)}), bf16[4,32,1024]{2,1,0:T(8,128)(2,1)}, u32[]{:S(2)}, u32[]{:S(2)}) %all-to-all-start) | async-done | bytes 262176 | tf_op jit(solution)/shard_map/all_to_all | solution.py:382
  153.4 11.0 %all-to-all-start.1 = ((bf16[4,32,1024]{2,1,0:T(8,128)(2,1)}), bf16[4,32,1024]{2,1,0:T(8,128)(2,1)}, u32[]{:S(2)}, u32[]{:S(2)}) async-start(bf16[4,32,1024]{2,1,0:T(8,128)(2,1)} %broadcast_in_dim.2), calls=%async_computation.1 | async-start | bytes 524288 | tf_op jit(solution)/shard_map/all_to_all | solution.py:385
  164.4 2.4 %fusion.2 = f32[128,1280]{1,0:T(8,128)} fusion(f32[2,128,1280]{2,1,0:T(8,128)} %copy-done.26, bf16[128,1280]{1,0:T(8,128)(2,1)} %collective-permute-done.34, bf16[128,1280]{1,0:T(8,128)(2,1)} %collective-permute-done.31, bf16[128,1280]{1,0:T(8,128)(2,1)} %collective-permute-done.30), kind=kLoop, calls=%fused_computation.6 | loop fusion | flops 1146880 | bytes 2293760 | tf_op jit(solution)/shard_map/mul | solution.py:367
  166.8 5.8 %input_cotangent.7 = bf16[512,5120]{1,0:T(8,128)(2,1)} custom-call(s32[7]{0:T(128)S(1)} %stack.115.scalars, bf16[512,512]{1,0:T(8,128)(2,1)S(1)} %get-tuple-element.8.low_ref, bf16[512,1024]{1,0:T(8,128)(2,1)S(1)} %get-tuple-element.9.refs_0_.refs_1_.refs_2_.refs_3_.masked_ref, ...), custom_call_target="tpu_custom_call", output_to_operand_aliasing={{}: (18, {})} | custom-call | flops 2013265920 | bytes 16515072 | tf_op jit(solution)/shard_map/input_cotangent/pallas_call | solution.py:63
  (146 shorter events, 44.2 us)
Async XLA Ops:
  0.6 18.7 %collective-permute-start = (bf16[128,1024]{1,0:T(8,128)(2,1)}, bf16[128,1024]{1,0:T(8,128)(2,1)S(1)}, u32[]{:S(2)}, u32[]{:S(2)}) collective-permute-start(bf16[128,1024]{1,0:T(8,128)(2,1)} %bitcast.50), channel_id=1, source_target_pairs={{0,8},{8,0},{1,9},{9,1},{2,10},{10,2},{3,11},{11,3},{4,12},{12,4},... | collective-permute-start | bytes 786440 | tf_op jit(solution)/shard_map/ppermute | solution.py:21
  6.2 13.1 %collective-permute-start.10 = (bf16[64,1280]{1,0:T(8,128)(2,1)S(1)}, bf16[64,1280]{1,0:T(8,128)(2,1)S(1)}, u32[]{:S(2)}, u32[]{:S(2)}) collective-permute-start(bf16[64,1280]{1,0:T(8,128)(2,1)S(1)} %constant_dynamic-slice_fusion), channel_id=1, source_target_pairs={{0,2},{1,3},{2,0},{3,1},{4,6},{5,7},{6,4},{7,5},{8,10},{9,11},{10,... | collective-permute-start | bytes 491528 | tf_op jit(solution)/shard_map/ppermute | solution.py:21
  10.2 13.1 %collective-permute-start.25 = (bf16[128,1280]{1,0:T(8,128)(2,1)}, bf16[128,1280]{1,0:T(8,128)(2,1)}, u32[]{:S(2)}, u32[]{:S(2)}) collective-permute-start(bf16[128,1280]{1,0:T(8,128)(2,1)} %bitcast.46), channel_id=1, source_target_pairs={{0,8},{8,0},{1,9},{9,1},{2,10},{10,2},{3,11},{11,3},{4,12},{12,4},... | collective-permute-start | bytes 983048 | tf_op jit(solution)/shard_map/ppermute | solution.py:21
  19.9 17.6 %collective-permute-start.13 = (bf16[3,64,1280]{2,1,0:T(8,128)(2,1)S(1)}, bf16[3,64,1280]{2,1,0:T(8,128)(2,1)S(1)}, u32[]{:S(2)}, u32[]{:S(2)}) collective-permute-start(bf16[3,64,1280]{2,1,0:T(8,128)(2,1)S(1)} %pad_maximum_fusion.refs_8_.refs_0_), channel_id=1, source_target_pairs={{0,8},{8,0},{1,9},{9,1},{2,10},{10,2},{3,11},{11,3},{4,12},{12,4},... | collective-permute-start | bytes 1474568 | tf_op jit(solution)/shard_map/ppermute | solution.py:21
  21.7 22.5 %collective-permute-start.12 = (bf16[3,64,1280]{2,1,0:T(8,128)(2,1)S(1)}, bf16[3,64,1280]{2,1,0:T(8,128)(2,1)S(1)}, u32[]{:S(2)}, u32[]{:S(2)}) collective-permute-start(bf16[3,64,1280]{2,1,0:T(8,128)(2,1)S(1)} %pad_maximum_fusion.refs_8_.refs_0_), channel_id=1, source_target_pairs={{0,16},{16,0},{1,17},{17,1},{2,18},{18,2},{3,19},{19,3},{4,20},{20... | collective-permute-start | bytes 1474568 | tf_op jit(solution)/shard_map/ppermute | solution.py:21
  23.3 21.5 %collective-permute-start.15 = (bf16[3,64,1280]{2,1,0:T(8,128)(2,1)S(1)}, bf16[3,64,1280]{2,1,0:T(8,128)(2,1)S(1)}, u32[]{:S(2)}, u32[]{:S(2)}) collective-permute-start(bf16[3,64,1280]{2,1,0:T(8,128)(2,1)S(1)} %pad_maximum_fusion.refs_8_.refs_0_), channel_id=1, source_target_pairs={{0,4},{4,0},{1,5},{5,1},{2,6},{6,2},{3,7},{7,3},{8,12},{12,8},{9,1... | collective-permute-start | bytes 1474568 | tf_op jit(solution)/shard_map/ppermute | solution.py:21
  23.3 14.8 %collective-permute-start.27 = (bf16[128,1280]{1,0:T(8,128)(2,1)}, bf16[128,1280]{1,0:T(8,128)(2,1)}, u32[]{:S(2)}, u32[]{:S(2)}) collective-permute-start(bf16[128,1280]{1,0:T(8,128)(2,1)} %collective-permute-done.25.refs_3_.refs_1_), channel_id=1, source_target_pairs={{0,4},{4,0},{1,5},{5,1},{2,6},{6,2},{3,7},{7,3},{8,12},{12,8},{9,1... | collective-permute-start | bytes 983048 | tf_op jit(solution)/shard_map/ppermute | solution.py:21
  26.4 20.4 %collective-permute-start.3 = (bf16[1280,256]{1,0:T(8,128)(2,1)}, bf16[1280,256]{1,0:T(8,128)(2,1)}, u32[]{:S(2)}, u32[]{:S(2)}) collective-permute-start(bf16[1280,256]{1,0:T(8,128)(2,1)} %constant_dynamic-slice_fusion.1), channel_id=1, source_target_pairs={{0,1},{1,2},{2,3},{3,0},{4,5},{5,6},{6,7},{7,4},{8,9},{9,10},{10,1... | collective-permute-start | bytes 1966088 | tf_op jit(solution)/shard_map/ppermute | solution.py:21
  37.5 16.2 %collective-permute-start.14 = (bf16[3,64,1280]{2,1,0:T(8,128)(2,1)S(1)}, bf16[3,64,1280]{2,1,0:T(8,128)(2,1)}, u32[]{:S(2)}, u32[]{:S(2)}) collective-permute-start(bf16[3,64,1280]{2,1,0:T(8,128)(2,1)S(1)} %collective-permute-done.13.refs_10_.refs_2_), channel_id=1, source_target_pairs={{0,16},{16,0},{1,17},{17,1},{2,18},{18,2},{3,19},{19,3},{4,20},{20... | collective-permute-start | bytes 1474568 | tf_op jit(solution)/shard_map/ppermute | solution.py:21
  38.2 15.5 %collective-permute-start.17 = (bf16[3,64,1280]{2,1,0:T(8,128)(2,1)S(1)}, bf16[3,64,1280]{2,1,0:T(8,128)(2,1)}, u32[]{:S(2)}, u32[]{:S(2)}) collective-permute-start(bf16[3,64,1280]{2,1,0:T(8,128)(2,1)S(1)} %collective-permute-done.13.refs_10_.refs_2_), channel_id=1, source_target_pairs={{0,4},{4,0},{1,5},{5,1},{2,6},{6,2},{3,7},{7,3},{8,12},{12,8},{9,1... | collective-permute-start | bytes 1474568 | tf_op jit(solution)/shard_map/ppermute | solution.py:21
  44.2 39.3 %collective-permute-start.28 = (bf16[2,256,1280]{2,1,0:T(8,128)(2,1)}, bf16[2,256,1280]{2,1,0:T(8,128)(2,1)}, u32[]{:S(2)}, u32[]{:S(2)}) collective-permute-start(bf16[2,256,1280]{2,1,0:T(8,128)(2,1)} %down_partial.6), channel_id=1, source_target_pairs={{0,4},{4,0},{1,5},{5,1},{2,6},{6,2},{3,7},{7,3},{8,12},{12,8},{9,1... | collective-permute-start | bytes 3932168 | tf_op jit(solution)/shard_map/ppermute | solution.py:21
  46.8 25.3 %collective-permute-start.4 = (bf16[1280,256]{1,0:T(8,128)(2,1)}, bf16[1280,256]{1,0:T(8,128)(2,1)}, u32[]{:S(2)}, u32[]{:S(2)}) collective-permute-start(bf16[1280,256]{1,0:T(8,128)(2,1)} %collective-permute-done.3.refs_4_), channel_id=1, source_target_pairs={{0,1},{1,2},{2,3},{3,0},{4,5},{5,6},{6,7},{7,4},{8,9},{9,10},{10,1... | collective-permute-start | bytes 1966088 | tf_op jit(solution)/shard_map/ppermute | solution.py:21
  53.7 33.3 %collective-permute-start.32 = (bf16[2,256,1280]{2,1,0:T(8,128)(2,1)}, bf16[2,256,1280]{2,1,0:T(8,128)(2,1)}, u32[]{:S(2)}, u32[]{:S(2)}) collective-permute-start(bf16[2,256,1280]{2,1,0:T(8,128)(2,1)} %down_partial.9), channel_id=1, source_target_pairs={{0,4},{4,0},{1,5},{5,1},{2,6},{6,2},{3,7},{7,3},{8,12},{12,8},{9,1... | collective-permute-start | bytes 3932168 | tf_op jit(solution)/shard_map/ppermute | solution.py:21
  53.7 18.4 %collective-permute-start.18 = (bf16[3,64,1280]{2,1,0:T(8,128)(2,1)}, bf16[3,64,1280]{2,1,0:T(8,128)(2,1)}, u32[]{:S(2)}, u32[]{:S(2)}) collective-permute-start(bf16[3,64,1280]{2,1,0:T(8,128)(2,1)} %collective-permute-done.14.refs_11_.refs_3_), channel_id=1, source_target_pairs={{0,4},{4,0},{1,5},{5,1},{2,6},{6,2},{3,7},{7,3},{8,12},{12,8},{9,1... | collective-permute-start | bytes 1474568 | tf_op jit(solution)/shard_map/ppermute | solution.py:21
  56.8 24.7 %collective-permute-start.23 = (bf16[1280,256]{1,0:T(8,128)(2,1)}, bf16[1280,256]{1,0:T(8,128)(2,1)S(1)}, u32[]{:S(2)}, u32[]{:S(2)}) collective-permute-start(bf16[1280,256]{1,0:T(8,128)(2,1)} %collective-permute-done.3.refs_4_), channel_id=1, source_target_pairs={{0,16},{16,0},{1,17},{17,1},{2,18},{18,2},{3,19},{19,3},{4,20},{20... | collective-permute-start | bytes 1966088 | tf_op jit(solution)/shard_map/ppermute | solution.py:21
  72.1 23.8 %collective-permute-start.22 = (bf16[1280,256]{1,0:T(8,128)(2,1)}, bf16[1280,256]{1,0:T(8,128)(2,1)S(1)}, u32[]{:S(2)}, u32[]{:S(2)}) collective-permute-start(bf16[1280,256]{1,0:T(8,128)(2,1)} %collective-permute-done.3.refs_4_), channel_id=1, source_target_pairs={{0,4},{4,0},{1,5},{5,1},{2,6},{6,2},{3,7},{7,3},{8,12},{12,8},{9,1... | collective-permute-start | bytes 1966088 | tf_op jit(solution)/shard_map/ppermute | solution.py:21
  72.2 34.8 %collective-permute-start.20 = (bf16[1280,256]{1,0:T(8,128)(2,1)}, bf16[1280,256]{1,0:T(8,128)(2,1)}, u32[]{:S(2)}, u32[]{:S(2)}) collective-permute-start(bf16[1280,256]{1,0:T(8,128)(2,1)} %collective-permute-done.4.refs_4_), channel_id=1, source_target_pairs={{0,16},{16,0},{1,17},{17,1},{2,18},{18,2},{3,19},{19,3},{4,20},{20... | collective-permute-start | bytes 1966088 | tf_op jit(solution)/shard_map/ppermute | solution.py:21
  81.5 21.3 %collective-permute-start.5 = (bf16[1280,256]{1,0:T(8,128)(2,1)}, bf16[1280,256]{1,0:T(8,128)(2,1)}, u32[]{:S(2)}, u32[]{:S(2)}) collective-permute-start(bf16[1280,256]{1,0:T(8,128)(2,1)} %collective-permute-done.4.refs_4_), channel_id=1, source_target_pairs={{0,1},{1,2},{2,3},{3,0},{4,5},{5,6},{6,7},{7,4},{8,9},{9,10},{10,1... | collective-permute-start | bytes 1966088 | tf_op jit(solution)/shard_map/ppermute | solution.py:21
  83.5 12.7 %collective-permute-start.24 = (bf16[1280,256]{1,0:T(8,128)(2,1)S(1)}, bf16[1280,256]{1,0:T(8,128)(2,1)S(1)}, u32[]{:S(2)}, u32[]{:S(2)}) collective-permute-start(bf16[1280,256]{1,0:T(8,128)(2,1)S(1)} %collective-permute-done.23.refs_6_), channel_id=1, source_target_pairs={{0,4},{4,0},{1,5},{5,1},{2,6},{6,2},{3,7},{7,3},{8,12},{12,8},{9,1... | collective-permute-start | bytes 1966088 | tf_op jit(solution)/shard_map/ppermute | solution.py:21
  87.0 17.6 %collective-permute-start.29 = (bf16[2,128,1280]{2,1,0:T(8,128)(2,1)S(1)}, bf16[2,128,1280]{2,1,0:T(8,128)(2,1)S(1)}, u32[]{:S(2)}, u32[]{:S(2)}) collective-permute-start(bf16[2,128,1280]{2,1,0:T(8,128)(2,1)S(1)} %down_partial.8), channel_id=1, source_target_pairs={{0,8},{8,0},{1,9},{9,1},{2,10},{10,2},{3,11},{11,3},{4,12},{12,4},... | collective-permute-start | bytes 1966088 | tf_op jit(solution)/shard_map/ppermute | solution.py:21
  95.9 39.4 %collective-permute-start.19 = (bf16[1280,256]{1,0:T(8,128)(2,1)}, bf16[1280,256]{1,0:T(8,128)(2,1)}, u32[]{:S(2)}, u32[]{:S(2)}) collective-permute-start(bf16[1280,256]{1,0:T(8,128)(2,1)} %collective-permute-done.4.refs_4_), channel_id=1, source_target_pairs={{0,4},{4,0},{1,5},{5,1},{2,6},{6,2},{3,7},{7,3},{8,12},{12,8},{9,1... | collective-permute-start | bytes 1966088 | tf_op jit(solution)/shard_map/ppermute | solution.py:21
  96.2 22.1 %collective-permute-start.33 = (bf16[2,128,1280]{2,1,0:T(8,128)(2,1)S(1)}, bf16[2,128,1280]{2,1,0:T(8,128)(2,1)S(1)}, u32[]{:S(2)}, u32[]{:S(2)}) collective-permute-start(bf16[2,128,1280]{2,1,0:T(8,128)(2,1)S(1)} %down_partial.11), channel_id=1, source_target_pairs={{0,8},{8,0},{1,9},{9,1},{2,10},{10,2},{3,11},{11,3},{4,12},{12,4},... | collective-permute-start | bytes 1966088 | tf_op jit(solution)/shard_map/ppermute | solution.py:21
  102.8 15.6 %collective-permute-start.35 = (f32[256,1024]{1,0:T(8,128)S(1)}, f32[256,1024]{1,0:T(8,128)S(1)}, u32[]{:S(2)}, u32[]{:S(2)}) collective-permute-start(f32[256,1024]{1,0:T(8,128)S(1)} %get-tuple-element.12), channel_id=1, source_target_pairs={{0,4},{4,0},{1,5},{5,1},{2,6},{6,2},{3,7},{7,3},{8,12},{12,8},{9,1... | collective-permute-start | bytes 3145736 | tf_op jit(solution)/shard_map/ppermute | solution.py:21
  104.6 35.1 %collective-permute-start.7 = (bf16[1280,256]{1,0:T(8,128)(2,1)}, bf16[1280,256]{1,0:T(8,128)(2,1)}, u32[]{:S(2)}, u32[]{:S(2)}) collective-permute-start(bf16[1280,256]{1,0:T(8,128)(2,1)} %collective-permute-done.5.refs_4_), channel_id=1, source_target_pairs={{0,16},{16,0},{1,17},{17,1},{2,18},{18,2},{3,19},{19,3},{4,20},{20... | collective-permute-start | bytes 1966088 | tf_op jit(solution)/shard_map/ppermute | solution.py:21
  107.0 59.8 %collective-permute-start.6 = (bf16[1280,256]{1,0:T(8,128)(2,1)}, bf16[1280,256]{1,0:T(8,128)(2,1)}, u32[]{:S(2)}, u32[]{:S(2)}) collective-permute-start(bf16[1280,256]{1,0:T(8,128)(2,1)} %collective-permute-done.5.refs_4_), channel_id=1, source_target_pairs={{0,4},{4,0},{1,5},{5,1},{2,6},{6,2},{3,7},{7,3},{8,12},{12,8},{9,1... | collective-permute-start | bytes 1966088 | tf_op jit(solution)/shard_map/ppermute | solution.py:21
  118.3 19.9 %collective-permute-start.21 = (bf16[1280,256]{1,0:T(8,128)(2,1)}, bf16[1280,256]{1,0:T(8,128)(2,1)}, u32[]{:S(2)}, u32[]{:S(2)}) collective-permute-start(bf16[1280,256]{1,0:T(8,128)(2,1)} %collective-permute-done.20.refs_6_), channel_id=1, source_target_pairs={{0,4},{4,0},{1,5},{5,1},{2,6},{6,2},{3,7},{7,3},{8,12},{12,8},{9,1... | collective-permute-start | bytes 1966088 | tf_op jit(solution)/shard_map/ppermute | solution.py:21
  127.4 37.0 %collective-permute-start.34 = (bf16[128,1280]{1,0:T(8,128)(2,1)}, bf16[128,1280]{1,0:T(8,128)(2,1)}, u32[]{:S(2)}, u32[]{:S(2)}) collective-permute-start(bf16[128,1280]{1,0:T(8,128)(2,1)} %fusion.4), channel_id=1, source_target_pairs={{0,1},{1,2},{2,3},{3,0},{4,5},{5,6},{6,7},{7,4},{8,9},{9,10},{10,1... | collective-permute-start | bytes 983048 | tf_op jit(solution)/shard_map/ppermute | solution.py:21
  129.2 22.5 %all-to-all-start = ((bf16[4,32,1024]{2,1,0:T(8,128)(2,1)}), bf16[4,32,1024]{2,1,0:T(8,128)(2,1)}, u32[]{:S(2)}, u32[]{:S(2)}) async-start(bf16[4,32,1024]{2,1,0:T(8,128)(2,1)} %bitcast.53), calls=%async_computation | async-start | bytes 524288 | tf_op jit(solution)/shard_map/all_to_all | solution.py:382
  135.3 29.1 %collective-permute-start.30 = (bf16[128,1280]{1,0:T(8,128)(2,1)}, bf16[128,1280]{1,0:T(8,128)(2,1)}, u32[]{:S(2)}, u32[]{:S(2)}) collective-permute-start(bf16[128,1280]{1,0:T(8,128)(2,1)} %get-tuple-element.17), channel_id=1, source_target_pairs={{0,2},{1,3},{2,0},{3,1},{4,6},{5,7},{6,4},{7,5},{8,10},{9,11},{10,... | collective-permute-start | bytes 983048 | tf_op jit(solution)/shard_map/ppermute | solution.py:21
  138.2 26.2 %collective-permute-start.31 = (bf16[128,1280]{1,0:T(8,128)(2,1)}, bf16[128,1280]{1,0:T(8,128)(2,1)}, u32[]{:S(2)}, u32[]{:S(2)}) collective-permute-start(bf16[128,1280]{1,0:T(8,128)(2,1)} %get-tuple-element.18), channel_id=1, source_target_pairs={{0,3},{1,0},{2,1},{3,2},{4,7},{5,4},{6,5},{7,6},{8,11},{9,8},{10,9... | collective-permute-start | bytes 983048 | tf_op jit(solution)/shard_map/ppermute | solution.py:21
  139.7 27.1 %collective-permute-start.8 = (bf16[1280,256]{1,0:T(8,128)(2,1)}, bf16[1280,256]{1,0:T(8,128)(2,1)}, u32[]{:S(2)}, u32[]{:S(2)}) collective-permute-start(bf16[1280,256]{1,0:T(8,128)(2,1)} %collective-permute-done.7.refs_6_), channel_id=1, source_target_pairs={{0,4},{4,0},{1,5},{5,1},{2,6},{6,2},{3,7},{7,3},{8,12},{12,8},{9,1... | collective-permute-start | bytes 1966088 | tf_op jit(solution)/shard_map/ppermute | solution.py:21
  153.4 19.2 %all-to-all-start.1 = ((bf16[4,32,1024]{2,1,0:T(8,128)(2,1)}), bf16[4,32,1024]{2,1,0:T(8,128)(2,1)}, u32[]{:S(2)}, u32[]{:S(2)}) async-start(bf16[4,32,1024]{2,1,0:T(8,128)(2,1)} %broadcast_in_dim.2), calls=%async_computation.1 | async-start | bytes 524288 | tf_op jit(solution)/shard_map/all_to_all | solution.py:385
  (36 other events, 209.1 us)

commit v3 on v2

--- a/solution.py
+++ b/solution.py
@@ -12,7 +12,8 @@
 adapter_scale = 2.0
 cores = 2
 bf16, f32 = jnp.bfloat16, jnp.float32
-vmem_bytes = 40 * 1024 * 1024
+vmem_bytes = 16 * 1024 * 1024
+cost_factor = 20
 nt = (((1,), (1,)), ((), ()))
 
 
@@ -58,7 +59,8 @@
     return value.reshape(value.shape[0], -1, cols).swapaxes(0, 1)
 
 
-def call(kernel, name, grid, in_specs, out_specs, out_shape, scratch, scalars, args, flops, aliases=None):
+def call(kernel, name, grid, in_specs, out_specs, out_shape, scratch, scalars, args, flops, aliases=None, in_hbm=()):
+    args = [pltpu.with_memory_space_constraint(a, pltpu.HBM) if n in in_hbm else a for n, a in enumerate(args)]
     moved = sum(math.prod(a.shape) * a.dtype.itemsize for a in args)
     return pl.pallas_call(
         kernel,
@@ -67,7 +69,7 @@
         ),
         out_shape=out_shape,
         compiler_params=pltpu.CompilerParams(vmem_limit_bytes=vmem_bytes),
-        cost_estimate=pl.CostEstimate(flops=flops, bytes_accessed=moved, transcendentals=0),
+        cost_estimate=pl.CostEstimate(flops=cost_factor * flops, bytes_accessed=cost_factor * moved, transcendentals=0),
         input_output_aliases=aliases or {},
         name=name,
     )(*scalars, *args)
@@ -125,37 +127,46 @@
         (first, policy, live),
         [cotangent, *ups],
         2 * rows * kv * total,
-    )
-
-
-def partial_kernel(adds, blocks, low_t_ref, tok_ref, *refs):
+        in_hbm=(0,),
+    )
+
+
+def partial_kernel(adds, low_t_ref, tok_ref, *refs):
     value = jnp.dot(low_t_ref[...], tok_ref[...], preferred_element_type=f32)
     if adds:
         value = value + refs[0][0].astype(f32)
-    refs[-1][0] = value.astype(refs[-1].dtype)
-
-
-def partial_call(low_t, tokens, blocks, cols, added, dtype):
-    rows = low_t.shape[0]
+    at = 0
+    for ref in refs[adds:]:
+        ref[0] = value[at : at + ref.shape[1]].astype(ref.dtype)
+        at += ref.shape[1]
+
+
+def partial_call(low_t, first, rows, tokens, blocks, cols, added, kinds):
     count = blocks.shape[0]
     bc = column_block(cols)
     per = cols // bc
-    in_specs = [whole(low_t), column_spec(low_t.shape[1], cols, lambda i, j, b: (b[i], j))]
+    depth = low_t.shape[1]
+    in_specs = [
+        pl.BlockSpec((rows, depth), lambda i, j, b: (first // rows, 0)),
+        column_spec(depth, cols, lambda i, j, b: (b[i], j)),
+    ]
     args = [low_t, tokens]
     if added is not None:
         in_specs.append(pl.BlockSpec((1, rows, bc), lambda i, j, b: (i, 0, j)))
         args.append(added)
+    part = rows // len(kinds)
     return call(
-        functools.partial(partial_kernel, added is not None),
+        lambda b, *refs: partial_kernel(int(added is not None), *refs),
         "down_partial",
         (count, per),
         in_specs,
-        pl.BlockSpec((1, rows, bc), lambda i, j, b: (i, 0, j)),
-        jax.ShapeDtypeStruct((count, rows, cols), dtype),
+        [pl.BlockSpec((1, part, bc), lambda i, j, b: (i, 0, j)) for _ in kinds],
+        [jax.ShapeDtypeStruct((count, part, cols), kind) for kind in kinds],
         [],
         (blocks,),
         args,
-        2 * rows * low_t.shape[1] * cols * count,
+        2 * rows * depth * cols * count,
+        in_hbm=(1,),
     )
 
 
@@ -195,6 +206,7 @@
         (blocks,),
         [tokens, *downs],
         2 * rows * cols * total,
+        in_hbm=(0,),
     )
 
 
@@ -249,6 +261,7 @@
         (scalars, first, policy),
         [tokens, base, masked, *pieces],
         2 * rows * cols * steps * total + 2 * rows * kv * total,
+        in_hbm=(0,),
     )
 
 
@@ -305,6 +318,7 @@
         args,
         2 * rows * cols * (kv + total),
         aliases,
+        (1 + len(weights),) if not y_size else (),
     )
 
 
@@ -351,15 +365,12 @@
     for chunk in chunks:
         places = ints(*[order[s] for s in chunk])
         sent = [
-            shift(partial_call(low_t[s * split : (s + 1) * split], tokens, places, cols, None, bf16), "core", -s)
+            shift(partial_call(low_t, s * split, split, tokens, places, cols, None, [bf16])[0], "core", -s)
             for s in range(1, c_size)
         ]
         added = sent[0] if len(sent) == 1 else sum(v.astype(f32) for v in sent)
-        for_x = [
-            shift(partial_call(low_t[s * group : (s + 1) * group], tokens, places, cols, added[:, s * group : (s + 1) * group], bf16), "x", -s)
-            for s in range(1, x_size)
-        ]
-        kept = partial_call(low_t[:group], tokens, places, cols, added[:, :group], f32)
+        kept, *for_x = partial_call(low_t, 0, split, tokens, places, cols, added, [f32] + [bf16] * (x_size - 1))
+        for_x = [shift(v, "x", -s - 1) for s, v in enumerate(for_x)]
         for value in for_x:
             kept = kept + value.astype(f32)
         for n, s in enumerate(chunk):

time: 176 us -> 169 us (0.960)
  waiting for transfers between devices: 36.9 us -> 58.8 us
  local copies, waits for them, and re-layouts: 29.7 us -> 14.5 us
  starting transfers between devices: 46.2 us -> 37.9 us
  other arithmetic: 8.61 us -> 4.91 us
    ppermute x37, waiting for transfers between devices: 30.8 us -> 49.4 us  [shift(): lax.ppermute(value, axis, [(i, (i + by) % size) for i in range(size)])]
    unnamed x58 -> x46, local copies, waits for them, and re-layouts: 17.6 us -> 9.52 us
    all_to_all x1, starting transfers between devices: 11 us -> 3.72 us  [body(): lax.all_to_all(spread, 'fsdp', split_axis=0, concat_axis=0, tiled=True)]
    slice x4 -> x0, local copies, waits for them, and re-layouts: 3.75 us -> none  [the longest x2 2.74 us: body(): added[:, s * group:(s + 1) * group]]
    all_to_all x1, waiting for transfers between devices: 6.18 us -> 9.38 us  [body(): lax.all_to_all(own_b, 'fsdp', split_axis=0, concat_axis=0, tiled=True)]
    pallas_call x13 -> x11, Pallas kernels: 51.9 us -> 50.8 us  [call(): pl.pallas_call(kernel, grid_spec=pltpu.PrefetchScalarGridSpec(num_scalar_...]
  transfers between devices with their start and end apart: 39 -> 39, of which waited for: 8 -> 13; matrix products, arithmetic and copies ran while one was open for 11% -> 5% of each run, Pallas kernels for 30% -> 30%
where the time goes in v3:
time: 169 us; the launch traced here: 168 us
  waiting for transfers between devices  58.8 us (35%)
  Pallas kernels  50.8 us (30%)
  starting transfers between devices  37.9 us (22%)
  local copies, waits for them, and re-layouts  14.5 us (9%)
  other arithmetic  4.91 us (3%)
    pallas_call x11, Pallas kernels, call(): pl.pallas_call(kernel, grid_spec=pltpu.PrefetchScalarGridSpec(num_scalar_...  50.8 us
    ppermute x37, waiting for transfers between devices, shift(): lax.ppermute(value, axis, [(i, (i + by) % size) for i in range(size)])  49.4 us
    ppermute x37, starting transfers between devices, shift(): lax.ppermute(value, axis, [(i, (i + by) % size) for i in range(size)])  30.8 us
    unnamed x46, local copies, waits for them, and re-layouts  9.52 us
    all_to_all x1, waiting for transfers between devices, body(): lax.all_to_all(own_b, 'fsdp', split_axis=0, concat_axis=0, tiled=True)  9.38 us
    all_to_all x1, starting transfers between devices, body(): lax.all_to_all(spread, 'fsdp', split_axis=0, concat_axis=0, tiled=True)  3.72 us
    all_to_all x1, starting transfers between devices, body(): lax.all_to_all(own_b, 'fsdp', split_axis=0, concat_axis=0, tiled=True)  3.4 us
  transfers between devices with their start and end apart: 39, of which 13 were waited for; matrix products, arithmetic and copies ran while one was open for 5% of the time, Pallas kernels for 30%

profile of v3, /device:TPU:0, one launch (start us, length us, event | category | flops | bytes accessed | tf_op | source)
XLA Modules:
  0.0 167.9 jit_solution(16117602443226351867)
XLA Ops:
  0.6 3.0 %collective-permute-start = (bf16[128,1024]{1,0:T(8,128)(2,1)}, bf16[128,1024]{1,0:T(8,128)(2,1)S(1)}, u32[]{:S(2)}, u32[]{:S(2)}) collective-permute-start(bf16[128,1024]{1,0:T(8,128)(2,1)} %bitcast.48), channel_id=1, source_target_pairs={{0,8},{8,0},{1,9},{9,1},{2,10},{10,2},{3,11},{11,3},{4,12},{12,4},... | collective-permute-start | bytes 786440 | tf_op jit(solution)/shard_map/ppermute | solution.py:22
  4.6 1.6 collective-permute-start.9
  6.2 2.6 %collective-permute-start.10 = (bf16[64,1280]{1,0:T(8,128)(2,1)S(1)}, bf16[64,1280]{1,0:T(8,128)(2,1)S(1)}, u32[]{:S(2)}, u32[]{:S(2)}) collective-permute-start(bf16[64,1280]{1,0:T(8,128)(2,1)S(1)} %constant_dynamic-slice_fusion), channel_id=1, source_target_pairs={{0,2},{1,3},{2,0},{3,1},{4,6},{5,7},{6,4},{7,5},{8,10},{9,11},{10,... | collective-permute-start | bytes 491528 | tf_op jit(solution)/shard_map/ppermute | solution.py:22
  11.6 1.9 %collective-permute-done.9 = bf16[64,1280]{1,0:T(8,128)(2,1)S(1)} collective-permute-done((bf16[64,1280]{1,0:T(8,128)(2,1)S(1)}, bf16[64,1280]{1,0:T(8,128)(2,1)S(1)}, u32[]{:S(2)}, u32[]{:S(2)}) %collective-permute-start.9) | collective-permute-done | bytes 163872 | tf_op jit(solution)/shard_map/ppermute | solution.py:22
  14.4 5.8 %collective-permute-done.10 = bf16[64,1280]{1,0:T(8,128)(2,1)S(1)} collective-permute-done((bf16[64,1280]{1,0:T(8,128)(2,1)S(1)}, bf16[64,1280]{1,0:T(8,128)(2,1)S(1)}, u32[]{:S(2)}, u32[]{:S(2)}) %collective-permute-start.10) | collective-permute-done | bytes 163872 | tf_op jit(solution)/shard_map/ppermute | solution.py:22
  20.2 4.0 %collective-permute-start.3 = (bf16[1280,256]{1,0:T(8,128)(2,1)S(1)}, bf16[1280,256]{1,0:T(8,128)(2,1)S(1)}, u32[]{:S(2)}, u32[]{:S(2)}) collective-permute-start(bf16[1280,256]{1,0:T(8,128)(2,1)S(1)} %constant_dynamic-slice_fusion.1), channel_id=1, source_target_pairs={{0,1},{1,2},{2,3},{3,0},{4,5},{5,6},{6,7},{7,4},{8,9},{9,10},{10,1... | collective-permute-start | bytes 1966088 | tf_op jit(solution)/shard_map/ppermute | solution.py:22
  26.4 4.2 %low_rank.1 = (bf16[512,1024]{1,0:T(8,128)(2,1)S(1)}, bf16[512,512]{1,0:T(8,128)(2,1)S(1)}, bf16[512,512]{1,0:T(8,128)(2,1)S(1)}) custom-call(s32[4]{0:T(128)S(1)} %pad_add_fusion.first, s32[4]{0:T(128)S(1)} %copy-done.17, s32[4]{0:T(128)S(1)} %copy-done.16, bf16[512,1024]{1,0:T(8,128)(2,1)} %cot_ref.1, bf16[128,1024]{1,0:T(8,128)(2,1)S(1)} %bitcast.50, ...), custom_call_target="tpu_custom_call" | custom-call | flops 10737418240 | bytes 41943040 | tf_op jit(solution)/shard_map/low_rank/pallas_call | solution.py:65
  30.7 4.0 %down_partial.6 = bf16[2,256,1280]{2,1,0:T(8,128)(2,1)S(1)} custom-call(s32[2]{0:T(128)S(1)} %pad_add_fusion.3.b, bf16[512,512]{1,0:T(8,128)(2,1)S(1)} %get-tuple-element.14.refs_0_, bf16[512,5120]{1,0:T(8,128)(2,1)} %tok_ref.3), custom_call_target="tpu_custom_call" | custom-call | flops 13421772800 | bytes 115343360 | tf_op jit(solution)/shard_map/down_partial/pallas_call | solution.py:65
  34.7 4.0 %down_partial.4 = bf16[2,256,1280]{2,1,0:T(8,128)(2,1)S(1)} custom-call(s32[2]{0:T(128)S(1)} %pad_add_fusion.2.b, bf16[512,512]{1,0:T(8,128)(2,1)S(1)} %get-tuple-element.14.refs_0_, bf16[512,5120]{1,0:T(8,128)(2,1)} %tok_ref.3), custom_call_target="tpu_custom_call" | custom-call | flops 13421772800 | bytes 115343360 | tf_op jit(solution)/shard_map/down_partial/pallas_call | solution.py:65
  41.7 5.5 %input_cotangent.4.refs_16_ = bf16[512,5120]{1,0:T(8,128)(2,1)} custom-call(s32[2]{0:T(128)S(1)} %pad_add_fusion.1.scalars, bf16[512,512]{1,0:T(8,128)(2,1)S(1)} %get-tuple-element.12.low_ref, bf16[512,1024]{1,0:T(8,128)(2,1)S(1)} %get-tuple-element.13.refs_0_.refs_1_.refs_2_.refs_3_.masked_ref, bf16[1280,1024]{1,0:T(8,128)(2,1)} %refs_1_.5, ...), custom_call_target="tpu_custom_call" | custom-call | flops 40265318400 | bytes 110100480 | tf_op jit(solution)/shard_map/input_cotangent/pallas_call | solution.py:65
  47.3 5.3 %collective-permute-done.14.refs_11_.refs_3_ = bf16[3,64,1280]{2,1,0:T(8,128)(2,1)S(1)} collective-permute-done((bf16[3,64,1280]{2,1,0:T(8,128)(2,1)S(1)}, bf16[3,64,1280]{2,1,0:T(8,128)(2,1)S(1)}, u32[]{:S(2)}, u32[]{:S(2)}) %collective-permute-start.14) | collective-permute-done | bytes 491552 | tf_op jit(solution)/shard_map/ppermute | solution.py:22
  52.5 3.0 %projected_own.1.base_ref = f32[512,512]{1,0:T(8,128)S(1)} custom-call(s32[4]{0:T(128)S(1)} %pad_add_fusion.4.blocks, bf16[512,5120]{1,0:T(8,128)(2,1)} %tok_ref.3, bf16[128,1280]{1,0:T(8,128)(2,1)S(1)} %bitcast.47, bf16[128,1280]{1,0:T(8,128)(2,1)S(1)} %collective-permute-done.25.refs_3_.refs_1_, ...), custom_call_target="tpu_custom_call" | custom-call | flops 13421772800 | bytes 131072000 | tf_op jit(solution)/shard_map/projected_own/pallas_call | solution.py:65
  56.8 2.2 %collective-permute-done.4.refs_4_ = bf16[1280,256]{1,0:T(8,128)(2,1)S(1)} collective-permute-done((bf16[1280,256]{1,0:T(8,128)(2,1)S(1)}, bf16[1280,256]{1,0:T(8,128)(2,1)S(1)}, u32[]{:S(2)}, u32[]{:S(2)}) %collective-permute-start.4) | collective-permute-done | bytes 655392 | tf_op jit(solution)/shard_map/ppermute | solution.py:22
  59.0 1.6 collective-permute-start.20
  60.6 7.6 %projected.1 = (f32[256,1024]{1,0:T(8,128)S(1)}, f32[256,1024]{1,0:T(8,128)S(1)}) custom-call(s32[5]{0:T(128)S(1)} %concatenate.5.scalars, s32[4]{0:T(128)S(1)} %pad_add_fusion.first, s32[4]{0:T(128)S(1)} %copy-done.17, bf16[512,5120]{1,0:T(8,128)(2,1)} %tok_ref.3, f32[512,512]{1,0:T(8,128)S(1)} %projected_own.1.base_ref, ...), custom_call_target="tpu_custom_call" | custom-call | flops 51002736640 | bytes 225443840 | tf_op jit(solution)/shard_map/projected/pallas_call | solution.py:65
  68.5 4.1 %down_partial.7 = (f32[2,128,1280]{2,1,0:T(8,128)S(1)}, bf16[2,128,1280]{2,1,0:T(8,128)(2,1)S(1)}) custom-call(s32[2]{0:T(128)S(1)} %pad_add_fusion.3.b, bf16[512,512]{1,0:T(8,128)(2,1)S(1)} %get-tuple-element.14.refs_0_, bf16[512,5120]{1,0:T(8,128)(2,1)} %tok_ref.3, bf16[2,256,1280]{2,1,0:T(8,128)(2,1)S(1)} %collective-permute-done.32.refs_2_), custom_call_target="tpu_custom_call" | custom-call | flops 13421772800 | bytes 141557760 | tf_op jit(solution)/shard_map/down_partial/pallas_call | solution.py:65
  75.2 4.1 %down_partial.5 = (f32[2,128,1280]{2,1,0:T(8,128)S(1)}, bf16[2,128,1280]{2,1,0:T(8,128)(2,1)S(1)}) custom-call(s32[2]{0:T(128)S(1)} %pad_add_fusion.2.b, bf16[512,512]{1,0:T(8,128)(2,1)S(1)} %get-tuple-element.14.refs_0_, bf16[512,5120]{1,0:T(8,128)(2,1)} %tok_ref.3, bf16[2,256,1280]{2,1,0:T(8,128)(2,1)S(1)} %collective-permute-done.28.refs_2_), custom_call_target="tpu_custom_call" | custom-call | flops 13421772800 | bytes 141557760 | tf_op jit(solution)/shard_map/down_partial/pallas_call | solution.py:65
  80.4 4.7 %input_cotangent.5.refs_16_ = bf16[512,5120]{1,0:T(8,128)(2,1)} custom-call(s32[7]{0:T(128)S(1)} %stack.128.scalars, bf16[512,512]{1,0:T(8,128)(2,1)S(1)} %get-tuple-element.12.low_ref, bf16[512,1024]{1,0:T(8,128)(2,1)S(1)} %get-tuple-element.13.refs_0_.refs_1_.refs_2_.refs_3_.masked_ref, ...), custom_call_target="tpu_custom_call", output_to_operand_aliasing={{}: (18, {})} | custom-call | flops 40265318400 | bytes 330301440 | tf_op jit(solution)/shard_map/input_cotangent/pallas_call | solution.py:65
  85.1 2.3 %collective-permute-done.20.refs_6_ = bf16[1280,256]{1,0:T(8,128)(2,1)S(1)} collective-permute-done((bf16[1280,256]{1,0:T(8,128)(2,1)S(1)}, bf16[1280,256]{1,0:T(8,128)(2,1)S(1)}, u32[]{:S(2)}, u32[]{:S(2)}) %collective-permute-start.20) | collective-permute-done | bytes 655392 | tf_op jit(solution)/shard_map/ppermute | solution.py:22
  88.9 2.6 %collective-permute-done.5.refs_4_ = bf16[1280,256]{1,0:T(8,128)(2,1)S(1)} collective-permute-done((bf16[1280,256]{1,0:T(8,128)(2,1)S(1)}, bf16[1280,256]{1,0:T(8,128)(2,1)S(1)}, u32[]{:S(2)}, u32[]{:S(2)}) %collective-permute-start.5) | collective-permute-done | bytes 655392 | tf_op jit(solution)/shard_map/ppermute | solution.py:22
  91.5 6.0 %collective-permute-done.33 = bf16[2,128,1280]{2,1,0:T(8,128)(2,1)S(1)} collective-permute-done((bf16[2,128,1280]{2,1,0:T(8,128)(2,1)S(1)}, bf16[2,128,1280]{2,1,0:T(8,128)(2,1)S(1)}, u32[]{:S(2)}, u32[]{:S(2)}) %collective-permute-start.33) | collective-permute-done | bytes 655392 | tf_op jit(solution)/shard_map/ppermute | solution.py:22
  99.0 11.7 %collective-permute-done.29 = bf16[2,128,1280]{2,1,0:T(8,128)(2,1)S(1)} collective-permute-done((bf16[2,128,1280]{2,1,0:T(8,128)(2,1)S(1)}, bf16[2,128,1280]{2,1,0:T(8,128)(2,1)S(1)}, u32[]{:S(2)}, u32[]{:S(2)}) %collective-permute-start.29) | collective-permute-done | bytes 655392 | tf_op jit(solution)/shard_map/ppermute | solution.py:22
  110.7 2.6 %collective-permute-start.34 = (bf16[128,1280]{1,0:T(8,128)(2,1)}, bf16[128,1280]{1,0:T(8,128)(2,1)}, u32[]{:S(2)}, u32[]{:S(2)}) collective-permute-start(bf16[128,1280]{1,0:T(8,128)(2,1)} %fusion.4), channel_id=1, source_target_pairs={{0,1},{1,2},{2,3},{3,0},{4,5},{5,6},{6,7},{7,4},{8,9},{9,10},{10,1... | collective-permute-start | bytes 983048 | tf_op jit(solution)/shard_map/ppermute | solution.py:22
  115.0 2.0 %collective-permute-start.31 = (bf16[128,1280]{1,0:T(8,128)(2,1)}, bf16[128,1280]{1,0:T(8,128)(2,1)}, u32[]{:S(2)}, u32[]{:S(2)}) collective-permute-start(bf16[128,1280]{1,0:T(8,128)(2,1)} %get-tuple-element.22), channel_id=1, source_target_pairs={{0,3},{1,0},{2,1},{3,2},{4,7},{5,4},{6,5},{7,6},{8,11},{9,8},{10,9... | collective-permute-start | bytes 983048 | tf_op jit(solution)/shard_map/ppermute | solution.py:22
  117.6 4.7 %input_cotangent.6.refs_16_ = bf16[512,5120]{1,0:T(8,128)(2,1)} custom-call(s32[7]{0:T(128)S(1)} %stack.126.scalars, bf16[512,512]{1,0:T(8,128)(2,1)S(1)} %get-tuple-element.12.low_ref, bf16[512,1024]{1,0:T(8,128)(2,1)S(1)} %get-tuple-element.13.refs_0_.refs_1_.refs_2_.refs_3_.masked_ref, ...), custom_call_target="tpu_custom_call", output_to_operand_aliasing={{}: (18, {})} | custom-call | flops 40265318400 | bytes 330301440 | tf_op jit(solution)/shard_map/input_cotangent/pallas_call | solution.py:65
  122.4 1.6 collective-permute-done.36
  124.7 3.4 %all-to-all-start = ((bf16[4,32,1024]{2,1,0:T(8,128)(2,1)}), bf16[4,32,1024]{2,1,0:T(8,128)(2,1)S(1)}, u32[]{:S(2)}, u32[]{:S(2)}) async-start(bf16[4,32,1024]{2,1,0:T(8,128)(2,1)} %bitcast.52), calls=%async_computation | async-start | bytes 524288 | tf_op jit(solution)/shard_map/all_to_all | solution.py:393
  128.1 8.5 %collective-permute-done.30 = bf16[128,1280]{1,0:T(8,128)(2,1)} collective-permute-done((bf16[128,1280]{1,0:T(8,128)(2,1)}, bf16[128,1280]{1,0:T(8,128)(2,1)}, u32[]{:S(2)}, u32[]{:S(2)}) %collective-permute-start.30) | collective-permute-done | bytes 327712 | tf_op jit(solution)/shard_map/ppermute | solution.py:22
  136.6 2.4 %fusion.2 = f32[128,1280]{1,0:T(8,128)} fusion(f32[2,128,1280]{2,1,0:T(8,128)} %copy-done.22, bf16[128,1280]{1,0:T(8,128)(2,1)} %collective-permute-done.34, bf16[128,1280]{1,0:T(8,128)(2,1)} %collective-permute-done.31, bf16[128,1280]{1,0:T(8,128)(2,1)} %collective-permute-done.30), kind=kLoop, calls=%fused_computation.6 | loop fusion | flops 1146880 | bytes 2293760 | tf_op jit(solution)/shard_map/mul | solution.py:378
  138.9 9.4 %all-to-all-done = bf16[4,32,1024]{2,1,0:T(8,128)(2,1)S(1)} async-done(((bf16[4,32,1024]{2,1,0:T(8,128)(2,1)}), bf16[4,32,1024]{2,1,0:T(8,128)(2,1)S(1)}, u32[]{:S(2)}, u32[]{:S(2)}) %all-to-all-start) | async-done | bytes 262176 | tf_op jit(solution)/shard_map/all_to_all | solution.py:393
  149.1 3.7 %all-to-all-start.1 = ((bf16[4,32,1024]{2,1,0:T(8,128)(2,1)}), bf16[4,32,1024]{2,1,0:T(8,128)(2,1)S(1)}, u32[]{:S(2)}, u32[]{:S(2)}) async-start(bf16[4,32,1024]{2,1,0:T(8,128)(2,1)} %broadcast_in_dim.2), calls=%async_computation.1 | async-start | bytes 524288 | tf_op jit(solution)/shard_map/all_to_all | solution.py:396
  162.3 4.7 %input_cotangent.7 = bf16[512,5120]{1,0:T(8,128)(2,1)} custom-call(s32[7]{0:T(128)S(1)} %stack.115.scalars, bf16[512,512]{1,0:T(8,128)(2,1)S(1)} %copy-done.21, bf16[512,1024]{1,0:T(8,128)(2,1)S(1)} %copy-done.19, bf16[512,1024]{1,0:T(8,128)(2,1)S(1)} %copy-done.19, bf16[512,1024]{1,0:T(8,128)(2,1)S(1)} %copy-done.19, ...), custom_call_target="tpu_custom_call", output_to_operand_aliasing={{}: (18, {})} | custom-call | flops 40265318400 | bytes 330301440 | tf_op jit(solution)/shard_map/input_cotangent/pallas_call | solution.py:65
  (127 shorter events, 32.0 us)
Async XLA Ops:
  0.6 13.3 %collective-permute-start = (bf16[128,1024]{1,0:T(8,128)(2,1)}, bf16[128,1024]{1,0:T(8,128)(2,1)S(1)}, u32[]{:S(2)}, u32[]{:S(2)}) collective-permute-start(bf16[128,1024]{1,0:T(8,128)(2,1)} %bitcast.48), channel_id=1, source_target_pairs={{0,8},{8,0},{1,9},{9,1},{2,10},{10,2},{3,11},{11,3},{4,12},{12,4},... | collective-permute-start | bytes 786440 | tf_op jit(solution)/shard_map/ppermute | solution.py:22
  3.6 20.6 %collective-permute-start.1 = (bf16[128,1024]{1,0:T(8,128)(2,1)}, bf16[128,1024]{1,0:T(8,128)(2,1)S(1)}, u32[]{:S(2)}, u32[]{:S(2)}) collective-permute-start(bf16[128,1024]{1,0:T(8,128)(2,1)} %bitcast.49), channel_id=1, source_target_pairs={{0,4},{4,0},{1,5},{5,1},{2,6},{6,2},{3,7},{7,3},{8,12},{12,8},{9,1... | collective-permute-start | bytes 786440 | tf_op jit(solution)/shard_map/ppermute | solution.py:22
  6.2 14.0 %collective-permute-start.10 = (bf16[64,1280]{1,0:T(8,128)(2,1)S(1)}, bf16[64,1280]{1,0:T(8,128)(2,1)S(1)}, u32[]{:S(2)}, u32[]{:S(2)}) collective-permute-start(bf16[64,1280]{1,0:T(8,128)(2,1)S(1)} %constant_dynamic-slice_fusion), channel_id=1, source_target_pairs={{0,2},{1,3},{2,0},{3,1},{4,6},{5,7},{6,4},{7,5},{8,10},{9,11},{10,... | collective-permute-start | bytes 491528 | tf_op jit(solution)/shard_map/ppermute | solution.py:22
  20.2 18.5 %collective-permute-start.26 = (bf16[128,1280]{1,0:T(8,128)(2,1)S(1)}, bf16[128,1280]{1,0:T(8,128)(2,1)S(1)}, u32[]{:S(2)}, u32[]{:S(2)}) collective-permute-start(bf16[128,1280]{1,0:T(8,128)(2,1)S(1)} %bitcast.45), channel_id=1, source_target_pairs={{0,4},{4,0},{1,5},{5,1},{2,6},{6,2},{3,7},{7,3},{8,12},{12,8},{9,1... | collective-permute-start | bytes 983048 | tf_op jit(solution)/shard_map/ppermute | solution.py:22
  20.2 20.5 %collective-permute-start.3 = (bf16[1280,256]{1,0:T(8,128)(2,1)S(1)}, bf16[1280,256]{1,0:T(8,128)(2,1)S(1)}, u32[]{:S(2)}, u32[]{:S(2)}) collective-permute-start(bf16[1280,256]{1,0:T(8,128)(2,1)S(1)} %constant_dynamic-slice_fusion.1), channel_id=1, source_target_pairs={{0,1},{1,2},{2,3},{3,0},{4,5},{5,6},{6,7},{7,4},{8,9},{9,10},{10,1... | collective-permute-start | bytes 1966088 | tf_op jit(solution)/shard_map/ppermute | solution.py:22
  24.3 15.0 %collective-permute-start.13 = (bf16[3,64,1280]{2,1,0:T(8,128)(2,1)S(1)}, bf16[3,64,1280]{2,1,0:T(8,128)(2,1)S(1)}, u32[]{:S(2)}, u32[]{:S(2)}) collective-permute-start(bf16[3,64,1280]{2,1,0:T(8,128)(2,1)S(1)} %pad_maximum_fusion.refs_8_.refs_0_), channel_id=1, source_target_pairs={{0,8},{8,0},{1,9},{9,1},{2,10},{10,2},{3,11},{11,3},{4,12},{12,4},... | collective-permute-start | bytes 1474568 | tf_op jit(solution)/shard_map/ppermute | solution.py:22
  24.9 15.0 %collective-permute-start.12 = (bf16[3,64,1280]{2,1,0:T(8,128)(2,1)S(1)}, bf16[3,64,1280]{2,1,0:T(8,128)(2,1)S(1)}, u32[]{:S(2)}, u32[]{:S(2)}) collective-permute-start(bf16[3,64,1280]{2,1,0:T(8,128)(2,1)S(1)} %pad_maximum_fusion.refs_8_.refs_0_), channel_id=1, source_target_pairs={{0,16},{16,0},{1,17},{17,1},{2,18},{18,2},{3,19},{19,3},{4,20},{20... | collective-permute-start | bytes 1474568 | tf_op jit(solution)/shard_map/ppermute | solution.py:22
  26.4 13.4 %collective-permute-start.27 = (bf16[128,1280]{1,0:T(8,128)(2,1)S(1)}, bf16[128,1280]{1,0:T(8,128)(2,1)S(1)}, u32[]{:S(2)}, u32[]{:S(2)}) collective-permute-start(bf16[128,1280]{1,0:T(8,128)(2,1)S(1)} %collective-permute-done.25.refs_3_.refs_1_), channel_id=1, source_target_pairs={{0,4},{4,0},{1,5},{5,1},{2,6},{6,2},{3,7},{7,3},{8,12},{12,8},{9,1... | collective-permute-start | bytes 983048 | tf_op jit(solution)/shard_map/ppermute | solution.py:22
  38.8 16.8 %collective-permute-start.15 = (bf16[3,64,1280]{2,1,0:T(8,128)(2,1)S(1)}, bf16[3,64,1280]{2,1,0:T(8,128)(2,1)S(1)}, u32[]{:S(2)}, u32[]{:S(2)}) collective-permute-start(bf16[3,64,1280]{2,1,0:T(8,128)(2,1)S(1)} %pad_maximum_fusion.refs_8_.refs_0_), channel_id=1, source_target_pairs={{0,4},{4,0},{1,5},{5,1},{2,6},{6,2},{3,7},{7,3},{8,12},{12,8},{9,1... | collective-permute-start | bytes 1474568 | tf_op jit(solution)/shard_map/ppermute | solution.py:22
  39.3 13.2 %collective-permute-start.14 = (bf16[3,64,1280]{2,1,0:T(8,128)(2,1)S(1)}, bf16[3,64,1280]{2,1,0:T(8,128)(2,1)S(1)}, u32[]{:S(2)}, u32[]{:S(2)}) collective-permute-start(bf16[3,64,1280]{2,1,0:T(8,128)(2,1)S(1)} %collective-permute-done.13.refs_10_.refs_2_), channel_id=1, source_target_pairs={{0,16},{16,0},{1,17},{17,1},{2,18},{18,2},{3,19},{19,3},{4,20},{20... | collective-permute-start | bytes 1474568 | tf_op jit(solution)/shard_map/ppermute | solution.py:22
  39.8 16.3 %collective-permute-start.17 = (bf16[3,64,1280]{2,1,0:T(8,128)(2,1)S(1)}, bf16[3,64,1280]{2,1,0:T(8,128)(2,1)S(1)}, u32[]{:S(2)}, u32[]{:S(2)}) collective-permute-start(bf16[3,64,1280]{2,1,0:T(8,128)(2,1)S(1)} %collective-permute-done.13.refs_10_.refs_2_), channel_id=1, source_target_pairs={{0,4},{4,0},{1,5},{5,1},{2,6},{6,2},{3,7},{7,3},{8,12},{12,8},{9,1... | collective-permute-start | bytes 1474568 | tf_op jit(solution)/shard_map/ppermute | solution.py:22
  39.9 16.4 %collective-permute-start.16 = (bf16[3,64,1280]{2,1,0:T(8,128)(2,1)S(1)}, bf16[3,64,1280]{2,1,0:T(8,128)(2,1)S(1)}, u32[]{:S(2)}, u32[]{:S(2)}) collective-permute-start(bf16[3,64,1280]{2,1,0:T(8,128)(2,1)S(1)} %collective-permute-done.12.refs_9_.refs_1_), channel_id=1, source_target_pairs={{0,4},{4,0},{1,5},{5,1},{2,6},{6,2},{3,7},{7,3},{8,12},{12,8},{9,1... | collective-permute-start | bytes 1474568 | tf_op jit(solution)/shard_map/ppermute | solution.py:22
  40.7 18.4 %collective-permute-start.4 = (bf16[1280,256]{1,0:T(8,128)(2,1)S(1)}, bf16[1280,256]{1,0:T(8,128)(2,1)S(1)}, u32[]{:S(2)}, u32[]{:S(2)}) collective-permute-start(bf16[1280,256]{1,0:T(8,128)(2,1)S(1)} %collective-permute-done.3.refs_4_), channel_id=1, source_target_pairs={{0,1},{1,2},{2,3},{3,0},{4,5},{5,6},{6,7},{7,4},{8,9},{9,10},{10,1... | collective-permute-start | bytes 1966088 | tf_op jit(solution)/shard_map/ppermute | solution.py:22
  55.6 12.7 %collective-permute-start.32 = (bf16[2,256,1280]{2,1,0:T(8,128)(2,1)S(1)}, bf16[2,256,1280]{2,1,0:T(8,128)(2,1)S(1)}, u32[]{:S(2)}, u32[]{:S(2)}) collective-permute-start(bf16[2,256,1280]{2,1,0:T(8,128)(2,1)S(1)} %down_partial.6), channel_id=1, source_target_pairs={{0,4},{4,0},{1,5},{5,1},{2,6},{6,2},{3,7},{7,3},{8,12},{12,8},{9,1... | collective-permute-start | bytes 3932168 | tf_op jit(solution)/shard_map/ppermute | solution.py:22
  56.2 19.0 %collective-permute-start.28 = (bf16[2,256,1280]{2,1,0:T(8,128)(2,1)S(1)}, bf16[2,256,1280]{2,1,0:T(8,128)(2,1)S(1)}, u32[]{:S(2)}, u32[]{:S(2)}) collective-permute-start(bf16[2,256,1280]{2,1,0:T(8,128)(2,1)S(1)} %down_partial.4), channel_id=1, source_target_pairs={{0,4},{4,0},{1,5},{5,1},{2,6},{6,2},{3,7},{7,3},{8,12},{12,8},{9,1... | collective-permute-start | bytes 3932168 | tf_op jit(solution)/shard_map/ppermute | solution.py:22
  56.3 17.5 %collective-permute-start.23 = (bf16[1280,256]{1,0:T(8,128)(2,1)S(1)}, bf16[1280,256]{1,0:T(8,128)(2,1)S(1)}, u32[]{:S(2)}, u32[]{:S(2)}) collective-permute-start(bf16[1280,256]{1,0:T(8,128)(2,1)S(1)} %collective-permute-done.3.refs_4_), channel_id=1, source_target_pairs={{0,16},{16,0},{1,17},{17,1},{2,18},{18,2},{3,19},{19,3},{4,20},{20... | collective-permute-start | bytes 1966088 | tf_op jit(solution)/shard_map/ppermute | solution.py:22
  59.0 20.3 %collective-permute-start.22 = (bf16[1280,256]{1,0:T(8,128)(2,1)S(1)}, bf16[1280,256]{1,0:T(8,128)(2,1)S(1)}, u32[]{:S(2)}, u32[]{:S(2)}) collective-permute-start(bf16[1280,256]{1,0:T(8,128)(2,1)S(1)} %collective-permute-done.3.refs_4_), channel_id=1, source_target_pairs={{0,4},{4,0},{1,5},{5,1},{2,6},{6,2},{3,7},{7,3},{8,12},{12,8},{9,1... | collective-permute-start | bytes 1966088 | tf_op jit(solution)/shard_map/ppermute | solution.py:22
  59.0 28.4 %collective-permute-start.20 = (bf16[1280,256]{1,0:T(8,128)(2,1)S(1)}, bf16[1280,256]{1,0:T(8,128)(2,1)S(1)}, u32[]{:S(2)}, u32[]{:S(2)}) collective-permute-start(bf16[1280,256]{1,0:T(8,128)(2,1)S(1)} %collective-permute-done.4.refs_4_), channel_id=1, source_target_pairs={{0,16},{16,0},{1,17},{17,1},{2,18},{18,2},{3,19},{19,3},{4,20},{20... | collective-permute-start | bytes 1966088 | tf_op jit(solution)/shard_map/ppermute | solution.py:22
  68.3 46.7 %collective-permute-start.19 = (bf16[1280,256]{1,0:T(8,128)(2,1)S(1)}, bf16[1280,256]{1,0:T(8,128)(2,1)S(1)}, u32[]{:S(2)}, u32[]{:S(2)}) collective-permute-start(bf16[1280,256]{1,0:T(8,128)(2,1)S(1)} %collective-permute-done.4.refs_4_), channel_id=1, source_target_pairs={{0,4},{4,0},{1,5},{5,1},{2,6},{6,2},{3,7},{7,3},{8,12},{12,8},{9,1... | collective-permute-start | bytes 1966088 | tf_op jit(solution)/shard_map/ppermute | solution.py:22
  73.8 17.6 %collective-permute-start.5 = (bf16[1280,256]{1,0:T(8,128)(2,1)S(1)}, bf16[1280,256]{1,0:T(8,128)(2,1)S(1)}, u32[]{:S(2)}, u32[]{:S(2)}) collective-permute-start(bf16[1280,256]{1,0:T(8,128)(2,1)S(1)} %collective-permute-done.4.refs_4_), channel_id=1, source_target_pairs={{0,1},{1,2},{2,3},{3,0},{4,5},{5,6},{6,7},{7,4},{8,9},{9,10},{10,1... | collective-permute-start | bytes 1966088 | tf_op jit(solution)/shard_map/ppermute | solution.py:22
  79.3 35.0 %collective-permute-start.35 = (f32[256,1024]{1,0:T(8,128)S(1)}, f32[256,1024]{1,0:T(8,128)S(1)}, u32[]{:S(2)}, u32[]{:S(2)}) collective-permute-start(f32[256,1024]{1,0:T(8,128)S(1)} %get-tuple-element.20), channel_id=1, source_target_pairs={{0,4},{4,0},{1,5},{5,1},{2,6},{6,2},{3,7},{7,3},{8,12},{12,8},{9,1... | collective-permute-start | bytes 3145736 | tf_op jit(solution)/shard_map/ppermute | solution.py:22
  79.9 17.6 %collective-permute-start.33 = (bf16[2,128,1280]{2,1,0:T(8,128)(2,1)S(1)}, bf16[2,128,1280]{2,1,0:T(8,128)(2,1)S(1)}, u32[]{:S(2)}, u32[]{:S(2)}) collective-permute-start(bf16[2,128,1280]{2,1,0:T(8,128)(2,1)S(1)} %get-tuple-element.18), channel_id=1, source_target_pairs={{0,8},{8,0},{1,9},{9,1},{2,10},{10,2},{3,11},{11,3},{4,12},{12,4},... | collective-permute-start | bytes 1966088 | tf_op jit(solution)/shard_map/ppermute | solution.py:22
  87.4 23.3 %collective-permute-start.29 = (bf16[2,128,1280]{2,1,0:T(8,128)(2,1)S(1)}, bf16[2,128,1280]{2,1,0:T(8,128)(2,1)S(1)}, u32[]{:S(2)}, u32[]{:S(2)}) collective-permute-start(bf16[2,128,1280]{2,1,0:T(8,128)(2,1)S(1)} %get-tuple-element.16), channel_id=1, source_target_pairs={{0,8},{8,0},{1,9},{9,1},{2,10},{10,2},{3,11},{11,3},{4,12},{12,4},... | collective-permute-start | bytes 1966088 | tf_op jit(solution)/shard_map/ppermute | solution.py:22
  91.5 25.6 %collective-permute-start.21 = (bf16[1280,256]{1,0:T(8,128)(2,1)S(1)}, bf16[1280,256]{1,0:T(8,128)(2,1)S(1)}, u32[]{:S(2)}, u32[]{:S(2)}) collective-permute-start(bf16[1280,256]{1,0:T(8,128)(2,1)S(1)} %collective-permute-done.20.refs_6_), channel_id=1, source_target_pairs={{0,4},{4,0},{1,5},{5,1},{2,6},{6,2},{3,7},{7,3},{8,12},{12,8},{9,1... | collective-permute-start | bytes 1966088 | tf_op jit(solution)/shard_map/ppermute | solution.py:22
  97.5 24.8 %collective-permute-start.7 = (bf16[1280,256]{1,0:T(8,128)(2,1)S(1)}, bf16[1280,256]{1,0:T(8,128)(2,1)S(1)}, u32[]{:S(2)}, u32[]{:S(2)}) collective-permute-start(bf16[1280,256]{1,0:T(8,128)(2,1)S(1)} %collective-permute-done.5.refs_4_), channel_id=1, source_target_pairs={{0,16},{16,0},{1,17},{17,1},{2,18},{18,2},{3,19},{19,3},{4,20},{20... | collective-permute-start | bytes 1966088 | tf_op jit(solution)/shard_map/ppermute | solution.py:22
  110.7 17.4 %collective-permute-start.34 = (bf16[128,1280]{1,0:T(8,128)(2,1)}, bf16[128,1280]{1,0:T(8,128)(2,1)}, u32[]{:S(2)}, u32[]{:S(2)}) collective-permute-start(bf16[128,1280]{1,0:T(8,128)(2,1)} %fusion.4), channel_id=1, source_target_pairs={{0,1},{1,2},{2,3},{3,0},{4,5},{5,6},{6,7},{7,4},{8,9},{9,10},{10,1... | collective-permute-start | bytes 983048 | tf_op jit(solution)/shard_map/ppermute | solution.py:22
  114.4 22.2 %collective-permute-start.30 = (bf16[128,1280]{1,0:T(8,128)(2,1)}, bf16[128,1280]{1,0:T(8,128)(2,1)}, u32[]{:S(2)}, u32[]{:S(2)}) collective-permute-start(bf16[128,1280]{1,0:T(8,128)(2,1)} %get-tuple-element.21), channel_id=1, source_target_pairs={{0,2},{1,3},{2,0},{3,1},{4,6},{5,7},{6,4},{7,5},{8,10},{9,11},{10,... | collective-permute-start | bytes 983048 | tf_op jit(solution)/shard_map/ppermute | solution.py:22
  115.0 21.6 %collective-permute-start.31 = (bf16[128,1280]{1,0:T(8,128)(2,1)}, bf16[128,1280]{1,0:T(8,128)(2,1)}, u32[]{:S(2)}, u32[]{:S(2)}) collective-permute-start(bf16[128,1280]{1,0:T(8,128)(2,1)} %get-tuple-element.22), channel_id=1, source_target_pairs={{0,3},{1,0},{2,1},{3,2},{4,7},{5,4},{6,5},{7,6},{8,11},{9,8},{10,9... | collective-permute-start | bytes 983048 | tf_op jit(solution)/shard_map/ppermute | solution.py:22
  122.4 30.5 %collective-permute-start.6 = (bf16[1280,256]{1,0:T(8,128)(2,1)S(1)}, bf16[1280,256]{1,0:T(8,128)(2,1)S(1)}, u32[]{:S(2)}, u32[]{:S(2)}) collective-permute-start(bf16[1280,256]{1,0:T(8,128)(2,1)S(1)} %collective-permute-done.5.refs_4_), channel_id=1, source_target_pairs={{0,4},{4,0},{1,5},{5,1},{2,6},{6,2},{3,7},{7,3},{8,12},{12,8},{9,1... | collective-permute-start | bytes 1966088 | tf_op jit(solution)/shard_map/ppermute | solution.py:22
  123.9 28.9 %collective-permute-start.8 = (bf16[1280,256]{1,0:T(8,128)(2,1)S(1)}, bf16[1280,256]{1,0:T(8,128)(2,1)S(1)}, u32[]{:S(2)}, u32[]{:S(2)}) collective-permute-start(bf16[1280,256]{1,0:T(8,128)(2,1)S(1)} %collective-permute-done.7.refs_6_), channel_id=1, source_target_pairs={{0,4},{4,0},{1,5},{5,1},{2,6},{6,2},{3,7},{7,3},{8,12},{12,8},{9,1... | collective-permute-start | bytes 1966088 | tf_op jit(solution)/shard_map/ppermute | solution.py:22
  124.7 23.6 %all-to-all-start = ((bf16[4,32,1024]{2,1,0:T(8,128)(2,1)}), bf16[4,32,1024]{2,1,0:T(8,128)(2,1)S(1)}, u32[]{:S(2)}, u32[]{:S(2)}) async-start(bf16[4,32,1024]{2,1,0:T(8,128)(2,1)} %bitcast.52), calls=%async_computation | async-start | bytes 524288 | tf_op jit(solution)/shard_map/all_to_all | solution.py:393
  149.1 17.9 %all-to-all-start.1 = ((bf16[4,32,1024]{2,1,0:T(8,128)(2,1)}), bf16[4,32,1024]{2,1,0:T(8,128)(2,1)S(1)}, u32[]{:S(2)}, u32[]{:S(2)}) async-start(bf16[4,32,1024]{2,1,0:T(8,128)(2,1)} %broadcast_in_dim.2), calls=%async_computation.1 | async-start | bytes 524288 | tf_op jit(solution)/shard_map/all_to_all | solution.py:396
  (30 other events, 788.5 us)

commit v4 on v3

--- a/solution.py
+++ b/solution.py
@@ -59,20 +59,21 @@
     return value.reshape(value.shape[0], -1, cols).swapaxes(0, 1)
 
 
-def call(kernel, name, grid, in_specs, out_specs, out_shape, scratch, scalars, args, flops, aliases=None, in_hbm=()):
+def call(kernel, name, grid, in_specs, out_specs, out_shape, scratch, scalars, args, flops, aliases=None, in_hbm=(), later_than=()):
     args = [pltpu.with_memory_space_constraint(a, pltpu.HBM) if n in in_hbm else a for n, a in enumerate(args)]
     moved = sum(math.prod(a.shape) * a.dtype.itemsize for a in args)
+    count, extra = len(scalars) + len(args), len(later_than)
     return pl.pallas_call(
-        kernel,
+        lambda *refs: kernel(*refs[:count], *refs[count + extra :]),
         grid_spec=pltpu.PrefetchScalarGridSpec(
-            num_scalar_prefetch=len(scalars), grid=grid, in_specs=in_specs, out_specs=out_specs, scratch_shapes=scratch
+            num_scalar_prefetch=len(scalars), grid=grid, in_specs=in_specs + [pl.BlockSpec(memory_space=pl.ANY)] * extra, out_specs=out_specs, scratch_shapes=scratch
         ),
         out_shape=out_shape,
         compiler_params=pltpu.CompilerParams(vmem_limit_bytes=vmem_bytes),
         cost_estimate=pl.CostEstimate(flops=cost_factor * flops, bytes_accessed=cost_factor * moved, transcendentals=0),
         input_output_aliases=aliases or {},
         name=name,
-    )(*scalars, *args)
+    )(*scalars, *args, *later_than)
 
 
 def whole(array):
@@ -170,6 +171,59 @@
     )
 
 
+def settle_kernel(kept_ref, *refs):
+    count = kept_ref.shape[0]
+    got_refs, out_refs = refs[:-count], refs[-count:]
+    for m, out_ref in enumerate(out_refs):
+        value = kept_ref[m]
+        for ref in got_refs:
+            value = value + ref[m].astype(f32)
+        out_ref[...] = value.astype(out_ref.dtype)
+
+
+def settle_call(kept, got, kinds, later_than):
+    shapes = [jax.ShapeDtypeStruct(kept.shape[1:], kind) for kind in kinds]
+    args = [kept, *got]
+    specs = [whole(v) for v in args]
+    outs = [whole(v) for v in shapes]
+    return call(settle_kernel, "settle", (1,), specs, outs, shapes, [], (), args, 0, later_than=later_than)
+
+
+def spread_kernel(group, x_at, kept_ref, *refs):
+    out_ref = refs[-1]
+    chunk = out_ref.shape[2]
+    for s in range(out_ref.shape[0]):
+        for m in range(out_ref.shape[1]):
+            here = slice(s * group + m * chunk, s * group + (m + 1) * chunk)
+            value = kept_ref[here, :]
+            for ref in refs[:-1]:
+                value = value + ref[here, :]
+            out_ref[x_at[s], m] = value.astype(bf16)
+
+
+def spread_call(x_at, kept, got, group, z_size):
+    rows, kv = kept.shape
+    shape = jax.ShapeDtypeStruct((rows // group, z_size, group // z_size, kv), bf16)
+    args = [kept, *got]
+    kernel = functools.partial(spread_kernel, group)
+    return call(kernel, "spread", (1,), [whole(v) for v in args], whole(shape), shape, [], (x_at,), args, 0)
+
+
+def share_kernel(scale, parts_ref, out_ref):
+    value = parts_ref[0].astype(f32)
+    for n in range(1, parts_ref.shape[0]):
+        value = value + parts_ref[n].astype(f32)
+    value = (value * scale).astype(bf16)
+    for n in range(out_ref.shape[0]):
+        out_ref[n] = value
+
+
+def share_call(parts, scale, copies, later_than=()):
+    shape = jax.ShapeDtypeStruct((copies,) + parts.shape[1:], bf16)
+    kernel = functools.partial(share_kernel, scale)
+    return call(kernel, "share", (1,), [whole(parts)], whole(shape), shape, [], (), [parts], 0, later_than=later_than)
+
+
 def place_down(store, refs, half, back, scalars, at):
     y_size = len(back)
     for n, ref in enumerate(refs):
@@ -284,7 +338,7 @@
     out_ref[...] = value.astype(bf16)
 
 
-def input_call(scalars, low, masked, weights, downs, step, y_size, out, width):
+def input_call(scalars, low, masked, weights, downs, step, y_size, out, width, last=False, later_than=()):
     rows, kv = masked.shape
     cols = weights[0].shape[0]
     depth = weights[0].shape[1]
@@ -318,7 +372,8 @@
         args,
         2 * rows * cols * (kv + total),
         aliases,
-        (1 + len(weights),) if not y_size else (),
+        (1 + len(weights),) if not y_size else range(1 + 2 * len(weights), 1 + 2 * len(weights) + len(downs)) if last else (),
+        later_than,
     )
 
 
@@ -361,7 +416,7 @@
     normalizer = 1.0 / math.sqrt(rows * x_size * c_size * z_size)
     order = [(z + s) % z_size for s in range(z_size)]
     chunks = [list(range(z_size // 2, z_size)), list(range(z_size // 2))]
-    got_a = []
+    over_x = []
     for chunk in chunks:
         places = ints(*[order[s] for s in chunk])
         sent = [
@@ -371,11 +426,7 @@
         added = sent[0] if len(sent) == 1 else sum(v.astype(f32) for v in sent)
         kept, *for_x = partial_call(low_t, 0, split, tokens, places, cols, added, [f32] + [bf16] * (x_size - 1))
         for_x = [shift(v, "x", -s - 1) for s, v in enumerate(for_x)]
-        for value in for_x:
-            kept = kept + value.astype(f32)
-        for n, s in enumerate(chunk):
-            got_a.append(shift(kept[n].astype(bf16), "fsdp", s).astype(f32) if s else kept[n])
-    grad_a = sum(got_a[1:], got_a[0]) * normalizer
+        over_x.append((kept, for_x))
 
     blocks = ints(*[(z - s) % z_size for s in range(z_size)])
     base = projected_first(tokens, own_downs, blocks, rows)
@@ -383,17 +434,20 @@
     sent_b, kept_b = projected_call(
         scalars, first, tile_token_policy, y_size, tokens, base, masked, downs, y_size, half, rank, split
     )
-    for s in range(1, c_size):
-        kept_b = kept_b + shift(sent_b[(s - 1) * split : s * split], "core", -s)
-    kept_b = kept_b.reshape(x_size, group, kv)
-    own_b = kept_b[0]
-    for s in range(1, x_size):
-        own_b = own_b + shift(kept_b[s].astype(bf16), "x", -s).astype(f32)
-    own_b = own_b.reshape(z_size, -1, kv).astype(bf16)
-    parts_b = lax.all_to_all(own_b, "fsdp", split_axis=0, concat_axis=0, tiled=True)
-    share_b = (jnp.sum(parts_b.astype(f32), axis=0) * (adapter_scale * normalizer)).astype(bf16)
-    spread = jnp.broadcast_to(share_b[None], (z_size,) + share_b.shape)
-    grad_b = lax.all_to_all(spread, "fsdp", split_axis=0, concat_axis=0, tiled=True).astype(f32)
+    got_b = [shift(sent_b[(s - 1) * split : s * split], "core", -s) for s in range(1, c_size)]
+    x_at = ints(*[(x - s) % x_size for s in range(x_size)])
+    own_b = spread_call(x_at, kept_b, got_b, group, z_size)
+    own_b = own_b.reshape((x_size * z_size,) + own_b.shape[2:])
+    parts_b = lax.all_to_all(own_b, ("x", "fsdp"), split_axis=0, concat_axis=0, tiled=True)
+    share_b = share_call(parts_b, adapter_scale * normalizer, z_size)
+    grad_b = lax.all_to_all(share_b, "fsdp", split_axis=0, concat_axis=0, tiled=True).astype(f32)
+
+    got_a, early = [], []
+    for chunk, (kept, for_x), before in zip(chunks, over_x, (own_b, share_b)):
+        parts = settle_call(kept, for_x, [bf16 if s else f32 for s in chunk], [before])
+        early = early or list(parts[:1])
+        got_a += [shift(v, "fsdp", s).astype(f32) if s else v for s, v in zip(chunk, parts)]
+    grad_a = sum(got_a[1:], got_a[0]) * normalizer
 
     out = input_call(ints(z, 0), low, masked, [value_weight], own_downs, 0, 0, None, width)
     held = lax.dynamic_slice_in_dim(value_weight, (y * c_size + c) * depth, depth, 1)
@@ -405,7 +459,9 @@
                 weights.append(got)
                 places.append(league_back[dy] * c_size + (c - dc) % c_size)
         out = input_call(
-            ints((z - s) % z_size, *places, *league_back), low, masked, weights, downs, s - 1, y_size, out, width
+            ints((z - s) % z_size, *places, *league_back), low, masked, weights, downs, s - 1, y_size, out, width,
+            later_than=early if s == z_size - 2 else (),
+            last=s >= z_size - 2,
         )
     if cols % 128:
         out = out.swapaxes(0, 1).reshape(rows, width)

time: 169 us -> 153 us (0.905)
  waiting for transfers between devices: 58.8 us -> 46.9 us
  Pallas kernels: 50.8 us -> 60.1 us
  local copies, waits for them, and re-layouts: 14.5 us -> 5.55 us
  starting transfers between devices: 37.9 us -> 35.3 us
    ppermute x37 -> x36, waiting for transfers between devices: 49.4 us -> 31.6 us  [shift(): lax.ppermute(value, axis, [(i, (i + by) % size) for i in range(size)])]
    pallas_call x11 -> x15, Pallas kernels: 50.8 us -> 60.1 us  [call(): pl.pallas_call(lambda *refs: kernel(*refs[:count], *refs[count + extra:])...]
    unnamed x46 -> x36, local copies, waits for them, and re-layouts: 9.52 us -> 2.33 us
    all_to_all x2, waiting for transfers between devices: 9.38 us -> 15.3 us  [the longest x1 7.87 us: body(): lax.all_to_all(own_b, ('x', 'fsdp'), split_axis=0, concat_axis=0, tiled=T...]
    ppermute x37 -> x36, starting transfers between devices: 30.8 us -> 28.2 us  [shift(): lax.ppermute(value, axis, [(i, (i + by) % size) for i in range(size)])]
    convert_element_type x2 -> x0, local copies, waits for them, and re-layouts: 1.76 us -> none  [body(): kept[n].astype(bf16)]
  transfers between devices with their start and end apart: 39 -> 38, of which waited for: 13 -> 11; matrix products, arithmetic and copies ran while one was open for 5% -> 4% of each run, Pallas kernels for 30% -> 40%
where the time goes in v4:
time: 153 us; the launch traced here: 152 us
  Pallas kernels  60.1 us (39%)
  waiting for transfers between devices  46.9 us (31%)
  starting transfers between devices  35.3 us (23%)
  local copies, waits for them, and re-layouts  5.55 us (4%)
  other arithmetic  3.31 us (2%)
    pallas_call x15, Pallas kernels, call(): pl.pallas_call(lambda *refs: kernel(*refs[:count], *refs[count + extra:])...  60.1 us
    ppermute x36, waiting for transfers between devices, shift(): lax.ppermute(value, axis, [(i, (i + by) % size) for i in range(size)])  31.6 us
    ppermute x36, starting transfers between devices, shift(): lax.ppermute(value, axis, [(i, (i + by) % size) for i in range(size)])  28.2 us
    all_to_all x1, waiting for transfers between devices, body(): lax.all_to_all(own_b, ('x', 'fsdp'), split_axis=0, concat_axis=0, tiled=T...  7.87 us
    all_to_all x1, waiting for transfers between devices, body(): lax.all_to_all(share_b, 'fsdp', split_axis=0, concat_axis=0, tiled=True)  7.44 us
    all_to_all x1, starting transfers between devices, body(): lax.all_to_all(share_b, 'fsdp', split_axis=0, concat_axis=0, tiled=True)  3.65 us
    all_to_all x1, starting transfers between devices, body(): lax.all_to_all(own_b, ('x', 'fsdp'), split_axis=0, concat_axis=0, tiled=T...  3.49 us
  transfers between devices with their start and end apart: 38, of which 11 were waited for; matrix products, arithmetic and copies ran while one was open for 4% of the time, Pallas kernels for 40%

profile of v4, /device:TPU:0, one launch (start us, length us, event | category | flops | bytes accessed | tf_op | source)
XLA Modules:
  0.0 152.1 jit_solution(4876575895638120553)
XLA Ops:
  0.7 3.0 %collective-permute-start = (bf16[128,1024]{1,0:T(8,128)(2,1)}, bf16[128,1024]{1,0:T(8,128)(2,1)S(1)}, u32[]{:S(2)}, u32[]{:S(2)}) collective-permute-start(bf16[128,1024]{1,0:T(8,128)(2,1)} %bitcast.36), channel_id=1, source_target_pairs={{0,8},{8,0},{1,9},{9,1},{2,10},{10,2},{3,11},{11,3},{4,12},{12,4},... | collective-permute-start | bytes 786440 | tf_op jit(solution)/shard_map/ppermute | solution.py:22
  4.6 1.6 %collective-permute-start.9 = (bf16[64,1280]{1,0:T(8,128)(2,1)S(1)}, bf16[64,1280]{1,0:T(8,128)(2,1)S(1)}, u32[]{:S(2)}, u32[]{:S(2)}) collective-permute-start(bf16[64,1280]{1,0:T(8,128)(2,1)S(1)} %constant_dynamic-slice_fusion), channel_id=1, source_target_pairs={{0,1},{1,2},{2,3},{3,0},{4,5},{5,6},{6,7},{7,4},{8,9},{9,10},{10,1... | collective-permute-start | bytes 491528 | tf_op jit(solution)/shard_map/ppermute | solution.py:22
  6.2 2.6 %collective-permute-start.10 = (bf16[64,1280]{1,0:T(8,128)(2,1)S(1)}, bf16[64,1280]{1,0:T(8,128)(2,1)S(1)}, u32[]{:S(2)}, u32[]{:S(2)}) collective-permute-start(bf16[64,1280]{1,0:T(8,128)(2,1)S(1)} %constant_dynamic-slice_fusion), channel_id=1, source_target_pairs={{0,2},{1,3},{2,0},{3,1},{4,6},{5,7},{6,4},{7,5},{8,10},{9,11},{10,... | collective-permute-start | bytes 491528 | tf_op jit(solution)/shard_map/ppermute | solution.py:22
  10.3 2.0 %constant_dynamic-slice_fusion.1 = bf16[1280,256]{1,0:T(8,128)(2,1)} fusion(bf16[1280,1024]{1,0:T(8,128)(2,1)} %refs_3_.4, s32[]{:T(128)S(6)} %select_n.112), kind=kLoop, calls=%fused_computation.10 | loop fusion | bytes 1310724 | tf_op jit(solution)/shard_map/dynamic_slice | solution.py:453
  14.4 5.8 %collective-permute-done.10 = bf16[64,1280]{1,0:T(8,128)(2,1)S(1)} collective-permute-done((bf16[64,1280]{1,0:T(8,128)(2,1)S(1)}, bf16[64,1280]{1,0:T(8,128)(2,1)S(1)}, u32[]{:S(2)}, u32[]{:S(2)}) %collective-permute-start.10) | collective-permute-done | bytes 163872 | tf_op jit(solution)/shard_map/ppermute | solution.py:22
  20.2 4.0 %collective-permute-start.3 = (bf16[1280,256]{1,0:T(8,128)(2,1)}, bf16[1280,256]{1,0:T(8,128)(2,1)S(1)}, u32[]{:S(2)}, u32[]{:S(2)}) collective-permute-start(bf16[1280,256]{1,0:T(8,128)(2,1)} %constant_dynamic-slice_fusion.1), channel_id=1, source_target_pairs={{0,1},{1,2},{2,3},{3,0},{4,5},{5,6},{6,7},{7,4},{8,9},{9,10},{10,1... | collective-permute-start | bytes 1966088 | tf_op jit(solution)/shard_map/ppermute | solution.py:22
  24.9 1.5 collective-permute-start.12
  26.5 4.2 %low_rank.1 = (bf16[512,1024]{1,0:T(8,128)(2,1)S(1)}, bf16[512,512]{1,0:T(8,128)(2,1)S(1)}, bf16[512,512]{1,0:T(8,128)(2,1)S(1)}) custom-call(s32[4]{0:T(128)S(1)} %pad_add_fusion.refs_0_.refs_1_, s32[4]{0:T(128)S(1)} %copy-done.11, s32[4]{0:T(128)S(1)} %copy-done.10, bf16[512,1024]{1,0:T(8,128)(2,1)} %refs_3_.3, bf16[128,1024]{1,0:T(8,128)(2,1)S(1)} %bitcast.38, ...), custom_call_target="tpu_custom_call" | custom-call | flops 10737418240 | bytes 41943040 | tf_op jit(solution)/shard_map/low_rank/pallas_call | solution.py:66
  30.7 4.0 %down_partial.6 = bf16[2,256,1280]{2,1,0:T(8,128)(2,1)S(1)} custom-call(s32[2]{0:T(128)S(1)} %pad_add_fusion.5.refs_0_, bf16[512,512]{1,0:T(8,128)(2,1)S(1)} %get-tuple-element.18.refs_1_, bf16[512,5120]{1,0:T(8,128)(2,1)} %refs_2_.11), custom_call_target="tpu_custom_call" | custom-call | flops 13421772800 | bytes 115343360 | tf_op jit(solution)/shard_map/down_partial/pallas_call | solution.py:66
  34.8 4.0 %down_partial.4 = bf16[2,256,1280]{2,1,0:T(8,128)(2,1)S(1)} custom-call(s32[2]{0:T(128)S(1)} %pad_add_fusion.2.refs_0_, bf16[512,512]{1,0:T(8,128)(2,1)S(1)} %get-tuple-element.18.refs_1_, bf16[512,5120]{1,0:T(8,128)(2,1)} %refs_2_.11), custom_call_target="tpu_custom_call" | custom-call | flops 13421772800 | bytes 115343360 | tf_op jit(solution)/shard_map/down_partial/pallas_call | solution.py:66
  42.0 5.6 %input_cotangent.4.refs_18_ = bf16[512,5120]{1,0:T(8,128)(2,1)} custom-call(s32[2]{0:T(128)S(1)} %pad_add_fusion.1.refs_0_, bf16[512,512]{1,0:T(8,128)(2,1)S(1)} %get-tuple-element.16.refs_1_, bf16[512,1024]{1,0:T(8,128)(2,1)S(1)} %get-tuple-element.17.refs_2_.refs_3_.refs_4_.refs_5_, bf16[1280,1024]{1,0:T(8,128)(2,1)} %refs_3_.4, ...), custom_call_target="tpu_custom_call" | custom-call | flops 40265318400 | bytes 110100480 | tf_op jit(solution)/shard_map/input_cotangent/pallas_call | solution.py:66
  47.5 5.0 %collective-permute-done.14.refs_13_.refs_9_ = bf16[3,64,1280]{2,1,0:T(8,128)(2,1)S(1)} collective-permute-done((bf16[3,64,1280]{2,1,0:T(8,128)(2,1)S(1)}, bf16[3,64,1280]{2,1,0:T(8,128)(2,1)S(1)}, u32[]{:S(2)}, u32[]{:S(2)}) %collective-permute-start.14) | collective-permute-done | bytes 491552 | tf_op jit(solution)/shard_map/ppermute | solution.py:22
  52.6 3.0 %projected_own.1.refs_4_ = f32[512,512]{1,0:T(8,128)S(1)} custom-call(s32[4]{0:T(128)S(1)} %pad_add_fusion.4.refs_0_, bf16[512,5120]{1,0:T(8,128)(2,1)} %refs_2_.11, bf16[128,1280]{1,0:T(8,128)(2,1)S(1)} %bitcast.35, bf16[128,1280]{1,0:T(8,128)(2,1)S(1)} %collective-permute-done.25.refs_5_.refs_3_, ...), custom_call_target="tpu_custom_call" | custom-call | flops 13421772800 | bytes 131072000 | tf_op jit(solution)/shard_map/projected_own/pallas_call | solution.py:66
  56.9 2.5 %collective-permute-done.4.refs_6_ = bf16[1280,256]{1,0:T(8,128)(2,1)} collective-permute-done((bf16[1280,256]{1,0:T(8,128)(2,1)S(1)}, bf16[1280,256]{1,0:T(8,128)(2,1)}, u32[]{:S(2)}, u32[]{:S(2)}) %collective-permute-start.4) | collective-permute-done | bytes 655392 | tf_op jit(solution)/shard_map/ppermute | solution.py:22
  59.4 1.6 %collective-permute-start.20 = (bf16[1280,256]{1,0:T(8,128)(2,1)}, bf16[1280,256]{1,0:T(8,128)(2,1)}, u32[]{:S(2)}, u32[]{:S(2)}) collective-permute-start(bf16[1280,256]{1,0:T(8,128)(2,1)} %collective-permute-done.4.refs_6_), channel_id=1, source_target_pairs={{0,16},{16,0},{1,17},{17,1},{2,18},{18,2},{3,19},{19,3},{4,20},{20... | collective-permute-start | bytes 1966088 | tf_op jit(solution)/shard_map/ppermute | solution.py:22
  61.0 7.6 %projected.1 = (f32[256,1024]{1,0:T(8,128)S(1)}, f32[256,1024]{1,0:T(8,128)S(1)}) custom-call(s32[5]{0:T(128)S(1)} %concatenate.5.refs_0_, s32[4]{0:T(128)S(1)} %pad_add_fusion.refs_0_.refs_1_, s32[4]{0:T(128)S(1)} %copy-done.11, bf16[512,5120]{1,0:T(8,128)(2,1)} %refs_2_.11, f32[512,512]{1,0:T(8,128)S(1)} %projected_own.1.refs_4_, ...), custom_call_target="tpu_custom_call" | custom-call | flops 51002736640 | bytes 225443840 | tf_op jit(solution)/shard_map/projected/pallas_call | solution.py:66
  68.8 5.0 %down_partial.7 = (f32[2,128,1280]{2,1,0:T(8,128)S(1)}, bf16[2,128,1280]{2,1,0:T(8,128)(2,1)}) custom-call(s32[2]{0:T(128)S(1)} %pad_add_fusion.5.refs_0_, bf16[512,512]{1,0:T(8,128)(2,1)S(1)} %get-tuple-element.18.refs_1_, bf16[512,5120]{1,0:T(8,128)(2,1)} %refs_2_.11, bf16[2,256,1280]{2,1,0:T(8,128)(2,1)S(1)} %collective-permute-done.33.refs_3_), custom_call_target="tpu_custom_call" | custom-call | flops 13421772800 | bytes 141557760 | tf_op jit(solution)/shard_map/down_partial/pallas_call | solution.py:66
  73.9 1.6 %collective-permute-start.5 = (bf16[1280,256]{1,0:T(8,128)(2,1)}, bf16[1280,256]{1,0:T(8,128)(2,1)}, u32[]{:S(2)}, u32[]{:S(2)}) collective-permute-start(bf16[1280,256]{1,0:T(8,128)(2,1)} %collective-permute-done.4.refs_6_), channel_id=1, source_target_pairs={{0,1},{1,2},{2,3},{3,0},{4,5},{5,6},{6,7},{7,4},{8,9},{9,10},{10,1... | collective-permute-start | bytes 1966088 | tf_op jit(solution)/shard_map/ppermute | solution.py:22
  75.5 4.9 %down_partial.5 = (f32[2,128,1280]{2,1,0:T(8,128)S(1)}, bf16[2,128,1280]{2,1,0:T(8,128)(2,1)}) custom-call(s32[2]{0:T(128)S(1)} %pad_add_fusion.2.refs_0_, bf16[512,512]{1,0:T(8,128)(2,1)S(1)} %get-tuple-element.18.refs_1_, bf16[512,5120]{1,0:T(8,128)(2,1)} %refs_2_.11, bf16[2,256,1280]{2,1,0:T(8,128)(2,1)S(1)} %collective-permute-done.28.refs_3_), custom_call_target="tpu_custom_call" | custom-call | flops 13421772800 | bytes 141557760 | tf_op jit(solution)/shard_map/down_partial/pallas_call | solution.py:66
  81.4 6.2 %collective-permute-done.20.refs_8_ = bf16[1280,256]{1,0:T(8,128)(2,1)} collective-permute-done((bf16[1280,256]{1,0:T(8,128)(2,1)}, bf16[1280,256]{1,0:T(8,128)(2,1)}, u32[]{:S(2)}, u32[]{:S(2)}) %collective-permute-start.20) | collective-permute-done | bytes 655392 | tf_op jit(solution)/shard_map/ppermute | solution.py:22
  87.5 5.4 %collective-permute-done.5.refs_6_ = bf16[1280,256]{1,0:T(8,128)(2,1)} collective-permute-done((bf16[1280,256]{1,0:T(8,128)(2,1)}, bf16[1280,256]{1,0:T(8,128)(2,1)}, u32[]{:S(2)}, u32[]{:S(2)}) %collective-permute-start.5) | collective-permute-done | bytes 655392 | tf_op jit(solution)/shard_map/ppermute | solution.py:22
  93.5 4.7 %input_cotangent.5.refs_18_ = bf16[512,5120]{1,0:T(8,128)(2,1)} custom-call(s32[7]{0:T(128)S(1)} %stack.137.refs_0_, bf16[512,512]{1,0:T(8,128)(2,1)S(1)} %get-tuple-element.16.refs_1_, bf16[512,1024]{1,0:T(8,128)(2,1)S(1)} %get-tuple-element.17.refs_2_.refs_3_.refs_4_.refs_5_, ...), custom_call_target="tpu_custom_call", output_to_operand_aliasing={{}: (18, {})} | custom-call | flops 40265318400 | bytes 330301440 | tf_op jit(solution)/shard_map/input_cotangent/pallas_call | solution.py:66
  100.8 3.5 %all-to-all-start = ((bf16[8,32,1024]{2,1,0:T(8,128)(2,1)}), bf16[8,32,1024]{2,1,0:T(8,128)(2,1)S(1)}, u32[]{:S(2)}, u32[]{:S(2)}) async-start(bf16[8,32,1024]{2,1,0:T(8,128)(2,1)} %bitcast.24.refs_2_), calls=%async_computation | async-start | bytes 1048576 | tf_op jit(solution)/shard_map/all_to_all | solution.py:441
  104.3 5.0 %collective-permute-done.7.refs_8_ = bf16[1280,256]{1,0:T(8,128)(2,1)} collective-permute-done((bf16[1280,256]{1,0:T(8,128)(2,1)}, bf16[1280,256]{1,0:T(8,128)(2,1)}, u32[]{:S(2)}, u32[]{:S(2)}) %collective-permute-start.7) | collective-permute-done | bytes 655392 | tf_op jit(solution)/shard_map/ppermute | solution.py:22
  109.4 1.9 %settle.2 = (bf16[128,1280]{1,0:T(8,128)(2,1)}, bf16[128,1280]{1,0:T(8,128)(2,1)S(1)}) custom-call(f32[2,128,1280]{2,1,0:T(8,128)S(1)} %get-tuple-element.19.refs_0_, bf16[2,128,1280]{2,1,0:T(8,128)(2,1)} %collective-permute-done.29.refs_1_, bf16[8,32,1024]{2,1,0:T(8,128)(2,1)} %bitcast.24.refs_2_), custom_call_target="tpu_custom_call" | custom-call | bytes 39321600 | tf_op jit(solution)/shard_map/settle/pallas_call | solution.py:66
  113.6 5.9 %input_cotangent.6.refs_18_ = bf16[512,5120]{1,0:T(8,128)(2,1)} custom-call(s32[7]{0:T(128)S(1)} %stack.135.refs_0_, bf16[512,512]{1,0:T(8,128)(2,1)S(1)} %copy-done.16, bf16[512,1024]{1,0:T(8,128)(2,1)S(1)} %copy-done.13, bf16[512,1024]{1,0:T(8,128)(2,1)S(1)} %copy-done.13, bf16[512,1024]{1,0:T(8,128)(2,1)S(1)} %copy-done.13, ...), custom_call_target="tpu_custom_call", output_to_operand_aliasing={{}: (18, {})} | custom-call | flops 40265318400 | bytes 330301440 | tf_op jit(solution)/shard_map/input_cotangent/pallas_call | solution.py:66
  119.5 7.9 %all-to-all-done.refs_0_ = bf16[8,32,1024]{2,1,0:T(8,128)(2,1)S(1)} async-done(((bf16[8,32,1024]{2,1,0:T(8,128)(2,1)}), bf16[8,32,1024]{2,1,0:T(8,128)(2,1)S(1)}, u32[]{:S(2)}, u32[]{:S(2)}) %all-to-all-start) | async-done | bytes 524320 | tf_op jit(solution)/shard_map/all_to_all | solution.py:441
  129.3 3.0 %collective-permute-start.35 = (bf16[128,1280]{1,0:T(8,128)(2,1)S(1)}, bf16[128,1280]{1,0:T(8,128)(2,1)S(1)}, u32[]{:S(2)}, u32[]{:S(2)}) collective-permute-start(bf16[128,1280]{1,0:T(8,128)(2,1)S(1)} %get-tuple-element.28), channel_id=1, source_target_pairs={{0,1},{1,2},{2,3},{3,0},{4,5},{5,6},{6,7},{7,4},{8,9},{9,10},{10,1... | collective-permute-start | bytes 983048 | tf_op jit(solution)/shard_map/ppermute | solution.py:22
  132.4 5.9 %input_cotangent.7 = bf16[512,5120]{1,0:T(8,128)(2,1)} custom-call(s32[7]{0:T(128)S(1)} %stack.124.refs_0_, bf16[512,512]{1,0:T(8,128)(2,1)S(1)} %copy-done.17, bf16[512,1024]{1,0:T(8,128)(2,1)S(1)} %copy-done.14, bf16[512,1024]{1,0:T(8,128)(2,1)S(1)} %copy-done.14, bf16[512,1024]{1,0:T(8,128)(2,1)S(1)} %copy-done.14, ...), custom_call_target="tpu_custom_call", output_to_operand_aliasing={{}: (18, {})} | custom-call | flops 40265318400 | bytes 330301440 | tf_op jit(solution)/shard_map/input_cotangent/pallas_call | solution.py:66
  138.2 3.7 %all-to-all-start.1 = ((bf16[4,32,1024]{2,1,0:T(8,128)(2,1)}), bf16[4,32,1024]{2,1,0:T(8,128)(2,1)S(1)}, u32[]{:S(2)}, u32[]{:S(2)}) async-start(bf16[4,32,1024]{2,1,0:T(8,128)(2,1)} %share.1.refs_2_), calls=%async_computation.1 | async-start | bytes 524288 | tf_op jit(solution)/shard_map/all_to_all | solution.py:443
  141.9 2.0 %add_multiply_fusion = f32[128,1280]{1,0:T(8,128)} fusion(bf16[128,1280]{1,0:T(8,128)(2,1)S(1)} %collective-permute-done.35, f32[128,1280]{1,0:T(8,128)S(1)} %get-tuple-element.27, bf16[128,1280]{1,0:T(8,128)(2,1)} %collective-permute-done.32, bf16[128,1280]{1,0:T(8,128)(2,1)S(1)} %collective-permute-done.31), kind=kLoop, calls=%fused_computation | loop fusion | flops 1146880 | bytes 2293760 | tf_op jit(solution)/shard_map/mul | solution.py:450
  143.9 7.4 %all-to-all-done.1 = bf16[4,32,1024]{2,1,0:T(8,128)(2,1)S(1)} async-done(((bf16[4,32,1024]{2,1,0:T(8,128)(2,1)}), bf16[4,32,1024]{2,1,0:T(8,128)(2,1)S(1)}, u32[]{:S(2)}, u32[]{:S(2)}) %all-to-all-start.1) | async-done | bytes 262176 | tf_op jit(solution)/shard_map/all_to_all | solution.py:443
  (110 shorter events, 19.3 us)
Async XLA Ops:
  0.7 13.3 %collective-permute-start = (bf16[128,1024]{1,0:T(8,128)(2,1)}, bf16[128,1024]{1,0:T(8,128)(2,1)S(1)}, u32[]{:S(2)}, u32[]{:S(2)}) collective-permute-start(bf16[128,1024]{1,0:T(8,128)(2,1)} %bitcast.36), channel_id=1, source_target_pairs={{0,8},{8,0},{1,9},{9,1},{2,10},{10,2},{3,11},{11,3},{4,12},{12,4},... | collective-permute-start | bytes 786440 | tf_op jit(solution)/shard_map/ppermute | solution.py:22
  3.7 20.6 %collective-permute-start.1 = (bf16[128,1024]{1,0:T(8,128)(2,1)}, bf16[128,1024]{1,0:T(8,128)(2,1)S(1)}, u32[]{:S(2)}, u32[]{:S(2)}) collective-permute-start(bf16[128,1024]{1,0:T(8,128)(2,1)} %bitcast.37), channel_id=1, source_target_pairs={{0,4},{4,0},{1,5},{5,1},{2,6},{6,2},{3,7},{7,3},{8,12},{12,8},{9,1... | collective-permute-start | bytes 786440 | tf_op jit(solution)/shard_map/ppermute | solution.py:22
  6.2 14.0 %collective-permute-start.10 = (bf16[64,1280]{1,0:T(8,128)(2,1)S(1)}, bf16[64,1280]{1,0:T(8,128)(2,1)S(1)}, u32[]{:S(2)}, u32[]{:S(2)}) collective-permute-start(bf16[64,1280]{1,0:T(8,128)(2,1)S(1)} %constant_dynamic-slice_fusion), channel_id=1, source_target_pairs={{0,2},{1,3},{2,0},{3,1},{4,6},{5,7},{6,4},{7,5},{8,10},{9,11},{10,... | collective-permute-start | bytes 491528 | tf_op jit(solution)/shard_map/ppermute | solution.py:22
  20.2 18.6 %collective-permute-start.26 = (bf16[128,1280]{1,0:T(8,128)(2,1)}, bf16[128,1280]{1,0:T(8,128)(2,1)S(1)}, u32[]{:S(2)}, u32[]{:S(2)}) collective-permute-start(bf16[128,1280]{1,0:T(8,128)(2,1)} %bitcast.33), channel_id=1, source_target_pairs={{0,4},{4,0},{1,5},{5,1},{2,6},{6,2},{3,7},{7,3},{8,12},{12,8},{9,1... | collective-permute-start | bytes 983048 | tf_op jit(solution)/shard_map/ppermute | solution.py:22
  20.2 20.7 %collective-permute-start.3 = (bf16[1280,256]{1,0:T(8,128)(2,1)}, bf16[1280,256]{1,0:T(8,128)(2,1)S(1)}, u32[]{:S(2)}, u32[]{:S(2)}) collective-permute-start(bf16[1280,256]{1,0:T(8,128)(2,1)} %constant_dynamic-slice_fusion.1), channel_id=1, source_target_pairs={{0,1},{1,2},{2,3},{3,0},{4,5},{5,6},{6,7},{7,4},{8,9},{9,10},{10,1... | collective-permute-start | bytes 1966088 | tf_op jit(solution)/shard_map/ppermute | solution.py:22
  24.3 15.0 %collective-permute-start.13 = (bf16[3,64,1280]{2,1,0:T(8,128)(2,1)S(1)}, bf16[3,64,1280]{2,1,0:T(8,128)(2,1)S(1)}, u32[]{:S(2)}, u32[]{:S(2)}) collective-permute-start(bf16[3,64,1280]{2,1,0:T(8,128)(2,1)S(1)} %pad_maximum_fusion.refs_10_.refs_6_), channel_id=1, source_target_pairs={{0,8},{8,0},{1,9},{9,1},{2,10},{10,2},{3,11},{11,3},{4,12},{12,4},... | collective-permute-start | bytes 1474568 | tf_op jit(solution)/shard_map/ppermute | solution.py:22
  24.9 15.0 %collective-permute-start.12 = (bf16[3,64,1280]{2,1,0:T(8,128)(2,1)S(1)}, bf16[3,64,1280]{2,1,0:T(8,128)(2,1)S(1)}, u32[]{:S(2)}, u32[]{:S(2)}) collective-permute-start(bf16[3,64,1280]{2,1,0:T(8,128)(2,1)S(1)} %pad_maximum_fusion.refs_10_.refs_6_), channel_id=1, source_target_pairs={{0,16},{16,0},{1,17},{17,1},{2,18},{18,2},{3,19},{19,3},{4,20},{20... | collective-permute-start | bytes 1474568 | tf_op jit(solution)/shard_map/ppermute | solution.py:22
  26.4 13.4 %collective-permute-start.27 = (bf16[128,1280]{1,0:T(8,128)(2,1)S(1)}, bf16[128,1280]{1,0:T(8,128)(2,1)S(1)}, u32[]{:S(2)}, u32[]{:S(2)}) collective-permute-start(bf16[128,1280]{1,0:T(8,128)(2,1)S(1)} %collective-permute-done.25.refs_5_.refs_3_), channel_id=1, source_target_pairs={{0,4},{4,0},{1,5},{5,1},{2,6},{6,2},{3,7},{7,3},{8,12},{12,8},{9,1... | collective-permute-start | bytes 983048 | tf_op jit(solution)/shard_map/ppermute | solution.py:22
  38.8 16.8 %collective-permute-start.15 = (bf16[3,64,1280]{2,1,0:T(8,128)(2,1)S(1)}, bf16[3,64,1280]{2,1,0:T(8,128)(2,1)S(1)}, u32[]{:S(2)}, u32[]{:S(2)}) collective-permute-start(bf16[3,64,1280]{2,1,0:T(8,128)(2,1)S(1)} %pad_maximum_fusion.refs_10_.refs_6_), channel_id=1, source_target_pairs={{0,4},{4,0},{1,5},{5,1},{2,6},{6,2},{3,7},{7,3},{8,12},{12,8},{9,1... | collective-permute-start | bytes 1474568 | tf_op jit(solution)/shard_map/ppermute | solution.py:22
  39.4 13.2 %collective-permute-start.14 = (bf16[3,64,1280]{2,1,0:T(8,128)(2,1)S(1)}, bf16[3,64,1280]{2,1,0:T(8,128)(2,1)S(1)}, u32[]{:S(2)}, u32[]{:S(2)}) collective-permute-start(bf16[3,64,1280]{2,1,0:T(8,128)(2,1)S(1)} %collective-permute-done.13.refs_12_.refs_8_), channel_id=1, source_target_pairs={{0,16},{16,0},{1,17},{17,1},{2,18},{18,2},{3,19},{19,3},{4,20},{20... | collective-permute-start | bytes 1474568 | tf_op jit(solution)/shard_map/ppermute | solution.py:22
  39.9 16.3 %collective-permute-start.17 = (bf16[3,64,1280]{2,1,0:T(8,128)(2,1)S(1)}, bf16[3,64,1280]{2,1,0:T(8,128)(2,1)S(1)}, u32[]{:S(2)}, u32[]{:S(2)}) collective-permute-start(bf16[3,64,1280]{2,1,0:T(8,128)(2,1)S(1)} %collective-permute-done.13.refs_12_.refs_8_), channel_id=1, source_target_pairs={{0,4},{4,0},{1,5},{5,1},{2,6},{6,2},{3,7},{7,3},{8,12},{12,8},{9,1... | collective-permute-start | bytes 1474568 | tf_op jit(solution)/shard_map/ppermute | solution.py:22
  39.9 16.4 %collective-permute-start.16 = (bf16[3,64,1280]{2,1,0:T(8,128)(2,1)S(1)}, bf16[3,64,1280]{2,1,0:T(8,128)(2,1)S(1)}, u32[]{:S(2)}, u32[]{:S(2)}) collective-permute-start(bf16[3,64,1280]{2,1,0:T(8,128)(2,1)S(1)} %collective-permute-done.12.refs_11_.refs_7_), channel_id=1, source_target_pairs={{0,4},{4,0},{1,5},{5,1},{2,6},{6,2},{3,7},{7,3},{8,12},{12,8},{9,1... | collective-permute-start | bytes 1474568 | tf_op jit(solution)/shard_map/ppermute | solution.py:22
  40.9 18.5 %collective-permute-start.4 = (bf16[1280,256]{1,0:T(8,128)(2,1)S(1)}, bf16[1280,256]{1,0:T(8,128)(2,1)}, u32[]{:S(2)}, u32[]{:S(2)}) collective-permute-start(bf16[1280,256]{1,0:T(8,128)(2,1)S(1)} %collective-permute-done.3.refs_6_), channel_id=1, source_target_pairs={{0,1},{1,2},{2,3},{3,0},{4,5},{5,6},{6,7},{7,4},{8,9},{9,10},{10,1... | collective-permute-start | bytes 1966088 | tf_op jit(solution)/shard_map/ppermute | solution.py:22
  55.6 13.0 %collective-permute-start.33 = (bf16[2,256,1280]{2,1,0:T(8,128)(2,1)S(1)}, bf16[2,256,1280]{2,1,0:T(8,128)(2,1)S(1)}, u32[]{:S(2)}, u32[]{:S(2)}) collective-permute-start(bf16[2,256,1280]{2,1,0:T(8,128)(2,1)S(1)} %down_partial.6), channel_id=1, source_target_pairs={{0,4},{4,0},{1,5},{5,1},{2,6},{6,2},{3,7},{7,3},{8,12},{12,8},{9,1... | collective-permute-start | bytes 3932168 | tf_op jit(solution)/shard_map/ppermute | solution.py:22
  56.2 19.2 %collective-permute-start.28 = (bf16[2,256,1280]{2,1,0:T(8,128)(2,1)S(1)}, bf16[2,256,1280]{2,1,0:T(8,128)(2,1)S(1)}, u32[]{:S(2)}, u32[]{:S(2)}) collective-permute-start(bf16[2,256,1280]{2,1,0:T(8,128)(2,1)S(1)} %down_partial.4), channel_id=1, source_target_pairs={{0,4},{4,0},{1,5},{5,1},{2,6},{6,2},{3,7},{7,3},{8,12},{12,8},{9,1... | collective-permute-start | bytes 3932168 | tf_op jit(solution)/shard_map/ppermute | solution.py:22
  56.3 17.5 %collective-permute-start.23 = (bf16[1280,256]{1,0:T(8,128)(2,1)S(1)}, bf16[1280,256]{1,0:T(8,128)(2,1)S(1)}, u32[]{:S(2)}, u32[]{:S(2)}) collective-permute-start(bf16[1280,256]{1,0:T(8,128)(2,1)S(1)} %collective-permute-done.3.refs_6_), channel_id=1, source_target_pairs={{0,16},{16,0},{1,17},{17,1},{2,18},{18,2},{3,19},{19,3},{4,20},{20... | collective-permute-start | bytes 1966088 | tf_op jit(solution)/shard_map/ppermute | solution.py:22
  59.4 21.0 %collective-permute-start.22 = (bf16[1280,256]{1,0:T(8,128)(2,1)S(1)}, bf16[1280,256]{1,0:T(8,128)(2,1)S(1)}, u32[]{:S(2)}, u32[]{:S(2)}) collective-permute-start(bf16[1280,256]{1,0:T(8,128)(2,1)S(1)} %collective-permute-done.3.refs_6_), channel_id=1, source_target_pairs={{0,4},{4,0},{1,5},{5,1},{2,6},{6,2},{3,7},{7,3},{8,12},{12,8},{9,1... | collective-permute-start | bytes 1966088 | tf_op jit(solution)/shard_map/ppermute | solution.py:22
  59.4 28.2 %collective-permute-start.20 = (bf16[1280,256]{1,0:T(8,128)(2,1)}, bf16[1280,256]{1,0:T(8,128)(2,1)}, u32[]{:S(2)}, u32[]{:S(2)}) collective-permute-start(bf16[1280,256]{1,0:T(8,128)(2,1)} %collective-permute-done.4.refs_6_), channel_id=1, source_target_pairs={{0,16},{16,0},{1,17},{17,1},{2,18},{18,2},{3,19},{19,3},{4,20},{20... | collective-permute-start | bytes 1966088 | tf_op jit(solution)/shard_map/ppermute | solution.py:22
  68.6 42.6 %collective-permute-start.19 = (bf16[1280,256]{1,0:T(8,128)(2,1)}, bf16[1280,256]{1,0:T(8,128)(2,1)}, u32[]{:S(2)}, u32[]{:S(2)}) collective-permute-start(bf16[1280,256]{1,0:T(8,128)(2,1)} %collective-permute-done.4.refs_6_), channel_id=1, source_target_pairs={{0,4},{4,0},{1,5},{5,1},{2,6},{6,2},{3,7},{7,3},{8,12},{12,8},{9,1... | collective-permute-start | bytes 1966088 | tf_op jit(solution)/shard_map/ppermute | solution.py:22
  73.9 19.0 %collective-permute-start.5 = (bf16[1280,256]{1,0:T(8,128)(2,1)}, bf16[1280,256]{1,0:T(8,128)(2,1)}, u32[]{:S(2)}, u32[]{:S(2)}) collective-permute-start(bf16[1280,256]{1,0:T(8,128)(2,1)} %collective-permute-done.4.refs_6_), channel_id=1, source_target_pairs={{0,1},{1,2},{2,3},{3,0},{4,5},{5,6},{6,7},{7,4},{8,9},{9,10},{10,1... | collective-permute-start | bytes 1966088 | tf_op jit(solution)/shard_map/ppermute | solution.py:22
  80.3 17.9 %collective-permute-start.30 = (f32[256,1024]{1,0:T(8,128)S(1)}, f32[256,1024]{1,0:T(8,128)S(1)}, u32[]{:S(2)}, u32[]{:S(2)}) collective-permute-start(f32[256,1024]{1,0:T(8,128)S(1)} %get-tuple-element.22), channel_id=1, source_target_pairs={{0,4},{4,0},{1,5},{5,1},{2,6},{6,2},{3,7},{7,3},{8,12},{12,8},{9,1... | collective-permute-start | bytes 3145736 | tf_op jit(solution)/shard_map/ppermute | solution.py:22
  80.9 23.4 %collective-permute-start.29 = (bf16[2,128,1280]{2,1,0:T(8,128)(2,1)}, bf16[2,128,1280]{2,1,0:T(8,128)(2,1)}, u32[]{:S(2)}, u32[]{:S(2)}) collective-permute-start(bf16[2,128,1280]{2,1,0:T(8,128)(2,1)} %get-tuple-element.20), channel_id=1, source_target_pairs={{0,8},{8,0},{1,9},{9,1},{2,10},{10,2},{3,11},{11,3},{4,12},{12,4},... | collective-permute-start | bytes 1966088 | tf_op jit(solution)/shard_map/ppermute | solution.py:22
  87.5 23.7 %collective-permute-start.21 = (bf16[1280,256]{1,0:T(8,128)(2,1)}, bf16[1280,256]{1,0:T(8,128)(2,1)}, u32[]{:S(2)}, u32[]{:S(2)}) collective-permute-start(bf16[1280,256]{1,0:T(8,128)(2,1)} %collective-permute-done.20.refs_8_), channel_id=1, source_target_pairs={{0,4},{4,0},{1,5},{5,1},{2,6},{6,2},{3,7},{7,3},{8,12},{12,8},{9,1... | collective-permute-start | bytes 1966088 | tf_op jit(solution)/shard_map/ppermute | solution.py:22
  92.9 16.4 %collective-permute-start.7 = (bf16[1280,256]{1,0:T(8,128)(2,1)}, bf16[1280,256]{1,0:T(8,128)(2,1)}, u32[]{:S(2)}, u32[]{:S(2)}) collective-permute-start(bf16[1280,256]{1,0:T(8,128)(2,1)} %collective-permute-done.5.refs_6_), channel_id=1, source_target_pairs={{0,16},{16,0},{1,17},{17,1},{2,18},{18,2},{3,19},{19,3},{4,20},{20... | collective-permute-start | bytes 1966088 | tf_op jit(solution)/shard_map/ppermute | solution.py:22
  98.2 29.9 %collective-permute-start.34 = (bf16[2,128,1280]{2,1,0:T(8,128)(2,1)}, bf16[2,128,1280]{2,1,0:T(8,128)(2,1)}, u32[]{:S(2)}, u32[]{:S(2)}) collective-permute-start(bf16[2,128,1280]{2,1,0:T(8,128)(2,1)} %get-tuple-element.26), channel_id=1, source_target_pairs={{0,8},{8,0},{1,9},{9,1},{2,10},{10,2},{3,11},{11,3},{4,12},{12,4},... | collective-permute-start | bytes 1966088 | tf_op jit(solution)/shard_map/ppermute | solution.py:22
  100.8 26.6 %all-to-all-start = ((bf16[8,32,1024]{2,1,0:T(8,128)(2,1)}), bf16[8,32,1024]{2,1,0:T(8,128)(2,1)S(1)}, u32[]{:S(2)}, u32[]{:S(2)}) async-start(bf16[8,32,1024]{2,1,0:T(8,128)(2,1)} %bitcast.24.refs_2_), calls=%async_computation | async-start | bytes 1048576 | tf_op jit(solution)/shard_map/all_to_all | solution.py:441
  104.3 28.1 %collective-permute-start.6 = (bf16[1280,256]{1,0:T(8,128)(2,1)}, bf16[1280,256]{1,0:T(8,128)(2,1)}, u32[]{:S(2)}, u32[]{:S(2)}) collective-permute-start(bf16[1280,256]{1,0:T(8,128)(2,1)} %collective-permute-done.5.refs_6_), channel_id=1, source_target_pairs={{0,4},{4,0},{1,5},{5,1},{2,6},{6,2},{3,7},{7,3},{8,12},{12,8},{9,1... | collective-permute-start | bytes 1966088 | tf_op jit(solution)/shard_map/ppermute | solution.py:22
  109.4 23.0 %collective-permute-start.8 = (bf16[1280,256]{1,0:T(8,128)(2,1)}, bf16[1280,256]{1,0:T(8,128)(2,1)}, u32[]{:S(2)}, u32[]{:S(2)}) collective-permute-start(bf16[1280,256]{1,0:T(8,128)(2,1)} %collective-permute-done.7.refs_8_), channel_id=1, source_target_pairs={{0,4},{4,0},{1,5},{5,1},{2,6},{6,2},{3,7},{7,3},{8,12},{12,8},{9,1... | collective-permute-start | bytes 1966088 | tf_op jit(solution)/shard_map/ppermute | solution.py:22
  111.3 30.6 %collective-permute-start.31 = (bf16[128,1280]{1,0:T(8,128)(2,1)}, bf16[128,1280]{1,0:T(8,128)(2,1)S(1)}, u32[]{:S(2)}, u32[]{:S(2)}) collective-permute-start(bf16[128,1280]{1,0:T(8,128)(2,1)} %get-tuple-element.23.refs_19_), channel_id=1, source_target_pairs={{0,2},{1,3},{2,0},{3,1},{4,6},{5,7},{6,4},{7,5},{8,10},{9,11},{10,... | collective-permute-start | bytes 983048 | tf_op jit(solution)/shard_map/ppermute | solution.py:22
  111.3 30.6 %collective-permute-start.32 = (bf16[128,1280]{1,0:T(8,128)(2,1)S(1)}, bf16[128,1280]{1,0:T(8,128)(2,1)}, u32[]{:S(2)}, u32[]{:S(2)}) collective-permute-start(bf16[128,1280]{1,0:T(8,128)(2,1)S(1)} %get-tuple-element.24), channel_id=1, source_target_pairs={{0,3},{1,0},{2,1},{3,2},{4,7},{5,4},{6,5},{7,6},{8,11},{9,8},{10,9... | collective-permute-start | bytes 983048 | tf_op jit(solution)/shard_map/ppermute | solution.py:22
  129.3 12.6 %collective-permute-start.35 = (bf16[128,1280]{1,0:T(8,128)(2,1)S(1)}, bf16[128,1280]{1,0:T(8,128)(2,1)S(1)}, u32[]{:S(2)}, u32[]{:S(2)}) collective-permute-start(bf16[128,1280]{1,0:T(8,128)(2,1)S(1)} %get-tuple-element.28), channel_id=1, source_target_pairs={{0,1},{1,2},{2,3},{3,0},{4,5},{5,6},{6,7},{7,4},{8,9},{9,10},{10,1... | collective-permute-start | bytes 983048 | tf_op jit(solution)/shard_map/ppermute | solution.py:22
  138.2 13.1 %all-to-all-start.1 = ((bf16[4,32,1024]{2,1,0:T(8,128)(2,1)}), bf16[4,32,1024]{2,1,0:T(8,128)(2,1)S(1)}, u32[]{:S(2)}, u32[]{:S(2)}) async-start(bf16[4,32,1024]{2,1,0:T(8,128)(2,1)} %share.1.refs_2_), calls=%async_computation.1 | async-start | bytes 524288 | tf_op jit(solution)/shard_map/all_to_all | solution.py:443
  (24 other events, 650.6 us)

commit v5 on v4

--- a/solution.py
+++ b/solution.py
@@ -460,7 +460,7 @@
                 places.append(league_back[dy] * c_size + (c - dc) % c_size)
         out = input_call(
             ints((z - s) % z_size, *places, *league_back), low, masked, weights, downs, s - 1, y_size, out, width,
-            later_than=early if s == z_size - 2 else (),
+            later_than=early if s == z_size - 2 else [own_b] if s == 1 else (),
             last=s >= z_size - 2,
         )
     if cols % 128:

time: 153 us -> 168 us (1.098)
  local copies, waits for them, and re-layouts: 5.55 us -> 13.8 us
  waiting for transfers between devices: 46.9 us -> 51.1 us
  starting transfers between devices: 35.3 us -> 39.3 us
  Pallas kernels: 60.1 us -> 58.3 us
    ppermute x36, waiting for transfers between devices: 31.6 us -> 41.6 us  [shift(): lax.ppermute(value, axis, [(i, (i + by) % size) for i in range(size)])]
    unnamed x36 -> x60, local copies, waits for them, and re-layouts: 2.33 us -> 10.6 us
    all_to_all x1, waiting for transfers between devices: 7.87 us -> 0.01 us  [body(): lax.all_to_all(own_b, ('x', 'fsdp'), split_axis=0, concat_axis=0, tiled=T...]
    ppermute x36, starting transfers between devices: 28.2 us -> 30.3 us  [shift(): lax.ppermute(value, axis, [(i, (i + by) % size) for i in range(size)])]
    all_to_all x1, waiting for transfers between devices: 7.44 us -> 9.52 us  [body(): lax.all_to_all(share_b, 'fsdp', split_axis=0, concat_axis=0, tiled=True)]
    pallas_call x15, Pallas kernels: 60.1 us -> 58.3 us  [call(): pl.pallas_call(lambda *refs: kernel(*refs[:count], *refs[count + extra:])...]
  transfers between devices with their start and end apart: 38 -> 38, of which waited for: 11 -> 9; matrix products, arithmetic and copies ran while one was open for 4% -> 3% of each run, Pallas kernels for 40% -> 35%
where the time goes in v5:
time: 168 us; the launch traced here: 167 us
  Pallas kernels  58.3 us (35%)
  waiting for transfers between devices  51.1 us (30%)
  starting transfers between devices  39.3 us (23%)
  local copies, waits for them, and re-layouts  13.8 us (8%)
  other arithmetic  3.33 us (2%)
    pallas_call x15, Pallas kernels, call(): pl.pallas_call(lambda *refs: kernel(*refs[:count], *refs[count + extra:])...  58.3 us
    ppermute x36, waiting for transfers between devices, shift(): lax.ppermute(value, axis, [(i, (i + by) % size) for i in range(size)])  41.6 us
    ppermute x36, starting transfers between devices, shift(): lax.ppermute(value, axis, [(i, (i + by) % size) for i in range(size)])  30.3 us
    unnamed x60, local copies, waits for them, and re-layouts  10.6 us
    all_to_all x1, waiting for transfers between devices, body(): lax.all_to_all(share_b, 'fsdp', split_axis=0, concat_axis=0, tiled=True)  9.52 us
    all_to_all x1, starting transfers between devices, body(): lax.all_to_all(share_b, 'fsdp', split_axis=0, concat_axis=0, tiled=True)  4.54 us
    all_to_all x1, starting transfers between devices, body(): lax.all_to_all(own_b, ('x', 'fsdp'), split_axis=0, concat_axis=0, tiled=T...  4.46 us
  transfers between devices with their start and end apart: 38, of which 9 were waited for; matrix products, arithmetic and copies ran while one was open for 3% of the time, Pallas kernels for 35%

profile of v5, /device:TPU:0, one launch (start us, length us, event | category | flops | bytes accessed | tf_op | source)
XLA Modules:
  0.0 166.9 jit_solution(15380722691309403711)
XLA Ops:
  0.7 3.0 %collective-permute-start = (bf16[128,1024]{1,0:T(8,128)(2,1)}, bf16[128,1024]{1,0:T(8,128)(2,1)S(1)}, u32[]{:S(2)}, u32[]{:S(2)}) collective-permute-start(bf16[128,1024]{1,0:T(8,128)(2,1)} %bitcast.36), channel_id=1, source_target_pairs={{0,8},{8,0},{1,9},{9,1},{2,10},{10,2},{3,11},{11,3},{4,12},{12,4},... | collective-permute-start | bytes 786440 | tf_op jit(solution)/shard_map/ppermute | solution.py:22
  4.6 1.6 collective-permute-start.9
  6.2 2.6 %collective-permute-start.10 = (bf16[64,1280]{1,0:T(8,128)(2,1)S(1)}, bf16[64,1280]{1,0:T(8,128)(2,1)S(1)}, u32[]{:S(2)}, u32[]{:S(2)}) collective-permute-start(bf16[64,1280]{1,0:T(8,128)(2,1)S(1)} %constant_dynamic-slice_fusion), channel_id=1, source_target_pairs={{0,2},{1,3},{2,0},{3,1},{4,6},{5,7},{6,4},{7,5},{8,10},{9,11},{10,... | collective-permute-start | bytes 491528 | tf_op jit(solution)/shard_map/ppermute | solution.py:22
  10.3 2.0 %constant_dynamic-slice_fusion.1 = bf16[1280,256]{1,0:T(8,128)(2,1)} fusion(bf16[1280,1024]{1,0:T(8,128)(2,1)} %refs_3_.4, s32[]{:T(128)S(6)} %select_n.112), kind=kLoop, calls=%fused_computation.10 | loop fusion | bytes 1310724 | tf_op jit(solution)/shard_map/dynamic_slice | solution.py:453
  14.4 5.8 %collective-permute-done.10 = bf16[64,1280]{1,0:T(8,128)(2,1)S(1)} collective-permute-done((bf16[64,1280]{1,0:T(8,128)(2,1)S(1)}, bf16[64,1280]{1,0:T(8,128)(2,1)S(1)}, u32[]{:S(2)}, u32[]{:S(2)}) %collective-permute-start.10) | collective-permute-done | bytes 163872 | tf_op jit(solution)/shard_map/ppermute | solution.py:22
  20.2 4.0 %collective-permute-start.3 = (bf16[1280,256]{1,0:T(8,128)(2,1)}, bf16[1280,256]{1,0:T(8,128)(2,1)}, u32[]{:S(2)}, u32[]{:S(2)}) collective-permute-start(bf16[1280,256]{1,0:T(8,128)(2,1)} %constant_dynamic-slice_fusion.1), channel_id=1, source_target_pairs={{0,1},{1,2},{2,3},{3,0},{4,5},{5,6},{6,7},{7,4},{8,9},{9,10},{10,1... | collective-permute-start | bytes 1966088 | tf_op jit(solution)/shard_map/ppermute | solution.py:22
  24.9 1.5 collective-permute-start.12
  26.5 4.2 %low_rank.1 = (bf16[512,1024]{1,0:T(8,128)(2,1)S(1)}, bf16[512,512]{1,0:T(8,128)(2,1)S(1)}, bf16[512,512]{1,0:T(8,128)(2,1)S(1)}) custom-call(s32[4]{0:T(128)S(1)} %pad_add_fusion.refs_0_.refs_1_, s32[4]{0:T(128)S(1)} %copy-done.21, s32[4]{0:T(128)S(1)} %copy-done.20, bf16[512,1024]{1,0:T(8,128)(2,1)} %refs_3_.3, bf16[128,1024]{1,0:T(8,128)(2,1)S(1)} %bitcast.38, ...), custom_call_target="tpu_custom_call" | custom-call | flops 10737418240 | bytes 41943040 | tf_op jit(solution)/shard_map/low_rank/pallas_call | solution.py:66
  30.7 4.0 %down_partial.6 = bf16[2,256,1280]{2,1,0:T(8,128)(2,1)S(1)} custom-call(s32[2]{0:T(128)S(1)} %pad_add_fusion.5.refs_0_, bf16[512,512]{1,0:T(8,128)(2,1)S(1)} %get-tuple-element.20.refs_1_, bf16[512,5120]{1,0:T(8,128)(2,1)} %refs_2_.11), custom_call_target="tpu_custom_call" | custom-call | flops 13421772800 | bytes 115343360 | tf_op jit(solution)/shard_map/down_partial/pallas_call | solution.py:66
  34.8 4.0 %down_partial.4 = bf16[2,256,1280]{2,1,0:T(8,128)(2,1)S(1)} custom-call(s32[2]{0:T(128)S(1)} %pad_add_fusion.4.refs_0_, bf16[512,512]{1,0:T(8,128)(2,1)S(1)} %get-tuple-element.20.refs_1_, bf16[512,5120]{1,0:T(8,128)(2,1)} %refs_2_.11), custom_call_target="tpu_custom_call" | custom-call | flops 13421772800 | bytes 115343360 | tf_op jit(solution)/shard_map/down_partial/pallas_call | solution.py:66
  42.0 5.5 %input_cotangent.4.refs_18_ = bf16[512,5120]{1,0:T(8,128)(2,1)} custom-call(s32[2]{0:T(128)S(1)} %pad_add_fusion.1.refs_0_, bf16[512,512]{1,0:T(8,128)(2,1)S(1)} %get-tuple-element.16.refs_1_, bf16[512,1024]{1,0:T(8,128)(2,1)S(1)} %get-tuple-element.17.refs_2_.refs_5_.refs_3_.refs_4_, bf16[1280,1024]{1,0:T(8,128)(2,1)} %refs_3_.4, ...), custom_call_target="tpu_custom_call" | custom-call | flops 40265318400 | bytes 110100480 | tf_op jit(solution)/shard_map/input_cotangent/pallas_call | solution.py:66
  47.5 5.1 %collective-permute-done.14.refs_9_.refs_13_ = bf16[3,64,1280]{2,1,0:T(8,128)(2,1)S(1)} collective-permute-done((bf16[3,64,1280]{2,1,0:T(8,128)(2,1)S(1)}, bf16[3,64,1280]{2,1,0:T(8,128)(2,1)S(1)}, u32[]{:S(2)}, u32[]{:S(2)}) %collective-permute-start.14) | collective-permute-done | bytes 491552 | tf_op jit(solution)/shard_map/ppermute | solution.py:22
  52.6 3.0 %projected_own.1.refs_4_ = f32[512,512]{1,0:T(8,128)S(1)} custom-call(s32[4]{0:T(128)S(1)} %pad_add_fusion.3.refs_0_, bf16[512,5120]{1,0:T(8,128)(2,1)} %refs_2_.11, bf16[128,1280]{1,0:T(8,128)(2,1)S(1)} %bitcast.35, bf16[128,1280]{1,0:T(8,128)(2,1)S(1)} %collective-permute-done.25.refs_5_.refs_3_, ...), custom_call_target="tpu_custom_call" | custom-call | flops 13421772800 | bytes 131072000 | tf_op jit(solution)/shard_map/projected_own/pallas_call | solution.py:66
  56.9 2.8 %collective-permute-done.4.refs_6_ = bf16[1280,256]{1,0:T(8,128)(2,1)} collective-permute-done((bf16[1280,256]{1,0:T(8,128)(2,1)}, bf16[1280,256]{1,0:T(8,128)(2,1)}, u32[]{:S(2)}, u32[]{:S(2)}) %collective-permute-start.4) | collective-permute-done | bytes 655392 | tf_op jit(solution)/shard_map/ppermute | solution.py:22
  59.7 1.6 collective-permute-start.20
  61.3 7.7 %projected.1 = (f32[256,1024]{1,0:T(8,128)S(1)}, f32[256,1024]{1,0:T(8,128)S(1)}) custom-call(s32[5]{0:T(128)S(1)} %concatenate.5.refs_0_, s32[4]{0:T(128)S(1)} %pad_add_fusion.refs_0_.refs_1_, s32[4]{0:T(128)S(1)} %copy-done.21, bf16[512,5120]{1,0:T(8,128)(2,1)} %refs_2_.11, f32[512,512]{1,0:T(8,128)S(1)} %projected_own.1.refs_4_, ...), custom_call_target="tpu_custom_call" | custom-call | flops 51002736640 | bytes 225443840 | tf_op jit(solution)/shard_map/projected/pallas_call | solution.py:66
  69.0 5.2 %collective-permute-done.23.refs_8_ = bf16[1280,256]{1,0:T(8,128)(2,1)} collective-permute-done((bf16[1280,256]{1,0:T(8,128)(2,1)}, bf16[1280,256]{1,0:T(8,128)(2,1)}, u32[]{:S(2)}, u32[]{:S(2)}) %collective-permute-start.23) | collective-permute-done | bytes 655392 | tf_op jit(solution)/shard_map/ppermute | solution.py:22
  74.2 1.6 collective-permute-start.5
  75.8 4.1 %down_partial.7 = (f32[2,128,1280]{2,1,0:T(8,128)S(1)}, bf16[2,128,1280]{2,1,0:T(8,128)(2,1)S(1)}) custom-call(s32[2]{0:T(128)S(1)} %pad_add_fusion.5.refs_0_, bf16[512,512]{1,0:T(8,128)(2,1)S(1)} %get-tuple-element.20.refs_1_, bf16[512,5120]{1,0:T(8,128)(2,1)} %refs_2_.11, bf16[2,256,1280]{2,1,0:T(8,128)(2,1)S(1)} %collective-permute-done.33.refs_3_), custom_call_target="tpu_custom_call" | custom-call | flops 13421772800 | bytes 141557760 | tf_op jit(solution)/shard_map/down_partial/pallas_call | solution.py:66
  80.5 4.1 %down_partial.5 = (f32[2,128,1280]{2,1,0:T(8,128)S(1)}, bf16[2,128,1280]{2,1,0:T(8,128)(2,1)S(1)}) custom-call(s32[2]{0:T(128)S(1)} %pad_add_fusion.4.refs_0_, bf16[512,512]{1,0:T(8,128)(2,1)S(1)} %get-tuple-element.20.refs_1_, bf16[512,5120]{1,0:T(8,128)(2,1)} %refs_2_.11, bf16[2,256,1280]{2,1,0:T(8,128)(2,1)S(1)} %collective-permute-done.29.refs_3_), custom_call_target="tpu_custom_call" | custom-call | flops 13421772800 | bytes 141557760 | tf_op jit(solution)/shard_map/down_partial/pallas_call | solution.py:66
  86.1 4.5 %all-to-all-start = ((bf16[8,32,1024]{2,1,0:T(8,128)(2,1)}), bf16[8,32,1024]{2,1,0:T(8,128)(2,1)S(1)}, u32[]{:S(2)}, u32[]{:S(2)}) async-start(bf16[8,32,1024]{2,1,0:T(8,128)(2,1)} %bitcast.22.refs_19_.refs_2_), calls=%async_computation | async-start | bytes 1048576 | tf_op jit(solution)/shard_map/all_to_all | solution.py:441
  90.6 2.0 %collective-permute-start.34 = (bf16[2,128,1280]{2,1,0:T(8,128)(2,1)}, bf16[2,128,1280]{2,1,0:T(8,128)(2,1)}, u32[]{:S(2)}, u32[]{:S(2)}) collective-permute-start(bf16[2,128,1280]{2,1,0:T(8,128)(2,1)} %copy-done.3), channel_id=1, source_target_pairs={{0,8},{8,0},{1,9},{9,1},{2,10},{10,2},{3,11},{11,3},{4,12},{12,4},... | collective-permute-start | bytes 1966088 | tf_op jit(solution)/shard_map/ppermute | solution.py:22
  103.8 5.6 %input_cotangent.5.refs_18_ = bf16[512,5120]{1,0:T(8,128)(2,1)} custom-call(s32[7]{0:T(128)S(1)} %stack.137.refs_0_, bf16[512,512]{1,0:T(8,128)(2,1)S(1)} %copy-done.27, bf16[512,1024]{1,0:T(8,128)(2,1)S(1)} %copy-done.23, bf16[512,1024]{1,0:T(8,128)(2,1)S(1)} %copy-done.23, bf16[512,1024]{1,0:T(8,128)(2,1)S(1)} %copy-done.23, ...), custom_call_target="tpu_custom_call", output_to_operand_aliasing={{}: (18, {})} | custom-call | flops 40265318400 | bytes 330301440 | tf_op jit(solution)/shard_map/input_cotangent/pallas_call | solution.py:66
  109.5 17.9 %collective-permute-done.30.refs_1_ = bf16[2,128,1280]{2,1,0:T(8,128)(2,1)S(1)} collective-permute-done((bf16[2,128,1280]{2,1,0:T(8,128)(2,1)}, bf16[2,128,1280]{2,1,0:T(8,128)(2,1)S(1)}, u32[]{:S(2)}, u32[]{:S(2)}) %collective-permute-start.30) | collective-permute-done | bytes 655392 | tf_op jit(solution)/shard_map/ppermute | solution.py:22
  128.7 2.4 %collective-permute-start.31 = (bf16[128,1280]{1,0:T(8,128)(2,1)}, bf16[128,1280]{1,0:T(8,128)(2,1)S(1)}, u32[]{:S(2)}, u32[]{:S(2)}) collective-permute-start(bf16[128,1280]{1,0:T(8,128)(2,1)} %get-tuple-element.23.refs_19_), channel_id=1, source_target_pairs={{0,2},{1,3},{2,0},{3,1},{4,6},{5,7},{6,4},{7,5},{8,10},{9,11},{10,... | collective-permute-start | bytes 983048 | tf_op jit(solution)/shard_map/ppermute | solution.py:22
  131.0 1.5 collective-permute-start.32
  132.5 5.8 %input_cotangent.6.refs_18_ = bf16[512,5120]{1,0:T(8,128)(2,1)} custom-call(s32[7]{0:T(128)S(1)} %stack.135.refs_0_, bf16[512,512]{1,0:T(8,128)(2,1)S(1)} %copy-done.28, bf16[512,1024]{1,0:T(8,128)(2,1)S(1)} %copy-done.24, bf16[512,1024]{1,0:T(8,128)(2,1)S(1)} %copy-done.24, bf16[512,1024]{1,0:T(8,128)(2,1)S(1)} %copy-done.24, ...), custom_call_target="tpu_custom_call", output_to_operand_aliasing={{}: (18, {})} | custom-call | flops 40265318400 | bytes 330301440 | tf_op jit(solution)/shard_map/input_cotangent/pallas_call | solution.py:66
  141.0 5.9 %input_cotangent.7 = bf16[512,5120]{1,0:T(8,128)(2,1)} custom-call(s32[7]{0:T(128)S(1)} %stack.124.refs_0_, bf16[512,512]{1,0:T(8,128)(2,1)S(1)} %copy-done.29, bf16[512,1024]{1,0:T(8,128)(2,1)S(1)} %copy-done.25, bf16[512,1024]{1,0:T(8,128)(2,1)S(1)} %copy-done.25, bf16[512,1024]{1,0:T(8,128)(2,1)S(1)} %copy-done.25, ...), custom_call_target="tpu_custom_call", output_to_operand_aliasing={{}: (18, {})} | custom-call | flops 40265318400 | bytes 330301440 | tf_op jit(solution)/shard_map/input_cotangent/pallas_call | solution.py:66
  146.9 4.5 %all-to-all-start.1 = ((bf16[4,32,1024]{2,1,0:T(8,128)(2,1)}), bf16[4,32,1024]{2,1,0:T(8,128)(2,1)S(1)}, u32[]{:S(2)}, u32[]{:S(2)}) async-start(bf16[4,32,1024]{2,1,0:T(8,128)(2,1)} %share.1.refs_2_), calls=%async_computation.1 | async-start | bytes 524288 | tf_op jit(solution)/shard_map/all_to_all | solution.py:443
  151.4 3.1 %collective-permute-done.35 = bf16[128,1280]{1,0:T(8,128)(2,1)S(1)} collective-permute-done((bf16[128,1280]{1,0:T(8,128)(2,1)S(1)}, bf16[128,1280]{1,0:T(8,128)(2,1)S(1)}, u32[]{:S(2)}, u32[]{:S(2)}) %collective-permute-start.35) | collective-permute-done | bytes 327712 | tf_op jit(solution)/shard_map/ppermute | solution.py:22
  154.6 2.0 %add_multiply_fusion = f32[128,1280]{1,0:T(8,128)} fusion(bf16[128,1280]{1,0:T(8,128)(2,1)S(1)} %collective-permute-done.35, f32[128,1280]{1,0:T(8,128)S(1)} %get-tuple-element.27, bf16[128,1280]{1,0:T(8,128)(2,1)} %collective-permute-done.32, bf16[128,1280]{1,0:T(8,128)(2,1)S(1)} %collective-permute-done.31), kind=kLoop, calls=%fused_computation | loop fusion | flops 1146880 | bytes 2293760 | tf_op jit(solution)/shard_map/mul | solution.py:450
  156.6 9.5 %all-to-all-done.1 = bf16[4,32,1024]{2,1,0:T(8,128)(2,1)S(1)} async-done(((bf16[4,32,1024]{2,1,0:T(8,128)(2,1)}), bf16[4,32,1024]{2,1,0:T(8,128)(2,1)S(1)}, u32[]{:S(2)}, u32[]{:S(2)}) %all-to-all-start.1) | async-done | bytes 262176 | tf_op jit(solution)/shard_map/all_to_all | solution.py:443
  (134 shorter events, 27.7 us)
Async XLA Ops:
  0.7 13.3 %collective-permute-start = (bf16[128,1024]{1,0:T(8,128)(2,1)}, bf16[128,1024]{1,0:T(8,128)(2,1)S(1)}, u32[]{:S(2)}, u32[]{:S(2)}) collective-permute-start(bf16[128,1024]{1,0:T(8,128)(2,1)} %bitcast.36), channel_id=1, source_target_pairs={{0,8},{8,0},{1,9},{9,1},{2,10},{10,2},{3,11},{11,3},{4,12},{12,4},... | collective-permute-start | bytes 786440 | tf_op jit(solution)/shard_map/ppermute | solution.py:22
  3.7 20.6 %collective-permute-start.1 = (bf16[128,1024]{1,0:T(8,128)(2,1)}, bf16[128,1024]{1,0:T(8,128)(2,1)S(1)}, u32[]{:S(2)}, u32[]{:S(2)}) collective-permute-start(bf16[128,1024]{1,0:T(8,128)(2,1)} %bitcast.37), channel_id=1, source_target_pairs={{0,4},{4,0},{1,5},{5,1},{2,6},{6,2},{3,7},{7,3},{8,12},{12,8},{9,1... | collective-permute-start | bytes 786440 | tf_op jit(solution)/shard_map/ppermute | solution.py:22
  6.2 14.0 %collective-permute-start.10 = (bf16[64,1280]{1,0:T(8,128)(2,1)S(1)}, bf16[64,1280]{1,0:T(8,128)(2,1)S(1)}, u32[]{:S(2)}, u32[]{:S(2)}) collective-permute-start(bf16[64,1280]{1,0:T(8,128)(2,1)S(1)} %constant_dynamic-slice_fusion), channel_id=1, source_target_pairs={{0,2},{1,3},{2,0},{3,1},{4,6},{5,7},{6,4},{7,5},{8,10},{9,11},{10,... | collective-permute-start | bytes 491528 | tf_op jit(solution)/shard_map/ppermute | solution.py:22
  20.2 18.6 %collective-permute-start.26 = (bf16[128,1280]{1,0:T(8,128)(2,1)}, bf16[128,1280]{1,0:T(8,128)(2,1)S(1)}, u32[]{:S(2)}, u32[]{:S(2)}) collective-permute-start(bf16[128,1280]{1,0:T(8,128)(2,1)} %bitcast.33), channel_id=1, source_target_pairs={{0,4},{4,0},{1,5},{5,1},{2,6},{6,2},{3,7},{7,3},{8,12},{12,8},{9,1... | collective-permute-start | bytes 983048 | tf_op jit(solution)/shard_map/ppermute | solution.py:22
  20.2 20.8 %collective-permute-start.3 = (bf16[1280,256]{1,0:T(8,128)(2,1)}, bf16[1280,256]{1,0:T(8,128)(2,1)}, u32[]{:S(2)}, u32[]{:S(2)}) collective-permute-start(bf16[1280,256]{1,0:T(8,128)(2,1)} %constant_dynamic-slice_fusion.1), channel_id=1, source_target_pairs={{0,1},{1,2},{2,3},{3,0},{4,5},{5,6},{6,7},{7,4},{8,9},{9,10},{10,1... | collective-permute-start | bytes 1966088 | tf_op jit(solution)/shard_map/ppermute | solution.py:22
  24.3 15.1 %collective-permute-start.13 = (bf16[3,64,1280]{2,1,0:T(8,128)(2,1)S(1)}, bf16[3,64,1280]{2,1,0:T(8,128)(2,1)S(1)}, u32[]{:S(2)}, u32[]{:S(2)}) collective-permute-start(bf16[3,64,1280]{2,1,0:T(8,128)(2,1)S(1)} %pad_maximum_fusion.refs_6_.refs_10_), channel_id=1, source_target_pairs={{0,8},{8,0},{1,9},{9,1},{2,10},{10,2},{3,11},{11,3},{4,12},{12,4},... | collective-permute-start | bytes 1474568 | tf_op jit(solution)/shard_map/ppermute | solution.py:22
  24.9 15.0 %collective-permute-start.12 = (bf16[3,64,1280]{2,1,0:T(8,128)(2,1)S(1)}, bf16[3,64,1280]{2,1,0:T(8,128)(2,1)S(1)}, u32[]{:S(2)}, u32[]{:S(2)}) collective-permute-start(bf16[3,64,1280]{2,1,0:T(8,128)(2,1)S(1)} %pad_maximum_fusion.refs_6_.refs_10_), channel_id=1, source_target_pairs={{0,16},{16,0},{1,17},{17,1},{2,18},{18,2},{3,19},{19,3},{4,20},{20... | collective-permute-start | bytes 1474568 | tf_op jit(solution)/shard_map/ppermute | solution.py:22
  26.4 13.5 %collective-permute-start.27 = (bf16[128,1280]{1,0:T(8,128)(2,1)S(1)}, bf16[128,1280]{1,0:T(8,128)(2,1)S(1)}, u32[]{:S(2)}, u32[]{:S(2)}) collective-permute-start(bf16[128,1280]{1,0:T(8,128)(2,1)S(1)} %collective-permute-done.25.refs_5_.refs_3_), channel_id=1, source_target_pairs={{0,4},{4,0},{1,5},{5,1},{2,6},{6,2},{3,7},{7,3},{8,12},{12,8},{9,1... | collective-permute-start | bytes 983048 | tf_op jit(solution)/shard_map/ppermute | solution.py:22
  38.8 16.8 %collective-permute-start.15 = (bf16[3,64,1280]{2,1,0:T(8,128)(2,1)S(1)}, bf16[3,64,1280]{2,1,0:T(8,128)(2,1)S(1)}, u32[]{:S(2)}, u32[]{:S(2)}) collective-permute-start(bf16[3,64,1280]{2,1,0:T(8,128)(2,1)S(1)} %pad_maximum_fusion.refs_6_.refs_10_), channel_id=1, source_target_pairs={{0,4},{4,0},{1,5},{5,1},{2,6},{6,2},{3,7},{7,3},{8,12},{12,8},{9,1... | collective-permute-start | bytes 1474568 | tf_op jit(solution)/shard_map/ppermute | solution.py:22
  39.4 13.2 %collective-permute-start.14 = (bf16[3,64,1280]{2,1,0:T(8,128)(2,1)S(1)}, bf16[3,64,1280]{2,1,0:T(8,128)(2,1)S(1)}, u32[]{:S(2)}, u32[]{:S(2)}) collective-permute-start(bf16[3,64,1280]{2,1,0:T(8,128)(2,1)S(1)} %collective-permute-done.13.refs_8_.refs_12_), channel_id=1, source_target_pairs={{0,16},{16,0},{1,17},{17,1},{2,18},{18,2},{3,19},{19,3},{4,20},{20... | collective-permute-start | bytes 1474568 | tf_op jit(solution)/shard_map/ppermute | solution.py:22
  39.9 16.3 %collective-permute-start.17 = (bf16[3,64,1280]{2,1,0:T(8,128)(2,1)S(1)}, bf16[3,64,1280]{2,1,0:T(8,128)(2,1)S(1)}, u32[]{:S(2)}, u32[]{:S(2)}) collective-permute-start(bf16[3,64,1280]{2,1,0:T(8,128)(2,1)S(1)} %collective-permute-done.13.refs_8_.refs_12_), channel_id=1, source_target_pairs={{0,4},{4,0},{1,5},{5,1},{2,6},{6,2},{3,7},{7,3},{8,12},{12,8},{9,1... | collective-permute-start | bytes 1474568 | tf_op jit(solution)/shard_map/ppermute | solution.py:22
  39.9 16.4 %collective-permute-start.16 = (bf16[3,64,1280]{2,1,0:T(8,128)(2,1)S(1)}, bf16[3,64,1280]{2,1,0:T(8,128)(2,1)S(1)}, u32[]{:S(2)}, u32[]{:S(2)}) collective-permute-start(bf16[3,64,1280]{2,1,0:T(8,128)(2,1)S(1)} %collective-permute-done.12.refs_7_.refs_11_), channel_id=1, source_target_pairs={{0,4},{4,0},{1,5},{5,1},{2,6},{6,2},{3,7},{7,3},{8,12},{12,8},{9,1... | collective-permute-start | bytes 1474568 | tf_op jit(solution)/shard_map/ppermute | solution.py:22
  41.0 18.7 %collective-permute-start.4 = (bf16[1280,256]{1,0:T(8,128)(2,1)}, bf16[1280,256]{1,0:T(8,128)(2,1)}, u32[]{:S(2)}, u32[]{:S(2)}) collective-permute-start(bf16[1280,256]{1,0:T(8,128)(2,1)} %collective-permute-done.3.refs_6_), channel_id=1, source_target_pairs={{0,1},{1,2},{2,3},{3,0},{4,5},{5,6},{6,7},{7,4},{8,9},{9,10},{10,1... | collective-permute-start | bytes 1966088 | tf_op jit(solution)/shard_map/ppermute | solution.py:22
  55.7 20.1 %collective-permute-start.33 = (bf16[2,256,1280]{2,1,0:T(8,128)(2,1)S(1)}, bf16[2,256,1280]{2,1,0:T(8,128)(2,1)S(1)}, u32[]{:S(2)}, u32[]{:S(2)}) collective-permute-start(bf16[2,256,1280]{2,1,0:T(8,128)(2,1)S(1)} %down_partial.6), channel_id=1, source_target_pairs={{0,4},{4,0},{1,5},{5,1},{2,6},{6,2},{3,7},{7,3},{8,12},{12,8},{9,1... | collective-permute-start | bytes 3932168 | tf_op jit(solution)/shard_map/ppermute | solution.py:22
  56.2 23.7 %collective-permute-start.29 = (bf16[2,256,1280]{2,1,0:T(8,128)(2,1)S(1)}, bf16[2,256,1280]{2,1,0:T(8,128)(2,1)S(1)}, u32[]{:S(2)}, u32[]{:S(2)}) collective-permute-start(bf16[2,256,1280]{2,1,0:T(8,128)(2,1)S(1)} %down_partial.4), channel_id=1, source_target_pairs={{0,4},{4,0},{1,5},{5,1},{2,6},{6,2},{3,7},{7,3},{8,12},{12,8},{9,1... | collective-permute-start | bytes 3932168 | tf_op jit(solution)/shard_map/ppermute | solution.py:22
  56.3 17.9 %collective-permute-start.23 = (bf16[1280,256]{1,0:T(8,128)(2,1)}, bf16[1280,256]{1,0:T(8,128)(2,1)}, u32[]{:S(2)}, u32[]{:S(2)}) collective-permute-start(bf16[1280,256]{1,0:T(8,128)(2,1)} %collective-permute-done.3.refs_6_), channel_id=1, source_target_pairs={{0,16},{16,0},{1,17},{17,1},{2,18},{18,2},{3,19},{19,3},{4,20},{20... | collective-permute-start | bytes 1966088 | tf_op jit(solution)/shard_map/ppermute | solution.py:22
  59.7 30.9 %collective-permute-start.22 = (bf16[1280,256]{1,0:T(8,128)(2,1)}, bf16[1280,256]{1,0:T(8,128)(2,1)}, u32[]{:S(2)}, u32[]{:S(2)}) collective-permute-start(bf16[1280,256]{1,0:T(8,128)(2,1)} %collective-permute-done.3.refs_6_), channel_id=1, source_target_pairs={{0,4},{4,0},{1,5},{5,1},{2,6},{6,2},{3,7},{7,3},{8,12},{12,8},{9,1... | collective-permute-start | bytes 1966088 | tf_op jit(solution)/shard_map/ppermute | solution.py:22
  59.7 33.0 %collective-permute-start.20 = (bf16[1280,256]{1,0:T(8,128)(2,1)}, bf16[1280,256]{1,0:T(8,128)(2,1)}, u32[]{:S(2)}, u32[]{:S(2)}) collective-permute-start(bf16[1280,256]{1,0:T(8,128)(2,1)} %collective-permute-done.4.refs_6_), channel_id=1, source_target_pairs={{0,16},{16,0},{1,17},{17,1},{2,18},{18,2},{3,19},{19,3},{4,20},{20... | collective-permute-start | bytes 1966088 | tf_op jit(solution)/shard_map/ppermute | solution.py:22
  74.2 18.5 %collective-permute-start.5 = (bf16[1280,256]{1,0:T(8,128)(2,1)}, bf16[1280,256]{1,0:T(8,128)(2,1)}, u32[]{:S(2)}, u32[]{:S(2)}) collective-permute-start(bf16[1280,256]{1,0:T(8,128)(2,1)} %collective-permute-done.4.refs_6_), channel_id=1, source_target_pairs={{0,1},{1,2},{2,3},{3,0},{4,5},{5,6},{6,7},{7,4},{8,9},{9,10},{10,1... | collective-permute-start | bytes 1966088 | tf_op jit(solution)/shard_map/ppermute | solution.py:22
  75.8 16.9 %collective-permute-start.24 = (bf16[1280,256]{1,0:T(8,128)(2,1)}, bf16[1280,256]{1,0:T(8,128)(2,1)}, u32[]{:S(2)}, u32[]{:S(2)}) collective-permute-start(bf16[1280,256]{1,0:T(8,128)(2,1)} %collective-permute-done.23.refs_8_), channel_id=1, source_target_pairs={{0,4},{4,0},{1,5},{5,1},{2,6},{6,2},{3,7},{7,3},{8,12},{12,8},{9,1... | collective-permute-start | bytes 1966088 | tf_op jit(solution)/shard_map/ppermute | solution.py:22
  84.7 44.0 %collective-permute-start.19 = (bf16[1280,256]{1,0:T(8,128)(2,1)}, bf16[1280,256]{1,0:T(8,128)(2,1)}, u32[]{:S(2)}, u32[]{:S(2)}) collective-permute-start(bf16[1280,256]{1,0:T(8,128)(2,1)} %collective-permute-done.4.refs_6_), channel_id=1, source_target_pairs={{0,4},{4,0},{1,5},{5,1},{2,6},{6,2},{3,7},{7,3},{8,12},{12,8},{9,1... | collective-permute-start | bytes 1966088 | tf_op jit(solution)/shard_map/ppermute | solution.py:22
  86.1 52.2 %all-to-all-start = ((bf16[8,32,1024]{2,1,0:T(8,128)(2,1)}), bf16[8,32,1024]{2,1,0:T(8,128)(2,1)S(1)}, u32[]{:S(2)}, u32[]{:S(2)}) async-start(bf16[8,32,1024]{2,1,0:T(8,128)(2,1)} %bitcast.22.refs_19_.refs_2_), calls=%async_computation | async-start | bytes 1048576 | tf_op jit(solution)/shard_map/all_to_all | solution.py:441
  90.6 48.5 %collective-permute-start.34 = (bf16[2,128,1280]{2,1,0:T(8,128)(2,1)}, bf16[2,128,1280]{2,1,0:T(8,128)(2,1)}, u32[]{:S(2)}, u32[]{:S(2)}) collective-permute-start(bf16[2,128,1280]{2,1,0:T(8,128)(2,1)} %copy-done.3), channel_id=1, source_target_pairs={{0,8},{8,0},{1,9},{9,1},{2,10},{10,2},{3,11},{11,3},{4,12},{12,4},... | collective-permute-start | bytes 1966088 | tf_op jit(solution)/shard_map/ppermute | solution.py:22
  92.6 34.7 %collective-permute-start.30 = (bf16[2,128,1280]{2,1,0:T(8,128)(2,1)}, bf16[2,128,1280]{2,1,0:T(8,128)(2,1)S(1)}, u32[]{:S(2)}, u32[]{:S(2)}) collective-permute-start(bf16[2,128,1280]{2,1,0:T(8,128)(2,1)} %copy-done.4), channel_id=1, source_target_pairs={{0,8},{8,0},{1,9},{9,1},{2,10},{10,2},{3,11},{11,3},{4,12},{12,4},... | collective-permute-start | bytes 1966088 | tf_op jit(solution)/shard_map/ppermute | solution.py:22
  92.7 38.3 %collective-permute-start.21 = (bf16[1280,256]{1,0:T(8,128)(2,1)}, bf16[1280,256]{1,0:T(8,128)(2,1)S(1)}, u32[]{:S(2)}, u32[]{:S(2)}) collective-permute-start(bf16[1280,256]{1,0:T(8,128)(2,1)} %collective-permute-done.20.refs_8_), channel_id=1, source_target_pairs={{0,4},{4,0},{1,5},{5,1},{2,6},{6,2},{3,7},{7,3},{8,12},{12,8},{9,1... | collective-permute-start | bytes 1966088 | tf_op jit(solution)/shard_map/ppermute | solution.py:22
  92.7 34.6 %collective-permute-start.7 = (bf16[1280,256]{1,0:T(8,128)(2,1)}, bf16[1280,256]{1,0:T(8,128)(2,1)}, u32[]{:S(2)}, u32[]{:S(2)}) collective-permute-start(bf16[1280,256]{1,0:T(8,128)(2,1)} %collective-permute-done.5.refs_6_), channel_id=1, source_target_pairs={{0,16},{16,0},{1,17},{17,1},{2,18},{18,2},{3,19},{19,3},{4,20},{20... | collective-permute-start | bytes 1966088 | tf_op jit(solution)/shard_map/ppermute | solution.py:22
  127.3 13.7 %collective-permute-start.6 = (bf16[1280,256]{1,0:T(8,128)(2,1)}, bf16[1280,256]{1,0:T(8,128)(2,1)}, u32[]{:S(2)}, u32[]{:S(2)}) collective-permute-start(bf16[1280,256]{1,0:T(8,128)(2,1)} %collective-permute-done.5.refs_6_), channel_id=1, source_target_pairs={{0,4},{4,0},{1,5},{5,1},{2,6},{6,2},{3,7},{7,3},{8,12},{12,8},{9,1... | collective-permute-start | bytes 1966088 | tf_op jit(solution)/shard_map/ppermute | solution.py:22
  127.3 13.7 %collective-permute-start.8 = (bf16[1280,256]{1,0:T(8,128)(2,1)}, bf16[1280,256]{1,0:T(8,128)(2,1)}, u32[]{:S(2)}, u32[]{:S(2)}) collective-permute-start(bf16[1280,256]{1,0:T(8,128)(2,1)} %collective-permute-done.7.refs_8_), channel_id=1, source_target_pairs={{0,4},{4,0},{1,5},{5,1},{2,6},{6,2},{3,7},{7,3},{8,12},{12,8},{9,1... | collective-permute-start | bytes 1966088 | tf_op jit(solution)/shard_map/ppermute | solution.py:22
  128.7 22.8 %collective-permute-start.31 = (bf16[128,1280]{1,0:T(8,128)(2,1)}, bf16[128,1280]{1,0:T(8,128)(2,1)S(1)}, u32[]{:S(2)}, u32[]{:S(2)}) collective-permute-start(bf16[128,1280]{1,0:T(8,128)(2,1)} %get-tuple-element.23.refs_19_), channel_id=1, source_target_pairs={{0,2},{1,3},{2,0},{3,1},{4,6},{5,7},{6,4},{7,5},{8,10},{9,11},{10,... | collective-permute-start | bytes 983048 | tf_op jit(solution)/shard_map/ppermute | solution.py:22
  131.0 20.4 %collective-permute-start.32 = (bf16[128,1280]{1,0:T(8,128)(2,1)S(1)}, bf16[128,1280]{1,0:T(8,128)(2,1)}, u32[]{:S(2)}, u32[]{:S(2)}) collective-permute-start(bf16[128,1280]{1,0:T(8,128)(2,1)S(1)} %get-tuple-element.24), channel_id=1, source_target_pairs={{0,3},{1,0},{2,1},{3,2},{4,7},{5,4},{6,5},{7,6},{8,11},{9,8},{10,9... | collective-permute-start | bytes 983048 | tf_op jit(solution)/shard_map/ppermute | solution.py:22
  140.4 14.2 %collective-permute-start.35 = (bf16[128,1280]{1,0:T(8,128)(2,1)S(1)}, bf16[128,1280]{1,0:T(8,128)(2,1)S(1)}, u32[]{:S(2)}, u32[]{:S(2)}) collective-permute-start(bf16[128,1280]{1,0:T(8,128)(2,1)S(1)} %get-tuple-element.28), channel_id=1, source_target_pairs={{0,1},{1,2},{2,3},{3,0},{4,5},{5,6},{6,7},{7,4},{8,9},{9,10},{10,1... | collective-permute-start | bytes 983048 | tf_op jit(solution)/shard_map/ppermute | solution.py:22
  146.9 19.2 %all-to-all-start.1 = ((bf16[4,32,1024]{2,1,0:T(8,128)(2,1)}), bf16[4,32,1024]{2,1,0:T(8,128)(2,1)S(1)}, u32[]{:S(2)}, u32[]{:S(2)}) async-start(bf16[4,32,1024]{2,1,0:T(8,128)(2,1)} %share.1.refs_2_), calls=%async_computation.1 | async-start | bytes 524288 | tf_op jit(solution)/shard_map/all_to_all | solution.py:443
  (36 other events, 399.1 us)
